TPU v7x, 32 devices: a whole 2x2x4 slice. The times are simulated.
32 devices in a mesh: wide: 8 (over y, x, core), narrow: 4 (over z).
Axes of the slice: x: 2, y: 2, z: 4, core: 2. Of those that a mesh axis runs over, the one named last changes fastest.
Arguments:
- initial: float32 [64, 64, 128, 128], P(None, 'wide', 'narrow'), may hold values from 0.2 to 1.8
- target: float32 [64, 64, 128, 128], P(None, 'wide', 'narrow'), may hold values from 0.2 to 1.8
- rates_small: float32 [2, 64, 64], replicated, may hold values from 0.1 to 1
- rates_large: float32 [2, 128, 128], replicated, may hold values from 0.1 to 1
- pattern_small: int32 [2, 64, 64], replicated, may hold values 0 or 1
- pattern_large: int32 [2, 128, 128], replicated, may hold values 0 or 1
- spare_small: float32 [64, 64], replicated, may hold values from 0.02 to 0.2
- spare_large: float32 [128, 128], replicated, may hold values from 0.02 to 0.2
- trigger_first: int32 [64], replicated, may hold values 0 or 1
- trigger_last: int32 [128], replicated, may hold values 0 or 1
Outputs:
- grad_small: float32 [2, 64, 64], replicated
- grad_large: float32 [2, 128, 128], replicated
All inputs are finite; a program needn't handle non-finite values.
Results may differ from a plain program's by a relative error of at most 0.00005.
Values sent between devices are 32-bit elements; how exact they have to be, the bound alone decides.
No kernel may reach another device: no remote copies, remote signals or barrier semaphores. Data moves between devices by JAX's collectives and lax.ppermute only.
A program may use at most 192 MiB of HBM per device.

v0:
```python
import math

import jax
import jax.numpy as jnp
from jax import lax
from jax.sharding import PartitionSpec as P

highest = lax.Precision.HIGHEST


def generator(rate_matrix, pattern):
    extent = rate_matrix.shape[-1]
    identity = jnp.eye(extent, dtype=jnp.float32)
    opened = pattern.astype(jnp.float32) * (1.0 - identity)
    flow_rates = rate_matrix * opened
    leaving = jnp.sum(flow_rates, axis=-1)
    return (flow_rates - leaving[..., :, None] * identity, leaving, opened)


def enter_first(tensor):
    return lax.all_to_all(tensor, "wide", split_axis=0, concat_axis=1, tiled=True)


def leave_first(tensor):
    return lax.all_to_all(tensor, "wide", split_axis=1, concat_axis=0, tiled=True)


def enter_second(tensor):
    return lax.all_to_all(tensor, "narrow", split_axis=0, concat_axis=2, tiled=True)


def leave_second(tensor):
    return lax.all_to_all(tensor, "narrow", split_axis=2, concat_axis=0, tiled=True)


def rearranged(tensor):
    return (enter_first(tensor), enter_second(tensor))


def local_part(tensor, mode_zero, mode_three):
    local_terms = jnp.einsum("abcd,ae->ebcd", tensor, mode_zero, precision=highest)
    return local_terms + jnp.einsum("abcd,de->abce", tensor, mode_three, precision=highest)


def operate(tensor, matrices, weights):
    mode_zero, mode_one, mode_two, mode_three, spare_one, spare_two, rim_one, rim_two = matrices
    weight_part, weight_last, weight_tail = weights
    local_terms = local_part(tensor, mode_zero, mode_three)
    tensor_wide = enter_first(tensor)
    tensor_narrow = enter_second(tensor)
    lifted = tensor_wide * weight_part[:, None, None, None]
    wide_terms = jnp.einsum("abcd,be->aecd", tensor_wide, mode_one, precision=highest)
    wide_terms = (
        wide_terms
        + jnp.einsum("abcd,be->aecd", lifted, spare_one, precision=highest)
        - lifted * rim_one[None, :, None, None]
    )
    lowered = tensor_narrow * weight_last[None, None, None, :]
    narrow_terms = jnp.einsum("abcd,ce->abed", tensor_narrow, mode_two, precision=highest)
    narrow_terms = (
        narrow_terms
        + jnp.einsum("abcd,ce->abed", lowered, spare_two, precision=highest)
        - lowered * rim_two[None, None, :, None]
    )
    return (
        local_terms + leave_first(wide_terms) + leave_second(narrow_terms),
        tensor_wide,
        tensor_narrow,
    )


def cross_terms(state_prev, adjoint_now, state_wide, adjoint_wide, state_narrow, adjoint_narrow):
    cross_zero = jnp.einsum("abcd,ebcd->ae", state_prev, adjoint_now, precision=highest)
    cross_three = jnp.einsum("abcd,abce->de", state_prev, adjoint_now, precision=highest)
    cross_one = jnp.einsum("abcd,aecd->be", state_wide, adjoint_wide, precision=highest)
    cross_two = jnp.einsum("abcd,abed->ce", state_narrow, adjoint_narrow, precision=highest)
    return (jnp.stack([cross_zero, cross_one]), jnp.stack([cross_two, cross_three]))


def on_device(
    initial,
    target,
    rates_small,
    rates_large,
    pattern_small,
    pattern_large,
    spare_small,
    spare_large,
    trigger_first,
    trigger_last,
):
    gen_small, exit_small, open_small = generator(rates_small, pattern_small)
    gen_large, exit_large, open_large = generator(rates_large, pattern_large)
    rim_one = jnp.sum(spare_small, axis=1)
    rim_two = jnp.sum(spare_large, axis=1)
    weight_first = trigger_first.astype(jnp.float32)
    weight_last = trigger_last.astype(jnp.float32)
    bound = jnp.sum(jnp.max(exit_small, axis=1)) + jnp.sum(jnp.max(exit_large, axis=1))
    bound = (
        bound + jnp.max(weight_first) * jnp.max(rim_one) + jnp.max(weight_last) * jnp.max(rim_two)
    )
    step_size = 1.0 / bound
    wide_pos = lax.axis_index("wide")
    rows_wide = initial.shape[0] // lax.axis_size("wide")
    weight_part = lax.dynamic_slice_in_dim(weight_first, wide_pos * rows_wide, rows_wide)
    narrow_pos = lax.axis_index("narrow")
    rows_narrow = initial.shape[3] // lax.axis_size("narrow")
    weight_tail = lax.dynamic_slice_in_dim(weight_last, narrow_pos * rows_narrow, rows_narrow)
    weights = (weight_part, weight_last, weight_tail)
    onward = (
        gen_small[0],
        gen_small[1],
        gen_large[0],
        gen_large[1],
        spare_small,
        spare_large,
        rim_one,
        rim_two,
    )
    new_terms, start_wide, start_narrow = operate(initial, onward, weights)
    state = initial + step_size * new_terms
    adjoint = state - target
    adjoint_wide, adjoint_narrow = rearranged(adjoint)
    again_wide, again_narrow = rearranged(initial)
    terms = cross_terms(initial, adjoint, again_wide, adjoint_wide, again_narrow, adjoint_narrow)
    small, large = lax.psum((terms[0], terms[1]), ("wide", "narrow"))
    size_small = initial.shape[0]
    size_large = initial.shape[3]
    small = small / math.sqrt(size_small * size_large * size_large)
    large = large / math.sqrt(size_small * size_small * size_large)
    grad_small = open_small * (small - jnp.diagonal(small, axis1=1, axis2=2)[:, :, None])
    grad_large = open_large * (large - jnp.diagonal(large, axis1=1, axis2=2)[:, :, None])
    return (grad_small, grad_large)


def solution(mesh):
    return jax.shard_map(
        on_device,
        mesh=mesh,
        in_specs=(
            P(None, "wide", "narrow", None),
            P(None, "wide", "narrow", None),
            P(),
            P(),
            P(),
            P(),
            P(),
            P(),
            P(),
            P(),
        ),
        out_specs=(P(), P()),
        check_vma=False,
    )
```

profile of v0, /device:TPU:0, one launch (start us, length us, event | category | flops | bytes accessed | tf_op | source)
XLA Modules:
  0.0 1099.0 jit_solution(3662692372860372819)
XLA Ops:
  7.2 192.2 %all_to_all.118 = f32[64,8,32,128]{3,2,1,0:T(8,128)} all-to-all(f32[64,8,32,128]{3,2,1,0:T(8,128)} %param.10), channel_id=1, replica_groups=mesh['wide'=8,'narrow'=4] {'narrow'}, dimensions={0} | all-to-all | bytes 16777216 | tf_op jit(solution)/shard_map/all_to_all | solution.py:29
  199.4 5.2 all-to-all-start
  209.4 9.6 fusion.43
  219.0 12.7 %fusion.5 = f32[16,8,128,128]{3,2,1,0:T(8,128)S(1)} fusion(f32[128,16,8,128]{3,0,2,1:T(8,128)} %fusion.43, f32[16,8,128,128]{3,2,1,0:T(8,128)S(1)} %bitcast.140, f32[128]{0:T(128)S(1)} %reduce_sum.59, f32[128]{0:T(128)S(1)} %convert_element_type.41, f32[128,128]{1,0:T(8,128)S(1)} %copy-done.8), kind=kOutput, calls=%fused_computation.10 | convolution fusion | flops 3231711232 | bytes 25232384 | tf_op jit(solution)/shard_map/abcd,ce->abed/dot_general | solution.py:62
  231.7 8.1 copy.49
  239.8 58.9 %all-to-all-done = f32[64,8,32,128]{3,2,1,0:T(8,128)} async-done(((f32[64,8,32,128]{3,2,1,0:T(8,128)}), f32[64,8,32,128]{3,2,1,0:T(8,128)}, u32[]{:S(2)}, u32[]{:S(2)}) %all-to-all-start) | async-done | bytes 8388640 | tf_op jit(solution)/shard_map/all_to_all | solution.py:21
  298.7 5.7 all-to-all-start.3
  304.8 16.0 %fusion.8 = f32[64,8,32,128]{3,0,2,1:T(8,128)S(1)} fusion(f32[8,8,8,32,128]{4,3,2,1,0:T(8,128)} %bitcast.10, f32[2,64,64]{1,2,0:T(8,128)S(1)} %multiply_subtract_fusion.1), kind=kOutput, calls=%fused_computation.15 | convolution fusion | flops 1610612736 | bytes 16809984 | tf_op jit(solution)/shard_map/abcd,be->aecd/dot_general | solution.py:52
  320.8 23.9 %fusion.6 = f32[8,64,32,128]{3,1,2,0:T(8,128)S(1)} fusion(f32[64,8,32,128]{3,0,2,1:T(8,128)S(1)} %fusion.8, f32[8,8,8,32,128]{4,3,2,1,0:T(8,128)} %bitcast.10, f32[64]{0:T(128)S(1)} %reduce_sum.58, f32[8]{0:T(128)S(1)} %dynamic_slice.3, f32[64,64]{1,0:T(8,128)S(1)} %copy-done.9), kind=kOutput, calls=%fused_computation.12 | convolution fusion | flops 1621098496 | bytes 25182496 | tf_op jit(solution)/shard_map/abcd,be->aecd/dot_general | solution.py:55
  344.7 8.1 copy.43
  352.7 132.0 %all-to-all-done.3 = f32[16,8,128,128]{3,1,0,2:T(8,128)} async-done(((f32[16,8,128,128]{3,1,0,2:T(8,128)}), f32[16,8,128,128]{3,1,0,2:T(8,128)}, u32[]{:S(2)}, u32[]{:S(2)}) %all-to-all-start.3) | async-done | bytes 8388640 | tf_op jit(solution)/shard_map/all_to_all | solution.py:33
  484.7 5.0 all-to-all-start.1
  497.4 14.8 %fusion.21 = f32[128,64,8,32]{0,1,3,2:T(8,128)} fusion(f32[64,8,32,128]{3,2,1,0:T(8,128)} %param.10, f32[2,128,128]{2,1,0:T(8,128)S(1)} %multiply_subtract_fusion), kind=kOutput, calls=%fused_computation.29 | convolution fusion | flops 3221225472 | bytes 16842752 | tf_op jit(solution)/shard_map/abcd,de->abce/dot_general | solution.py:42
  512.2 8.2 copy.50
  520.4 63.4 %all-to-all-done.1 = f32[8,64,32,128]{3,2,0,1:T(8,128)} async-done(((f32[8,64,32,128]{3,2,0,1:T(8,128)}), f32[8,64,32,128]{3,2,0,1:T(8,128)}, u32[]{:S(2)}, u32[]{:S(2)}) %all-to-all-start.1) | async-done | bytes 8388640 | tf_op jit(solution)/shard_map/all_to_all | solution.py:25
  583.9 45.9 %fusion.4 = f32[64,8,32,128]{3,0,2,1:T(8,128)S(1)} fusion(f32[16,8,4,32,128]{4,0,2,3,1:T(8,128)} %copy.50, f32[128,64,8,32]{0,1,3,2:T(8,128)} %fusion.21, f32[64,8,32,128]{3,2,1,0:T(8,128)} %param.11, f32[8,8,8,32,128]{4,3,0,2,1:T(8,128)} %bitcast.17, f32[64,8,32,128]{3,2,1,0:T(8,128)} %param.10, f32[]{:T(128)S(6)} %div.15, ...), kind=kOutput, calls=%fused_computation.7 | convolution fusion | flops 1623195648 | bytes 58753028 | tf_op jit(solution)/shard_map/abcd,ae->ebcd/dot_general | solution.py:41
  637.8 97.4 %all_to_all.119 = f32[64,8,32,128]{3,2,1,0:T(8,128)} all-to-all(f32[64,8,32,128]{3,2,1,0:T(8,128)S(1)} %copy.54), channel_id=1, replica_groups=mesh['wide'=8,'narrow'=4] {'wide'}, dimensions={0} | all-to-all | bytes 16777216 | tf_op jit(solution)/shard_map/all_to_all | solution.py:21
  735.3 5.7 all-to-all-start.5
  741.1 22.1 %fusion.31 = f32[1,128,128]{2,1,0:T(8,128)S(1)} fusion(f32[64,8,32,128]{3,0,2,1:T(8,128)} %copy-done.1, f32[64,8,32,128]{3,2,1,0:T(8,128)} %param.10), kind=kOutput, calls=%fused_computation.35 | convolution fusion | flops 3221225472 | bytes 16842752 | tf_op jit(solution)/shard_map/abcd,abce->de/dot_general | solution.py:74
  763.2 16.0 %fusion.34 = f32[1,64,64]{1,2,0:T(8,128)S(1)} fusion(f32[64,8,32,128]{3,0,2,1:T(8,128)S(1)} %copy-done.2, f32[64,8,32,128]{3,2,1,0:T(8,128)} %param.10), kind=kOutput, calls=%fused_computation.37 | convolution fusion | flops 1610612736 | bytes 16793600 | tf_op jit(solution)/shard_map/abcd,ebcd->ae/dot_general | solution.py:73
  779.2 15.9 %fusion.37 = f32[1,64,64]{1,2,0:T(8,128)S(1)} fusion(f32[8,8,8,32,128]{4,3,2,1,0:T(8,128)} %bitcast.10, f32[8,8,8,32,128]{4,3,2,1,0:T(8,128)S(1)} %bitcast.142), kind=kOutput, calls=%fused_computation.38 | convolution fusion | flops 1610612736 | bytes 16793600 | tf_op jit(solution)/shard_map/abcd,aecd->be/dot_general | solution.py:75
  795.1 147.9 %psum.14 = f32[2,64,64]{1,2,0:T(8,128)S(1)} all-reduce(f32[2,64,64]{1,2,0:T(8,128)S(1)} %pad_maximum_fusion.1), channel_id=1, replica_groups=mesh['wide'=8,'narrow'=4] {'wide','narrow'}, use_global_device_ids=true, to_apply=%region_12.0 | all-reduce | flops 8192 | bytes 65536 | tf_op jit(solution)/shard_map/psum | solution.py:126
  950.4 9.3 convolution_bitcast_fusion
  961.1 122.3 %all-reduce.2.cloned.1.call-done = f32[2,128,128]{2,1,0:T(8,128)} async-done(((f32[2,128,128]{2,1,0:T(8,128)}), f32[2,128,128]{2,1,0:T(8,128)}) %all-reduce.2.cloned.1.call-update) | async-done | bytes 131088 | tf_op jit(solution)/shard_map/psum | solution.py:126
  (72 shorter events, 34.2 us)
Async XLA Ops:
  199.4 5.2 copy-start.13
  199.4 5.2 copy-start.8
  199.4 5.4 copy-start.5
  199.4 5.4 copy-start.7
  199.4 99.3 %all-to-all-start = ((f32[64,8,32,128]{3,2,1,0:T(8,128)}), f32[64,8,32,128]{3,2,1,0:T(8,128)}, u32[]{:S(2)}, u32[]{:S(2)}) async-start(f32[64,8,32,128]{3,2,1,0:T(8,128)} %param.10), calls=%async_computation | async-start | bytes 16777216 | tf_op jit(solution)/shard_map/all_to_all | solution.py:21
  209.4 9.6 copy-start
  239.8 64.6 %copy-start.10 = (s32[2,64,64]{2,1,0:T(8,128)S(1)}, s32[2,64,64]{2,1,0:T(8,128)}, u32[]{:S(2)}) copy-start(s32[2,64,64]{2,1,0:T(8,128)} %param.14) | copy-start | bytes 98308
  239.8 64.7 %copy-start.11 = (f32[2,64,64]{2,1,0:T(8,128)S(1)}, f32[2,64,64]{2,1,0:T(8,128)}, u32[]{:S(2)}) copy-start(f32[2,64,64]{2,1,0:T(8,128)} %param.12) | copy-start | bytes 98308
  239.8 64.8 %copy-start.12 = (s32[64]{0:T(128)S(1)}, s32[64]{0:T(128)}, u32[]{:S(2)}) copy-start(s32[64]{0:T(128)} %param.18) | copy-start | bytes 772
  239.8 64.8 %copy-start.9 = (f32[64,64]{1,0:T(8,128)S(1)}, f32[64,64]{1,0:T(8,128)}, u32[]{:S(2)}) copy-start(f32[64,64]{1,0:T(8,128)} %param.16) | copy-start | bytes 49156
  298.7 186.1 %all-to-all-start.3 = ((f32[16,8,128,128]{3,1,0,2:T(8,128)}), f32[16,8,128,128]{3,1,0,2:T(8,128)}, u32[]{:S(2)}, u32[]{:S(2)}) async-start(f32[16,8,128,128]{3,1,0,2:T(8,128)} %copy.49), calls=%async_computation.3 | async-start | bytes 16777216 | tf_op jit(solution)/shard_map/all_to_all | solution.py:33
  484.7 99.1 %all-to-all-start.1 = ((f32[8,64,32,128]{3,2,0,1:T(8,128)}), f32[8,64,32,128]{3,2,0,1:T(8,128)}, u32[]{:S(2)}, u32[]{:S(2)}) async-start(f32[8,64,32,128]{3,2,0,1:T(8,128)} %copy.43), calls=%async_computation.1 | async-start | bytes 16777216 | tf_op jit(solution)/shard_map/all_to_all | solution.py:25
  629.7 4.9 copy-start.1
  634.6 3.2 copy-start.3
  735.3 210.7 %all-to-all-start.5 = ((f32[64,8,32,128]{3,2,1,0:T(8,128)}), f32[64,8,32,128]{3,2,1,0:T(8,128)}, u32[]{:S(2)}, u32[]{:S(2)}) async-start(f32[64,8,32,128]{3,2,1,0:T(8,128)} %copy-done.3), calls=%async_computation.5 | async-start | bytes 16777216 | tf_op jit(solution)/shard_map/all_to_all | solution.py:29
  741.0 342.5 %all-reduce.2.cloned.1.call-start = ((), (), s32[]{:S(2)}) async-start(), calls=%async_computation.6 | async-start | bytes 262144 | tf_op jit(solution)/shard_map/psum | solution.py:126
  741.0 22.1 %copy-start.2 = (f32[64,8,32,128]{3,0,2,1:T(8,128)S(1)}, f32[64,8,32,128]{3,0,2,1:T(8,128)}, u32[]{:S(2)}) copy-start(f32[64,8,32,128]{3,0,2,1:T(8,128)} %copy-done.1) | copy-start | bytes 25165828
  763.2 16.0 %copy-start.4 = (f32[64,8,32,128]{3,2,1,0:T(8,128)S(1)}, f32[64,8,32,128]{3,2,1,0:T(8,128)}, u32[]{:S(2)}) copy-start(f32[64,8,32,128]{3,2,1,0:T(8,128)} %all_to_all.119) | copy-start | bytes 25165828
  1083.5 7.5 copy-start.6
Sparse Core Ops, SparseCore 0:
  960.5 122.9 all-reduce.1
where the time goes:
time: 1110 us; the launch traced here: 1100 us
  blocking collectives  438 us (39%)
  waiting for transfers between devices  377 us (34%)
  matrix products  186 us (17%)
  local copies, waits for them, and re-layouts  51.5 us (5%)
  starting transfers between devices  21.6 us (2%)
  between operations  18.7 us (2%)
    all_to_all x1, blocking collectives, enter_second(): lax.all_to_all(tensor, 'narrow', split_axis=0, concat_axis=2, tiled=True)  192 us
    psum x1, blocking collectives, on_device(): small, large = lax.psum((terms[0], terms[1]), ('wide', 'narrow'))  148 us
    all_to_all x1, waiting for transfers between devices, leave_second(): lax.all_to_all(tensor, 'narrow', split_axis=2, concat_axis=0, tiled=True)  132 us
    psum x1, waiting for transfers between devices, on_device(): small, large = lax.psum((terms[0], terms[1]), ('wide', 'narrow'))  122 us
    all_to_all x1, blocking collectives, enter_first(): lax.all_to_all(tensor, 'wide', split_axis=0, concat_axis=1, tiled=True)  97.4 us
    all_to_all x1, waiting for transfers between devices, leave_first(): lax.all_to_all(tensor, 'wide', split_axis=1, concat_axis=0, tiled=True)  63.4 us
    all_to_all x1, waiting for transfers between devices, enter_first(): lax.all_to_all(tensor, 'wide', split_axis=0, concat_axis=1, tiled=True)  58.9 us
    dot_general x1, matrix products, local_part(): jnp.einsum('abcd,ae->ebcd', tensor, mode_zero, precision=highest)  45.9 us
  transfers between devices with their start and end apart: 5, of which 4 were waited for; matrix products, arithmetic and copies ran while one was open for 15% of the time, Pallas kernels for 0%

commit v1 on v0

--- a/solution.py
+++ b/solution.py
@@ -1,11 +1,26 @@
+import functools
 import math
 
 import jax
 import jax.numpy as jnp
 from jax import lax
+from jax.experimental import pallas as pl
+from jax.experimental.pallas import tpu as pltpu
 from jax.sharding import PartitionSpec as P
 
 highest = lax.Precision.HIGHEST
+f32 = jnp.float32
+VMEM_LIMIT = 40 * 1024 * 1024
+bf16 = jnp.bfloat16
+
+TO_INNER = [(0, 1), (3, 2)]
+INNER_SWAP = [(1, 2), (2, 1)]
+TO_OUTER = [(1, 0), (2, 3)]
+
+PIECES = [(0, 2), (2, 4), (4, 6), (6, 7), (7, 8)]
+
+ROWS_BY_ROWS = (((1,), (1,)), ((), ()))
+DEPTH_BY_DEPTH = (((0,), (0,)), ((), ()))
 
 
 def generator(rate_matrix, pattern):
@@ -15,6 +30,398 @@
     flow_rates = rate_matrix * opened
     leaving = jnp.sum(flow_rates, axis=-1)
     return (flow_rates - leaving[..., :, None] * identity, leaving, opened)
+
+
+def halves(value):
+    high = value.astype(bf16)
+    low = (value - high.astype(f32)).astype(bf16)
+    return high, low
+
+
+def all_sum(value, axes):
+    for axis in axes:
+        extent = lax.axis_size(axis)
+        step = 1
+        while step < extent:
+            pairs = [(i, i ^ step) for i in range(extent)]
+            value = value + lax.ppermute(value, axis, pairs)
+            step *= 2
+    return value
+
+
+def whole(array):
+    return pl.BlockSpec(array.shape, lambda i: (0,) * array.ndim)
+
+
+def stacked_rows(ref, count, inner, at):
+    rows = [ref[pl.ds(at + k, count, stride=inner), :] for k in (0, 1)]
+    high, low = halves(jnp.concatenate(rows, axis=1))
+    return jnp.concatenate([high, low], axis=0)
+
+
+def left_parts(matrix):
+    high, low = halves(matrix)
+    return jnp.concatenate(
+        [jnp.concatenate([high, high], axis=1), jnp.concatenate([low, low], axis=1)], axis=0
+    )
+
+
+def folded(total):
+    rows, cols = total.shape[0] // 2, total.shape[1] // 2
+    total = total[:rows] + total[rows:]
+    return total[:, :cols] + total[:, cols:]
+
+
+def product(matrix, in_ref, out_ref, count, inner, add):
+    width = in_ref.shape[1]
+    for at in range(0, inner, 2):
+        out = jnp.dot(matrix, stacked_rows(in_ref, count, inner, at), preferred_element_type=f32)
+        out = out[:count] + out[count:]
+        for k in (0, 1):
+            place = pl.ds(at + k, count, stride=inner)
+            piece = out[:, k * width : (k + 1) * width]
+            out_ref[place, :] = out_ref[place, :] + piece if add else piece
+
+
+def base_body(x_ref, t_ref, first_ref, last_ref, o_ref):
+    count, _, inner, width = x_ref.shape
+    x2, t2, o2 = (ref.reshape(count * inner, width) for ref in (x_ref, t_ref, o_ref))
+    high, low = halves(last_ref[...])
+    last = jnp.concatenate([jnp.concatenate([high, low], axis=1)] * 2, axis=0)
+    for r in range(0, count * inner, 256):
+        x = x2[r : r + 256]
+        high, low = halves(x)
+        out = jnp.dot(jnp.concatenate([high, low], axis=1), last, preferred_element_type=f32)
+        o2[r : r + 256] = x - t2[r : r + 256] + (out[:, :width] + out[:, width:])
+    product(left_parts(first_ref[...]), x2, o2, count, inner, True)
+
+
+def base_terms(x, t, first, last):
+    block = pl.BlockSpec((x.shape[0], 1) + x.shape[2:], lambda i: (0, i, 0, 0))
+    return pl.pallas_call(
+        base_body,
+        grid=(x.shape[1],),
+        in_specs=[block, block, whole(first), whole(last)],
+        out_specs=block,
+        out_shape=jax.ShapeDtypeStruct(x.shape, f32),
+        compiler_params=pltpu.CompilerParams(vmem_limit_bytes=VMEM_LIMIT),
+        cost_estimate=pl.CostEstimate(flops=x.size * 4096, bytes_accessed=x.size * 12, transcendentals=0),
+    )(x, t, first, last)
+
+
+def one_body(x_ref, k_ref, o_ref):
+    blocks, _, rows, inner, width = x_ref.shape
+    count = blocks * rows
+    x2, o2 = x_ref.reshape(count * inner, width), o_ref.reshape(count * inner, width)
+    product(left_parts(k_ref[0]), x2, o2, count, inner, False)
+
+
+def one_terms(x, matrices):
+    block = pl.BlockSpec((x.shape[0], 1) + x.shape[2:], lambda i: (0, i, 0, 0, 0))
+    return pl.pallas_call(
+        one_body,
+        grid=(x.shape[1],),
+        in_specs=[block, pl.BlockSpec((1,) + matrices.shape[1:], lambda i: (i, 0, 0))],
+        out_specs=block,
+        out_shape=jax.ShapeDtypeStruct(x.shape, f32),
+        compiler_params=pltpu.CompilerParams(vmem_limit_bytes=VMEM_LIMIT),
+        cost_estimate=pl.CostEstimate(flops=x.size * 4096, bytes_accessed=x.size * 8, transcendentals=0),
+    )(x, matrices)
+
+
+def one_cross_body(x_ref, a_ref, o_ref):
+    blocks, _, rows, inner, width = x_ref.shape
+    count = blocks * rows
+    x2, a2 = x_ref.reshape(count * inner, width), a_ref.reshape(count * inner, width)
+    total = None
+    for at in range(0, inner, 2):
+        term = lax.dot_general(
+            stacked_rows(x2, count, inner, at),
+            stacked_rows(a2, count, inner, at),
+            ROWS_BY_ROWS,
+            preferred_element_type=f32,
+        )
+        total = term if total is None else total + term
+    o_ref[0] = folded(total)
+
+
+def one_cross(x, a, skip):
+    count = x.shape[0] * x.shape[2]
+    shape = (x.shape[0], 1) + x.shape[2:]
+    out = pl.pallas_call(
+        one_cross_body,
+        grid=(a.shape[1],),
+        in_specs=[
+            pl.BlockSpec(shape, lambda i: (0, i + skip, 0, 0, 0)),
+            pl.BlockSpec(shape, lambda i: (0, i, 0, 0, 0)),
+        ],
+        out_specs=pl.BlockSpec((1, count, count), lambda i: (i, 0, 0)),
+        out_shape=jax.ShapeDtypeStruct((a.shape[1], count, count), f32),
+        compiler_params=pltpu.CompilerParams(vmem_limit_bytes=VMEM_LIMIT),
+        cost_estimate=pl.CostEstimate(flops=a.size * 4096, bytes_accessed=a.size * 8, transcendentals=0),
+    )(x, a)
+    return out
+
+
+def local_body(pieces, x_ref, *refs):
+    a_refs, o_ref, o3_ref = refs[: len(pieces)], refs[-2], refs[-1]
+    wide, deep, _, inner, width = x_ref.shape
+    x2 = x_ref.reshape(wide * deep * inner, width)
+    flat = [a.reshape(a.shape[0] * a.shape[1] * inner, width) for a in a_refs]
+    total = None
+    for at in range(0, inner, 2):
+        parts = []
+        for k in (0, 1):
+            rows = [
+                a[pl.ds(at + k, wide * (hi - lo), stride=inner), :] for a, (lo, hi) in zip(flat, pieces)
+            ]
+            parts.append(jnp.concatenate(rows, axis=0))
+        high, low = halves(jnp.concatenate(parts, axis=1))
+        term = lax.dot_general(
+            stacked_rows(x2, wide * deep, inner, at),
+            jnp.concatenate([high, low], axis=0),
+            ROWS_BY_ROWS,
+            preferred_element_type=f32,
+        )
+        total = term if total is None else total + term
+    o_ref[0] = folded(total)
+    total = None
+    for a_ref, (lo, hi) in zip(a_refs, pieces):
+        for s in range(lo, hi):
+            sides = []
+            for ref, at in ((x_ref, s), (a_ref, s - lo)):
+                rows = jnp.concatenate([ref[w, at, 0] for w in range(wide)], axis=0)
+                sides.append(jnp.concatenate(halves(rows), axis=1))
+            term = lax.dot_general(sides[0], sides[1], DEPTH_BY_DEPTH, preferred_element_type=f32)
+            total = term if total is None else total + term
+    o3_ref[0] = folded(total)
+
+
+def local_cross(x, adjoints):
+    wide, deep, rows, inner, width = x.shape
+    block = lambda a: pl.BlockSpec((wide, a.shape[1], 1, inner, width), lambda i: (0, 0, i, 0, 0))
+    count = wide * deep
+    zero, three = pl.pallas_call(
+        functools.partial(local_body, PIECES),
+        grid=(rows,),
+        in_specs=[block(x)] + [block(a) for a in adjoints],
+        out_specs=[
+            pl.BlockSpec((1, count, count), lambda i: (i, 0, 0)),
+            pl.BlockSpec((1, width, width), lambda i: (i, 0, 0)),
+        ],
+        out_shape=[
+            jax.ShapeDtypeStruct((rows, count, count), f32),
+            jax.ShapeDtypeStruct((rows, width, width), f32),
+        ],
+        compiler_params=pltpu.CompilerParams(vmem_limit_bytes=VMEM_LIMIT),
+        cost_estimate=pl.CostEstimate(flops=x.size * 4096, bytes_accessed=x.size * 8, transcendentals=0),
+    )(x, *adjoints)
+    zero = jnp.sum(zero, axis=0)
+    columns, at = [], 0
+    for lo, hi in PIECES:
+        size = wide * (hi - lo)
+        columns.append(zero[:, at : at + size].reshape(count, wide, hi - lo))
+        at += size
+    zero = jnp.concatenate(columns, axis=2).reshape(count, count)
+    return zero, jnp.sum(three, axis=0)
+
+
+def inner_body(slabs, w_ref, m_ref, x_ref, p_ref, q_ref, f_ref, b_ref, bp_ref, a_ref, y_ref, c_ref):
+    part = x_ref.shape[1]
+    width = x_ref.shape[2]
+
+    weights = left_parts(m_ref[...])
+    gate = jnp.concatenate([w_ref[...], w_ref[...]], axis=1)
+    total = None
+    for n in range(0, slabs, 2):
+        high, low = [], []
+        for k in (n, n + 1):
+            rows = jnp.concatenate([x_ref[k], p_ref[k], q_ref[k], f_ref[k]], axis=0)
+            hi, lo = halves(rows)
+            high.append(hi)
+            low.append(lo)
+        high = jnp.concatenate(high, axis=1)
+        low = jnp.concatenate(low, axis=1)
+        both = jnp.concatenate([high, low], axis=0)
+        out = jnp.dot(weights, both, preferred_element_type=f32)
+        rows = out.shape[0] // 2
+        out = out[:rows] + out[rows:]
+        out = out[: rows // 2] + gate * out[rows // 2 :]
+        own = jnp.concatenate([b_ref[n], b_ref[n + 1]], axis=1) + out[:part]
+        other = jnp.concatenate([bp_ref[n], bp_ref[n + 1]], axis=1) + out[part:]
+        for k in (0, 1):
+            a_ref[n + k] = own[:, k * width : (k + 1) * width]
+            y_ref[n + k] = out[part:, k * width : (k + 1) * width]
+        hi, lo = halves(jnp.concatenate([own, other], axis=0))
+        cross = lax.dot_general(
+            both,
+            jnp.concatenate([hi, lo], axis=0),
+            ROWS_BY_ROWS,
+            preferred_element_type=f32,
+        )
+        total = cross if total is None else total + cross
+    c_ref[0] = folded(total)
+
+
+def inner_terms(gate, weights, x, p, q, f, b, bp):
+    count, part, width = x.shape
+    slabs = 16
+    block = pl.BlockSpec((slabs, part, width), lambda i: (i, 0, 0))
+    return pl.pallas_call(
+        functools.partial(inner_body, slabs),
+        grid=(count // slabs,),
+        in_specs=[whole(gate), whole(weights)] + [block] * 6,
+        out_specs=[block, block, pl.BlockSpec((1, 4 * part, 2 * part), lambda i: (i, 0, 0))],
+        out_shape=[
+            jax.ShapeDtypeStruct(x.shape, f32),
+            jax.ShapeDtypeStruct(x.shape, f32),
+            jax.ShapeDtypeStruct((count // slabs, 4 * part, 2 * part), f32),
+        ],
+        compiler_params=pltpu.CompilerParams(vmem_limit_bytes=VMEM_LIMIT),
+        cost_estimate=pl.CostEstimate(
+            flops=count * 6 * 2 * 128 * 128 * 128, bytes_accessed=count * part * width * 4 * 8, transcendentals=0
+        ),
+    )(gate, weights, x, p, q, f, b, bp)
+
+
+def line_device(
+    initial, target, rates_small, rates_large, pattern_small, pattern_large,
+    spare_small, spare_large, trigger_first, trigger_last,
+):
+    gen_small, exit_small, open_small = generator(rates_small, pattern_small)
+    gen_large, exit_large, open_large = generator(rates_large, pattern_large)
+    rim_one = jnp.sum(spare_small, axis=1)
+    rim_two = jnp.sum(spare_large, axis=1)
+    weight_first = trigger_first.astype(f32)
+    weight_last = trigger_last.astype(f32)
+    bound = jnp.sum(jnp.max(exit_small, axis=1)) + jnp.sum(jnp.max(exit_large, axis=1))
+    bound = bound + jnp.max(weight_first) * jnp.max(rim_one) + jnp.max(weight_last) * jnp.max(rim_two)
+    step_size = 1.0 / bound
+
+    size_small, size_large = initial.shape[0], initial.shape[3]
+    wide = lax.axis_size("wide")
+    wide_pos = lax.axis_index("wide")
+    place = lax.axis_index("narrow")
+    deep = size_small // wide
+    rows, part = initial.shape[1], initial.shape[2]
+
+    spare_one = spare_small - jnp.diag(rim_one)
+    mine = lax.dynamic_slice_in_dim(weight_first, wide_pos * deep, deep)
+    mode_one = step_size * (gen_small[1][None] + mine[:, None, None] * spare_one[None])
+    mode_one = mode_one.transpose(0, 2, 1)
+
+    inner = (place == 1) | (place == 2)
+    partner = jnp.where(place < 2, 1 - place, 5 - place)
+    spare_two = spare_large - jnp.diag(rim_two)
+    factor = jnp.where(inner, step_size, 0.0)
+    places = jnp.concatenate(
+        [jnp.arange(part) + block * part for block in (place, partner, 3 - place, 3 - partner)]
+    )
+    spread = (places[:, None] == jnp.arange(size_large)[None]).astype(f32)
+    picked = functools.partial(jnp.einsum, "xr,rc,yc->xy", precision=highest)
+    weights = factor * jnp.concatenate(
+        [picked(spread, m, spread[: 2 * part]) for m in (gen_large[0], spare_two)], axis=1
+    ).T
+    gate = weight_last[None, :]
+
+    xv = initial.reshape(wide, deep, rows, part, size_large)
+    half = deep // 2
+
+    def shift(value, pairs):
+        return lax.ppermute(value, "narrow", pairs)
+
+    def exchange(value):
+        return lax.all_to_all(value, "wide", 0, 0, tiled=True)
+
+    def after(value, *done):
+        return lax.optimization_barrier((value,) + done)[0]
+
+    xs = [xv[:, lo:hi].reshape(-1, part, size_large) for lo, hi in PIECES]
+    ps, qs, fs = [], [], []
+    for k in range(len(PIECES)):
+        piece = xs[k] if k < 2 else after(xs[k], ps[k - 2])
+        ps.append(shift(piece, TO_INNER))
+        qs.append(shift(piece, INNER_SWAP))
+        fs.append(shift(ps[k], INNER_SWAP))
+
+    base = base_terms(initial, target, step_size * gen_small[0].T, step_size * gen_large[1])
+
+    wide_x = [exchange(xv[:, :half])]
+    first = after(wide_x[0], base, ps[0], qs[0])
+    back = [exchange(one_terms(first, mode_one[:half]))]
+    wide_x.append(exchange(after(xv[:, half:], back[0])))
+    bases = []
+
+    def add_base(k):
+        lo, hi = PIECES[k]
+        at = lo % half
+        total = base.reshape(xv.shape)[:, lo:hi] + back[lo // half][:, at : at + hi - lo]
+        bases.append(total.reshape(-1, part, size_large))
+
+    back[0] = after(back[0], ps[1], qs[1])
+    add_base(0)
+    add_base(1)
+    others = [shift(b, TO_INNER) for b in bases]
+    second = after(wide_x[1], fs[0], ps[2], *bases)
+    back.append(exchange(one_terms(second, mode_one[half:])))
+
+    adjoints, wide_a, sums_two, own, far = [], [], [], [], []
+
+    def inner_step(k, *done):
+        b = after(bases[k], *done) if done else bases[k]
+        a, y, c2 = inner_terms(gate, weights, xs[k], ps[k], qs[k], fs[k], b, others[k])
+        sums_two.append(c2)
+        own.append(a)
+        far.append(shift(y, TO_OUTER))
+
+    def finish(k, *done):
+        a = after(own[k], *done) if done else own[k]
+        lo, hi = PIECES[k]
+        adjoints.append((a + far[k]).reshape(wide, hi - lo, rows, part, size_large))
+        wide_a.append(exchange(adjoints[k]))
+
+    inner_step(0)
+    back[1] = after(back[1], own[0], qs[2])
+    for k in (2, 3, 4):
+        add_base(k)
+        others.append(shift(bases[k], TO_INNER))
+    finish(0, bases[2])
+    inner_step(1, adjoints[0])
+    finish(1, own[1])
+    inner_step(2, adjoints[1])
+    ones = []
+
+    def cross_step(k, *done):
+        a = after(wide_a[k], *done)
+        lo, _ = PIECES[k]
+        ones.append(one_cross(wide_x[lo // half], a, lo % half))
+
+    cross_step(0, own[2])
+    cross_step(1, ones[0])
+    inner_step(3, ones[1])
+    finish(2, own[3])
+    inner_step(4, adjoints[2])
+    finish(3, own[4])
+    cross_step(2, adjoints[3])
+    finish(4, ones[2])
+    cross_zero, cross_three = local_cross(xv, adjoints)
+    cross_step(3, cross_three)
+    cross_step(4, ones[3])
+    cross_one = jnp.sum(jnp.concatenate(ones, axis=0), axis=0)
+    found = jnp.where(inner, jnp.sum(jnp.concatenate(sums_two, axis=0), axis=0), 0.0)
+    cross_two = jnp.einsum("xr,xy,yc->rc", spread, found, spread[: 2 * part], precision=highest)
+
+    packed = jnp.concatenate(
+        [jnp.concatenate([cross_zero, cross_one], axis=1), cross_two, cross_three], axis=0
+    )
+    packed = all_sum(packed, ("wide", "narrow"))
+    small = jnp.stack([packed[:size_small, :size_small], packed[:size_small, size_small:]])
+    large = packed[size_small:].reshape(2, size_large, size_large)
+    small = small / math.sqrt(size_small * size_large * size_large)
+    large = large / math.sqrt(size_small * size_small * size_large)
+    grad_small = open_small * (small - jnp.diagonal(small, axis1=1, axis2=2)[:, :, None])
+    grad_large = open_large * (large - jnp.diagonal(large, axis1=1, axis2=2)[:, :, None])
+    return (grad_small, grad_large)
 
 
 def enter_first(tensor):
@@ -134,8 +541,9 @@
 
 
 def solution(mesh):
+    line = mesh.shape["narrow"] == 4 and mesh.shape["wide"] == 8
     return jax.shard_map(
-        on_device,
+        line_device if line else on_device,
         mesh=mesh,
         in_specs=(
             P(None, "wide", "narrow", None),

time: 1110 us -> 646 us (0.58)
  blocking collectives: 438 us -> 52.8 us
  matrix products: 186 us -> 2.37 us
  waiting for transfers between devices: 377 us -> 263 us
  Pallas kernels: 0 us -> 112 us
  starting transfers between devices: 21.6 us -> 129 us
  other arithmetic: 6.91 us -> 36.9 us
  between operations: 18.7 us -> 5.41 us
    ppermute x0 -> x30, waiting for transfers between devices: none -> 263 us  [the longest x25 237 us: shift(): return lax.ppermute(value, 'narrow', pairs)]
    all_to_all x4 -> x8, waiting for transfers between devices: 254 us -> 0.02 us  [exchange(): return lax.all_to_all(value, 'wide', 0, 0, tiled=True)]
    all_to_all x2 -> x1, blocking collectives: 290 us -> 52.8 us  [exchange(): return lax.all_to_all(value, 'wide', 0, 0, tiled=True)]
    dot_general x10 -> x6, matrix products: 186 us -> 2.37 us  [the longest x2 1.36 us: line_device(): jnp.einsum('xr,xy,yc->rc', spread, found, spread[:2 * part], precision=hi...]
    psum x1 -> x0, blocking collectives: 148 us -> none  [on_device(): small, large = lax.psum((terms[0], terms[1]), ('wide', 'narrow'))]
    psum x1 -> x0, waiting for transfers between devices: 122 us -> none  [on_device(): small, large = lax.psum((terms[0], terms[1]), ('wide', 'narrow'))]
    pallas_call x0 -> x14, Pallas kernels: none -> 112 us  [the longest x5 44 us: inner_terms(): pl.pallas_call(functools.partial(inner_body, slabs), grid=(count // slabs...]
    ppermute x0 -> x30, starting transfers between devices: none -> 93.6 us  [the longest x25 89.2 us: shift(): return lax.ppermute(value, 'narrow', pairs)]
  transfers between devices with their start and end apart: 5 -> 38, of which waited for: 4 -> 18; matrix products, arithmetic and copies ran while one was open for 15% -> 7% of each run, Pallas kernels for 0% -> 14%
where the time goes in v1:
time: 646 us; the launch traced here: 644 us
  waiting for transfers between devices  263 us (41%)
  starting transfers between devices  129 us (20%)
  Pallas kernels  112 us (17%)
  blocking collectives  52.8 us (8%)
  local copies, waits for them, and re-layouts  43 us (7%)
  other arithmetic  36.9 us (6%)
    ppermute x25, waiting for transfers between devices, shift(): return lax.ppermute(value, 'narrow', pairs)  237 us
    ppermute x25, starting transfers between devices, shift(): return lax.ppermute(value, 'narrow', pairs)  89.2 us
    all_to_all x1, blocking collectives, exchange(): return lax.all_to_all(value, 'wide', 0, 0, tiled=True)  52.8 us
    pallas_call x5, Pallas kernels, inner_terms(): pl.pallas_call(functools.partial(inner_body, slabs), grid=(count // slabs...  44 us
    all_to_all x8, starting transfers between devices, exchange(): return lax.all_to_all(value, 'wide', 0, 0, tiled=True)  35 us
    ppermute x5, waiting for transfers between devices, all_sum(): value = value + lax.ppermute(value, axis, pairs)  25.8 us
    pallas_call x1, Pallas kernels, base_terms(): pl.pallas_call(base_body, grid=(x.shape[1],), in_specs=[block, block, who...  21.2 us
    pallas_call x5, Pallas kernels, one_cross(): pl.pallas_call(one_cross_body, grid=(a.shape[1],), in_specs=[pl.BlockSpec...  18.7 us
  transfers between devices with their start and end apart: 38, of which 18 were waited for; matrix products, arithmetic and copies ran while one was open for 7% of the time, Pallas kernels for 14%

profile of v1, /device:TPU:0, one launch (start us, length us, event | category | flops | bytes accessed | tf_op | source)
XLA Modules:
  0.0 643.7 jit_solution(2174731961023175039)
XLA Ops:
  0.6 8.5 %fusion.37 = (f32[8,4,8,32,128]{4,3,2,1,0:T(8,128)}, f32[8,4,8,32,128]{4,3,2,1,0:T(8,128)}) fusion(f32[8,8,8,32,128]{4,3,2,1,0:T(8,128)} %bitcast.80), kind=kLoop, calls=%fused_computation.82 | loop fusion | bytes 16777216 | tf_op jit(solution)/shard_map/slice | solution.py:352
  37.3 21.2 %shard_map.113 = f32[64,8,32,128]{3,2,1,0:T(8,128)S(1)} custom-call(f32[64,8,32,128]{3,2,1,0:T(8,128)} %x_ref.1, f32[64,8,32,128]{3,2,1,0:T(8,128)} %t_ref.1, f32[64,64]{1,0:T(8,128)S(1)} %get-tuple-element.100.first_ref, f32[128,128]{1,0:T(8,128)S(1)} %fusion.1.last_ref), custom_call_target="tpu_custom_call" | custom-call | flops 8589934592 | bytes 25165824 | tf_op jit(solution)/shard_map/pallas_call | solution.py:101
  61.8 8.7 %collective-permute-done.p_ref = f32[128,32,128]{2,1,0:T(8,128)} collective-permute-done((f32[128,32,128]{2,1,0:T(8,128)}, f32[128,32,128]{2,1,0:T(8,128)}, u32[]{:S(2)}, u32[]{:S(2)}) %collective-permute-start) | collective-permute-done | bytes 2097184 | tf_op jit(solution)/shard_map/ppermute | solution.py:331
  77.3 52.8 %all_to_all.45 = f32[8,4,8,32,128]{4,3,2,1,0:T(8,128)} all-to-all(f32[8,4,8,32,128]{4,3,2,1,0:T(8,128)S(1)} %shard_map.114), channel_id=1, replica_groups=mesh['wide'=8,'narrow'=4] {'wide'}, dimensions={0} | all-to-all | bytes 8388608 | tf_op jit(solution)/shard_map/all_to_all | solution.py:334
  134.7 7.0 %collective-permute-start.3 = (f32[128,32,128]{2,1,0:T(8,128)}, f32[128,32,128]{2,1,0:T(8,128)}, u32[]{:S(2)}, u32[]{:S(2)}) collective-permute-start(f32[128,32,128]{2,1,0:T(8,128)} %bitcast.70), channel_id=1, source_target_pairs={{0,1},{3,2},{4,5},{7,6},{8,9},{11,10},{12,13},{15,14},{16,17},{19,... | collective-permute-start | bytes 6291464 | tf_op jit(solution)/shard_map/ppermute | solution.py:331
  148.9 37.7 %collective-permute-done.3.p_ref = f32[128,32,128]{2,1,0:T(8,128)} collective-permute-done((f32[128,32,128]{2,1,0:T(8,128)}, f32[128,32,128]{2,1,0:T(8,128)}, u32[]{:S(2)}, u32[]{:S(2)}) %collective-permute-start.3) | collective-permute-done | bytes 2097184 | tf_op jit(solution)/shard_map/ppermute | solution.py:331
  186.7 6.8 %slice_add_fusion = (f32[8,2,8,32,128]{4,3,2,1,0:T(8,128)}, f32[8,2,8,32,128]{4,3,2,1,0:T(8,128)}) fusion(f32[8,8,8,32,128]{4,3,2,1,0:T(8,128)} %bitcast.64, f32[8,4,8,32,128]{4,3,2,1,0:T(8,128)} %all_to_all.45), kind=kLoop, calls=%fused_computation.2 | loop fusion | flops 1048576 | bytes 12582912 | tf_op jit(solution)/shard_map/add | solution.py:358
  193.5 7.0 %collective-permute-start.5 = (f32[128,32,128]{2,1,0:T(8,128)}, f32[128,32,128]{2,1,0:T(8,128)}, u32[]{:S(2)}, u32[]{:S(2)}) collective-permute-start(f32[128,32,128]{2,1,0:T(8,128)} %bitcast.13.b_ref), channel_id=1, source_target_pairs={{0,1},{3,2},{4,5},{7,6},{8,9},{11,10},{12,13},{15,14},{16,17},{19,... | collective-permute-start | bytes 6291464 | tf_op jit(solution)/shard_map/ppermute | solution.py:331
  200.6 31.0 %collective-permute-done.6.p_ref = f32[128,32,128]{2,1,0:T(8,128)} collective-permute-done((f32[128,32,128]{2,1,0:T(8,128)S(1)}, f32[128,32,128]{2,1,0:T(8,128)}, u32[]{:S(2)}, u32[]{:S(2)}) %collective-permute-start.6) | collective-permute-done | bytes 2097184 | tf_op jit(solution)/shard_map/ppermute | solution.py:331
  246.9 29.1 %collective-permute-done.5.bp_ref = f32[128,32,128]{2,1,0:T(8,128)} collective-permute-done((f32[128,32,128]{2,1,0:T(8,128)}, f32[128,32,128]{2,1,0:T(8,128)}, u32[]{:S(2)}, u32[]{:S(2)}) %collective-permute-start.5) | collective-permute-done | bytes 2097184 | tf_op jit(solution)/shard_map/ppermute | solution.py:331
  276.0 11.2 %shard_map.115 = (f32[128,32,128]{2,1,0:T(8,128)S(1)}, f32[128,32,128]{2,1,0:T(8,128)}, f32[8,128,64]{2,1,0:T(8,128)S(1)}) custom-call(f32[1,128]{1,0:T(1,128)S(1)} %convert_bitcast_fusion.w_ref, f32[128,128]{1,0:T(8,128)S(1)} %fusion.3.m_ref, f32[128,32,128]{2,1,0:T(8,128)} %bitcast.4.x_ref, f32[128,32,128]{2,1,0:T(8,128)} %collective-permute-done.p_ref, ...), custom_call_target="tpu_custom_call" | custom-call | flops 3221225472 | bytes 16777216 | tf_op jit(solution)/shard_map/pallas_call | solution.py:270
  292.6 8.8 %collective-permute-start.10 = (f32[128,32,128]{2,1,0:T(8,128)}, f32[128,32,128]{2,1,0:T(8,128)}, u32[]{:S(2)}, u32[]{:S(2)}) collective-permute-start(f32[128,32,128]{2,1,0:T(8,128)} %bitcast.15.b_ref), channel_id=1, source_target_pairs={{0,1},{3,2},{4,5},{7,6},{8,9},{11,10},{12,13},{15,14},{16,17},{19,... | collective-permute-start | bytes 6291464 | tf_op jit(solution)/shard_map/ppermute | solution.py:331
  306.9 31.8 %collective-permute-done.8 = f32[128,32,128]{2,1,0:T(8,128)} collective-permute-done((f32[128,32,128]{2,1,0:T(8,128)}, f32[128,32,128]{2,1,0:T(8,128)}, u32[]{:S(2)}, u32[]{:S(2)}) %collective-permute-start.8) | collective-permute-done | bytes 2097184 | tf_op jit(solution)/shard_map/ppermute | solution.py:331
  344.5 10.8 %shard_map.117 = (f32[128,32,128]{2,1,0:T(8,128)S(1)}, f32[128,32,128]{2,1,0:T(8,128)}, f32[8,128,64]{2,1,0:T(8,128)S(1)}) custom-call(f32[1,128]{1,0:T(1,128)S(1)} %convert_bitcast_fusion.w_ref, f32[128,128]{1,0:T(8,128)S(1)} %fusion.3.m_ref, f32[128,32,128]{2,1,0:T(8,128)S(1)} %bitcast.72, f32[128,32,128]{2,1,0:T(8,128)} %collective-permute-done.3.p_ref, ...), custom_call_target="tpu_custom_call" | custom-call | flops 3221225472 | bytes 16777216 | tf_op jit(solution)/shard_map/pallas_call | solution.py:270
  360.7 7.6 %collective-permute-start.13 = (f32[128,32,128]{2,1,0:T(8,128)}, f32[128,32,128]{2,1,0:T(8,128)}, u32[]{:S(2)}, u32[]{:S(2)}) collective-permute-start(f32[128,32,128]{2,1,0:T(8,128)} %bitcast.16.b_ref), channel_id=1, source_target_pairs={{0,1},{3,2},{4,5},{7,6},{8,9},{11,10},{12,13},{15,14},{16,17},{19,... | collective-permute-start | bytes 6291464 | tf_op jit(solution)/shard_map/ppermute | solution.py:331
  377.9 27.6 %collective-permute-done.11 = f32[128,32,128]{2,1,0:T(8,128)} collective-permute-done((f32[128,32,128]{2,1,0:T(8,128)}, f32[128,32,128]{2,1,0:T(8,128)}, u32[]{:S(2)}, u32[]{:S(2)}) %collective-permute-start.11) | collective-permute-done | bytes 2097184 | tf_op jit(solution)/shard_map/ppermute | solution.py:331
  414.9 10.4 %shard_map.118 = (f32[128,32,128]{2,1,0:T(8,128)S(1)}, f32[128,32,128]{2,1,0:T(8,128)}, f32[8,128,64]{2,1,0:T(8,128)S(1)}) custom-call(f32[1,128]{1,0:T(1,128)S(1)} %convert_bitcast_fusion.w_ref, f32[128,128]{1,0:T(8,128)S(1)} %fusion.3.m_ref, f32[128,32,128]{2,1,0:T(8,128)S(1)} %bitcast.69, f32[128,32,128]{2,1,0:T(8,128)} %collective-permute-done.6.p_ref, ...), custom_call_target="tpu_custom_call" | custom-call | flops 3221225472 | bytes 16777216 | tf_op jit(solution)/shard_map/pallas_call | solution.py:270
  436.9 7.2 %collective-permute-start.17 = (f32[64,32,128]{2,1,0:T(8,128)S(1)}, f32[64,32,128]{2,1,0:T(8,128)}, u32[]{:S(2)}, u32[]{:S(2)}) collective-permute-start(f32[64,32,128]{2,1,0:T(8,128)S(1)} %bitcast.78), channel_id=1, source_target_pairs={{0,1},{3,2},{4,5},{7,6},{8,9},{11,10},{12,13},{15,14},{16,17},{19,... | collective-permute-start | bytes 3145736 | tf_op jit(solution)/shard_map/ppermute | solution.py:331
  456.0 10.8 %collective-permute-done.17.bp_ref = f32[64,32,128]{2,1,0:T(8,128)} collective-permute-done((f32[64,32,128]{2,1,0:T(8,128)S(1)}, f32[64,32,128]{2,1,0:T(8,128)}, u32[]{:S(2)}, u32[]{:S(2)}) %collective-permute-start.17) | collective-permute-done | bytes 1048608 | tf_op jit(solution)/shard_map/ppermute | solution.py:331
  486.4 16.1 %collective-permute-start.22 = (f32[64,32,128]{2,1,0:T(8,128)S(1)}, f32[64,32,128]{2,1,0:T(8,128)S(1)}, u32[]{:S(2)}, u32[]{:S(2)}) collective-permute-start(f32[64,32,128]{2,1,0:T(8,128)S(1)} %bitcast.76), channel_id=1, source_target_pairs={{0,1},{3,2},{4,5},{7,6},{8,9},{11,10},{12,13},{15,14},{16,17},{19,... | collective-permute-start | bytes 3145736 | tf_op jit(solution)/shard_map/ppermute | solution.py:331
  504.0 20.8 %collective-permute-done.22.bp_ref = f32[64,32,128]{2,1,0:T(8,128)S(1)} collective-permute-done((f32[64,32,128]{2,1,0:T(8,128)S(1)}, f32[64,32,128]{2,1,0:T(8,128)S(1)}, u32[]{:S(2)}, u32[]{:S(2)}) %collective-permute-start.22) | collective-permute-done | bytes 1048608 | tf_op jit(solution)/shard_map/ppermute | solution.py:331
  546.4 28.8 %collective-permute-done.24 = f32[64,32,128]{2,1,0:T(8,128)} collective-permute-done((f32[64,32,128]{2,1,0:T(8,128)}, f32[64,32,128]{2,1,0:T(8,128)}, u32[]{:S(2)}, u32[]{:S(2)}) %collective-permute-start.24) | collective-permute-done | bytes 1048608 | tf_op jit(solution)/shard_map/ppermute | solution.py:331
  581.2 14.2 %shard_map.124 = (f32[8,64,64]{2,1,0:T(8,128)S(1)}, f32[8,128,128]{2,1,0:T(8,128)S(1)}) custom-call(f32[8,8,8,32,128]{4,3,2,1,0:T(8,128)} %bitcast.83, f32[8,2,8,32,128]{4,3,2,1,0:T(8,128)} %bitcast.17.refs_0_, f32[8,2,8,32,128]{4,3,2,1,0:T(8,128)} %bitcast.18.refs_1_, f32[8,2,8,32,128]{4,3,2,1,0:T(8,128)} %bitcast.21.refs_2_, ...), custom_call_target="tpu_custom_call" | custom-call | flops 8589934592 | bytes 16777216 | tf_op jit(solution)/shard_map/pallas_call | solution.py:204
  623.4 9.1 %collective-permute-done.29 = f32[320,128]{0,1:T(8,128)S(1)} collective-permute-done((f32[320,128]{0,1:T(8,128)S(1)}, f32[320,128]{0,1:T(8,128)S(1)}, u32[]{:S(2)}, u32[]{:S(2)}) %collective-permute-start.29) | collective-permute-done | bytes 163872 | tf_op jit(solution)/shard_map/ppermute | solution.py:47
  (242 shorter events, 213.1 us)
Async XLA Ops:
  9.2 61.4 %all-to-all-start = ((f32[8,4,8,32,128]{4,3,2,1,0:T(8,128)}), f32[8,4,8,32,128]{4,3,2,1,0:T(8,128)}, u32[]{:S(2)}, u32[]{:S(2)}) async-start(f32[8,4,8,32,128]{4,3,2,1,0:T(8,128)} %get-tuple-element.94), calls=%async_computation | async-start | bytes 8388608 | tf_op jit(solution)/shard_map/all_to_all | solution.py:334
  20.5 50.0 %collective-permute-start = (f32[128,32,128]{2,1,0:T(8,128)}, f32[128,32,128]{2,1,0:T(8,128)}, u32[]{:S(2)}, u32[]{:S(2)}) collective-permute-start(f32[128,32,128]{2,1,0:T(8,128)} %bitcast.4.x_ref), channel_id=1, source_target_pairs={{0,1},{3,2},{4,5},{7,6},{8,9},{11,10},{12,13},{15,14},{16,17},{19,... | collective-permute-start | bytes 6291464 | tf_op jit(solution)/shard_map/ppermute | solution.py:331
  26.1 44.4 %collective-permute-start.1 = (f32[128,32,128]{2,1,0:T(8,128)}, f32[128,32,128]{2,1,0:T(8,128)}, u32[]{:S(2)}, u32[]{:S(2)}) collective-permute-start(f32[128,32,128]{2,1,0:T(8,128)} %bitcast.4.x_ref), channel_id=1, source_target_pairs={{1,2},{2,1},{5,6},{6,5},{9,10},{10,9},{13,14},{14,13},{17,18},{18,... | collective-permute-start | bytes 6291464 | tf_op jit(solution)/shard_map/ppermute | solution.py:331
  130.1 101.4 %all-to-all-start.2 = ((f32[8,4,8,32,128]{4,3,2,1,0:T(8,128)}), f32[8,4,8,32,128]{4,3,2,1,0:T(8,128)}, u32[]{:S(2)}, u32[]{:S(2)}) async-start(f32[8,4,8,32,128]{4,3,2,1,0:T(8,128)} %get-tuple-element.43), calls=%async_computation.2 | async-start | bytes 8388608 | tf_op jit(solution)/shard_map/all_to_all | solution.py:334
  134.7 52.0 %collective-permute-start.3 = (f32[128,32,128]{2,1,0:T(8,128)}, f32[128,32,128]{2,1,0:T(8,128)}, u32[]{:S(2)}, u32[]{:S(2)}) collective-permute-start(f32[128,32,128]{2,1,0:T(8,128)} %bitcast.70), channel_id=1, source_target_pairs={{0,1},{3,2},{4,5},{7,6},{8,9},{11,10},{12,13},{15,14},{16,17},{19,... | collective-permute-start | bytes 6291464 | tf_op jit(solution)/shard_map/ppermute | solution.py:331
  141.7 44.9 %collective-permute-start.4 = (f32[128,32,128]{2,1,0:T(8,128)}, f32[128,32,128]{2,1,0:T(8,128)}, u32[]{:S(2)}, u32[]{:S(2)}) collective-permute-start(f32[128,32,128]{2,1,0:T(8,128)} %bitcast.71), channel_id=1, source_target_pairs={{1,2},{2,1},{5,6},{6,5},{9,10},{10,9},{13,14},{14,13},{17,18},{18,... | collective-permute-start | bytes 6291464 | tf_op jit(solution)/shard_map/ppermute | solution.py:331
  143.7 56.9 %collective-permute-start.2 = (f32[128,32,128]{2,1,0:T(8,128)}, f32[128,32,128]{2,1,0:T(8,128)}, u32[]{:S(2)}, u32[]{:S(2)}) collective-permute-start(f32[128,32,128]{2,1,0:T(8,128)} %collective-permute-done.p_ref), channel_id=1, source_target_pairs={{1,2},{2,1},{5,6},{6,5},{9,10},{10,9},{13,14},{14,13},{17,18},{18,... | collective-permute-start | bytes 6291464 | tf_op jit(solution)/shard_map/ppermute | solution.py:331
  145.7 85.8 %collective-permute-start.6 = (f32[128,32,128]{2,1,0:T(8,128)S(1)}, f32[128,32,128]{2,1,0:T(8,128)}, u32[]{:S(2)}, u32[]{:S(2)}) collective-permute-start(f32[128,32,128]{2,1,0:T(8,128)S(1)} %bitcast.67), channel_id=1, source_target_pairs={{0,1},{3,2},{4,5},{7,6},{8,9},{11,10},{12,13},{15,14},{16,17},{19,... | collective-permute-start | bytes 6291464 | tf_op jit(solution)/shard_map/ppermute | solution.py:331
  193.5 82.5 %collective-permute-start.5 = (f32[128,32,128]{2,1,0:T(8,128)}, f32[128,32,128]{2,1,0:T(8,128)}, u32[]{:S(2)}, u32[]{:S(2)}) collective-permute-start(f32[128,32,128]{2,1,0:T(8,128)} %bitcast.13.b_ref), channel_id=1, source_target_pairs={{0,1},{3,2},{4,5},{7,6},{8,9},{11,10},{12,13},{15,14},{16,17},{19,... | collective-permute-start | bytes 6291464 | tf_op jit(solution)/shard_map/ppermute | solution.py:331
  240.3 62.4 %all-to-all-start.3 = ((f32[8,4,8,32,128]{4,3,2,1,0:T(8,128)}), f32[8,4,8,32,128]{4,3,2,1,0:T(8,128)}, u32[]{:S(2)}, u32[]{:S(2)}) async-start(f32[8,4,8,32,128]{4,3,2,1,0:T(8,128)} %copy-done.2), calls=%async_computation.3 | async-start | bytes 8388608 | tf_op jit(solution)/shard_map/all_to_all | solution.py:334
  246.1 55.2 %collective-permute-start.7 = (f32[128,32,128]{2,1,0:T(8,128)S(1)}, f32[128,32,128]{2,1,0:T(8,128)S(1)}, u32[]{:S(2)}, u32[]{:S(2)}) collective-permute-start(f32[128,32,128]{2,1,0:T(8,128)S(1)} %bitcast.68), channel_id=1, source_target_pairs={{1,2},{2,1},{5,6},{6,5},{9,10},{10,9},{13,14},{14,13},{17,18},{18,... | collective-permute-start | bytes 6291464 | tf_op jit(solution)/shard_map/ppermute | solution.py:331
  289.3 49.4 %collective-permute-start.8 = (f32[128,32,128]{2,1,0:T(8,128)}, f32[128,32,128]{2,1,0:T(8,128)}, u32[]{:S(2)}, u32[]{:S(2)}) collective-permute-start(f32[128,32,128]{2,1,0:T(8,128)} %get-tuple-element.48), channel_id=1, source_target_pairs={{1,0},{2,3},{5,4},{6,7},{9,8},{10,11},{13,12},{14,15},{17,16},{18,... | collective-permute-start | bytes 6291464 | tf_op jit(solution)/shard_map/ppermute | solution.py:331
  290.6 51.6 %collective-permute-start.9 = (f32[128,32,128]{2,1,0:T(8,128)}, f32[128,32,128]{2,1,0:T(8,128)}, u32[]{:S(2)}, u32[]{:S(2)}) collective-permute-start(f32[128,32,128]{2,1,0:T(8,128)} %collective-permute-done.3.p_ref), channel_id=1, source_target_pairs={{1,2},{2,1},{5,6},{6,5},{9,10},{10,9},{13,14},{14,13},{17,18},{18,... | collective-permute-start | bytes 6291464 | tf_op jit(solution)/shard_map/ppermute | solution.py:331
  292.6 51.9 %collective-permute-start.10 = (f32[128,32,128]{2,1,0:T(8,128)}, f32[128,32,128]{2,1,0:T(8,128)}, u32[]{:S(2)}, u32[]{:S(2)}) collective-permute-start(f32[128,32,128]{2,1,0:T(8,128)} %bitcast.15.b_ref), channel_id=1, source_target_pairs={{0,1},{3,2},{4,5},{7,6},{8,9},{11,10},{12,13},{15,14},{16,17},{19,... | collective-permute-start | bytes 6291464 | tf_op jit(solution)/shard_map/ppermute | solution.py:331
  357.4 48.0 %collective-permute-start.11 = (f32[128,32,128]{2,1,0:T(8,128)}, f32[128,32,128]{2,1,0:T(8,128)}, u32[]{:S(2)}, u32[]{:S(2)}) collective-permute-start(f32[128,32,128]{2,1,0:T(8,128)} %get-tuple-element.51), channel_id=1, source_target_pairs={{1,0},{2,3},{5,4},{6,7},{9,8},{10,11},{13,12},{14,15},{17,16},{18,... | collective-permute-start | bytes 6291464 | tf_op jit(solution)/shard_map/ppermute | solution.py:331
  358.7 54.6 %collective-permute-start.12 = (f32[128,32,128]{2,1,0:T(8,128)}, f32[128,32,128]{2,1,0:T(8,128)}, u32[]{:S(2)}, u32[]{:S(2)}) collective-permute-start(f32[128,32,128]{2,1,0:T(8,128)} %collective-permute-done.6.p_ref), channel_id=1, source_target_pairs={{1,2},{2,1},{5,6},{6,5},{9,10},{10,9},{13,14},{14,13},{17,18},{18,... | collective-permute-start | bytes 6291464 | tf_op jit(solution)/shard_map/ppermute | solution.py:331
  360.7 52.6 %collective-permute-start.13 = (f32[128,32,128]{2,1,0:T(8,128)}, f32[128,32,128]{2,1,0:T(8,128)}, u32[]{:S(2)}, u32[]{:S(2)}) collective-permute-start(f32[128,32,128]{2,1,0:T(8,128)} %bitcast.16.b_ref), channel_id=1, source_target_pairs={{0,1},{3,2},{4,5},{7,6},{8,9},{11,10},{12,13},{15,14},{16,17},{19,... | collective-permute-start | bytes 6291464 | tf_op jit(solution)/shard_map/ppermute | solution.py:331
  375.6 56.9 %collective-permute-start.14 = (f32[64,32,128]{2,1,0:T(8,128)}, f32[64,32,128]{2,1,0:T(8,128)}, u32[]{:S(2)}, u32[]{:S(2)}) collective-permute-start(f32[64,32,128]{2,1,0:T(8,128)} %bitcast.19.x_ref), channel_id=1, source_target_pairs={{0,1},{3,2},{4,5},{7,6},{8,9},{11,10},{12,13},{15,14},{16,17},{19,... | collective-permute-start | bytes 3145736 | tf_op jit(solution)/shard_map/ppermute | solution.py:331
  408.9 41.9 %all-to-all-start.4 = ((f32[8,2,8,32,128]{4,3,2,1,0:T(8,128)}), f32[8,2,8,32,128]{4,3,2,1,0:T(8,128)}, u32[]{:S(2)}, u32[]{:S(2)}) async-start(f32[8,2,8,32,128]{4,3,2,1,0:T(8,128)} %bitcast.18.refs_1_), calls=%async_computation.4 | async-start | bytes 4194304 | tf_op jit(solution)/shard_map/all_to_all | solution.py:334
  425.3 50.1 %collective-permute-start.18 = (f32[128,32,128]{2,1,0:T(8,128)}, f32[128,32,128]{2,1,0:T(8,128)}, u32[]{:S(2)}, u32[]{:S(2)}) collective-permute-start(f32[128,32,128]{2,1,0:T(8,128)} %get-tuple-element.60), channel_id=1, source_target_pairs={{1,0},{2,3},{5,4},{6,7},{9,8},{10,11},{13,12},{14,15},{17,16},{18,... | collective-permute-start | bytes 6291464 | tf_op jit(solution)/shard_map/ppermute | solution.py:331
  444.1 41.6 %collective-permute-start.19 = (f32[64,32,128]{2,1,0:T(8,128)S(1)}, f32[64,32,128]{2,1,0:T(8,128)}, u32[]{:S(2)}, u32[]{:S(2)}) collective-permute-start(f32[64,32,128]{2,1,0:T(8,128)S(1)} %bitcast.73), channel_id=1, source_target_pairs={{0,1},{3,2},{4,5},{7,6},{8,9},{11,10},{12,13},{15,14},{16,17},{19,... | collective-permute-start | bytes 3145736 | tf_op jit(solution)/shard_map/ppermute | solution.py:331
  478.9 54.7 %all-to-all-start.6 = ((f32[8,2,8,32,128]{4,3,2,1,0:T(8,128)}), f32[8,2,8,32,128]{4,3,2,1,0:T(8,128)}, u32[]{:S(2)}, u32[]{:S(2)}) async-start(f32[8,2,8,32,128]{4,3,2,1,0:T(8,128)} %bitcast.21.refs_2_), calls=%async_computation.6 | async-start | bytes 4194304 | tf_op jit(solution)/shard_map/all_to_all | solution.py:334
  531.1 44.1 %collective-permute-start.24 = (f32[64,32,128]{2,1,0:T(8,128)}, f32[64,32,128]{2,1,0:T(8,128)}, u32[]{:S(2)}, u32[]{:S(2)}) collective-permute-start(f32[64,32,128]{2,1,0:T(8,128)} %get-tuple-element.68), channel_id=1, source_target_pairs={{1,0},{2,3},{5,4},{6,7},{9,8},{10,11},{13,12},{14,15},{17,16},{18,... | collective-permute-start | bytes 3145736 | tf_op jit(solution)/shard_map/ppermute | solution.py:331
  533.6 44.0 %all-to-all-start.7 = ((f32[8,1,8,32,128]{4,3,2,1,0:T(8,128)}), f32[8,1,8,32,128]{4,3,2,1,0:T(8,128)S(1)}, u32[]{:S(2)}, u32[]{:S(2)}) async-start(f32[8,1,8,32,128]{4,3,2,1,0:T(8,128)} %bitcast.24.refs_3_), calls=%async_computation.7 | async-start | bytes 2097152 | tf_op jit(solution)/shard_map/all_to_all | solution.py:334
  (53 other events, 720.7 us)

commit v2 on v1

--- a/solution.py
+++ b/solution.py
@@ -47,6 +47,23 @@
             value = value + lax.ppermute(value, axis, pairs)
             step *= 2
     return value
+
+
+def run(body, grid, in_specs, out_specs, out_shape, args, done):
+    count, extra = len(args), len(done)
+
+    def kernel(*refs):
+        body(*refs[:count], *refs[count + extra :])
+
+    return pl.pallas_call(
+        kernel,
+        grid=grid,
+        in_specs=list(in_specs) + [pl.BlockSpec(memory_space=pltpu.HBM)] * extra,
+        out_specs=out_specs,
+        out_shape=out_shape,
+        compiler_params=pltpu.CompilerParams(vmem_limit_bytes=VMEM_LIMIT),
+        cost_estimate=pl.CostEstimate(flops=0, bytes_accessed=0, transcendentals=0),
+    )(*args, *done)
 
 
 def whole(array):
@@ -96,17 +113,17 @@
     product(left_parts(first_ref[...]), x2, o2, count, inner, True)
 
 
-def base_terms(x, t, first, last):
+def base_terms(x, t, first, last, *done):
     block = pl.BlockSpec((x.shape[0], 1) + x.shape[2:], lambda i: (0, i, 0, 0))
-    return pl.pallas_call(
+    return run(
         base_body,
-        grid=(x.shape[1],),
-        in_specs=[block, block, whole(first), whole(last)],
-        out_specs=block,
-        out_shape=jax.ShapeDtypeStruct(x.shape, f32),
-        compiler_params=pltpu.CompilerParams(vmem_limit_bytes=VMEM_LIMIT),
-        cost_estimate=pl.CostEstimate(flops=x.size * 4096, bytes_accessed=x.size * 12, transcendentals=0),
-    )(x, t, first, last)
+        (x.shape[1],),
+        [block, block, whole(first), whole(last)],
+        block,
+        jax.ShapeDtypeStruct(x.shape, f32),
+        (x, t, first, last,),
+        done,
+    )
 
 
 def one_body(x_ref, k_ref, o_ref):
@@ -116,17 +133,17 @@
     product(left_parts(k_ref[0]), x2, o2, count, inner, False)
 
 
-def one_terms(x, matrices):
-    block = pl.BlockSpec((x.shape[0], 1) + x.shape[2:], lambda i: (0, i, 0, 0, 0))
-    return pl.pallas_call(
+def one_terms(x, matrices, skip, states, *done):
+    block = lambda skip: pl.BlockSpec((x.shape[0], 1) + x.shape[2:], lambda i: (0, i + skip, 0, 0, 0))
+    return run(
         one_body,
-        grid=(x.shape[1],),
-        in_specs=[block, pl.BlockSpec((1,) + matrices.shape[1:], lambda i: (i, 0, 0))],
-        out_specs=block,
-        out_shape=jax.ShapeDtypeStruct(x.shape, f32),
-        compiler_params=pltpu.CompilerParams(vmem_limit_bytes=VMEM_LIMIT),
-        cost_estimate=pl.CostEstimate(flops=x.size * 4096, bytes_accessed=x.size * 8, transcendentals=0),
-    )(x, matrices)
+        (states,),
+        [block(skip), pl.BlockSpec((1,) + matrices.shape[1:], lambda i: (i + skip, 0, 0))],
+        block(0),
+        jax.ShapeDtypeStruct((x.shape[0], states) + x.shape[2:], f32),
+        (x, matrices,),
+        done,
+    )
 
 
 def one_cross_body(x_ref, a_ref, o_ref):
@@ -145,21 +162,21 @@
     o_ref[0] = folded(total)
 
 
-def one_cross(x, a, skip):
+def one_cross(x, a, skip, *done):
     count = x.shape[0] * x.shape[2]
     shape = (x.shape[0], 1) + x.shape[2:]
-    out = pl.pallas_call(
+    out = run(
         one_cross_body,
-        grid=(a.shape[1],),
-        in_specs=[
+        (a.shape[1],),
+        [
             pl.BlockSpec(shape, lambda i: (0, i + skip, 0, 0, 0)),
             pl.BlockSpec(shape, lambda i: (0, i, 0, 0, 0)),
         ],
-        out_specs=pl.BlockSpec((1, count, count), lambda i: (i, 0, 0)),
-        out_shape=jax.ShapeDtypeStruct((a.shape[1], count, count), f32),
-        compiler_params=pltpu.CompilerParams(vmem_limit_bytes=VMEM_LIMIT),
-        cost_estimate=pl.CostEstimate(flops=a.size * 4096, bytes_accessed=a.size * 8, transcendentals=0),
-    )(x, a)
+        pl.BlockSpec((1, count, count), lambda i: (i, 0, 0)),
+        jax.ShapeDtypeStruct((a.shape[1], count, count), f32),
+        (x, a,),
+        done,
+    )
     return out
 
 
@@ -197,25 +214,25 @@
     o3_ref[0] = folded(total)
 
 
-def local_cross(x, adjoints):
+def local_cross(x, adjoints, *done):
     wide, deep, rows, inner, width = x.shape
     block = lambda a: pl.BlockSpec((wide, a.shape[1], 1, inner, width), lambda i: (0, 0, i, 0, 0))
     count = wide * deep
-    zero, three = pl.pallas_call(
+    zero, three = run(
         functools.partial(local_body, PIECES),
-        grid=(rows,),
-        in_specs=[block(x)] + [block(a) for a in adjoints],
-        out_specs=[
+        (rows,),
+        [block(x)] + [block(a) for a in adjoints],
+        [
             pl.BlockSpec((1, count, count), lambda i: (i, 0, 0)),
             pl.BlockSpec((1, width, width), lambda i: (i, 0, 0)),
         ],
-        out_shape=[
+        [
             jax.ShapeDtypeStruct((rows, count, count), f32),
             jax.ShapeDtypeStruct((rows, width, width), f32),
         ],
-        compiler_params=pltpu.CompilerParams(vmem_limit_bytes=VMEM_LIMIT),
-        cost_estimate=pl.CostEstimate(flops=x.size * 4096, bytes_accessed=x.size * 8, transcendentals=0),
-    )(x, *adjoints)
+        (x, *adjoints,),
+        done,
+    )
     zero = jnp.sum(zero, axis=0)
     columns, at = [], 0
     for lo, hi in PIECES:
@@ -226,62 +243,116 @@
     return zero, jnp.sum(three, axis=0)
 
 
-def inner_body(slabs, w_ref, m_ref, x_ref, p_ref, q_ref, f_ref, b_ref, bp_ref, a_ref, y_ref, c_ref):
-    part = x_ref.shape[1]
-    width = x_ref.shape[2]
-
+def block_pair(refs, n):
+    sides = [jnp.concatenate([ref[k] for ref in refs], axis=0) for k in (n, n + 1)]
+    high, low = halves(jnp.concatenate(sides, axis=1))
+    return jnp.concatenate([high, low], axis=0)
+
+
+def pair_terms_body(w_ref, m_ref, x_ref, p_ref, q_ref, f_ref, own_ref, other_ref):
+    cells, part, width = x_ref.shape
     weights = left_parts(m_ref[...])
     gate = jnp.concatenate([w_ref[...], w_ref[...]], axis=1)
-    total = None
-    for n in range(0, slabs, 2):
-        high, low = [], []
-        for k in (n, n + 1):
-            rows = jnp.concatenate([x_ref[k], p_ref[k], q_ref[k], f_ref[k]], axis=0)
-            hi, lo = halves(rows)
-            high.append(hi)
-            low.append(lo)
-        high = jnp.concatenate(high, axis=1)
-        low = jnp.concatenate(low, axis=1)
-        both = jnp.concatenate([high, low], axis=0)
+    for n in range(0, cells, 2):
+        both = block_pair((x_ref, p_ref, q_ref, f_ref), n)
         out = jnp.dot(weights, both, preferred_element_type=f32)
         rows = out.shape[0] // 2
         out = out[:rows] + out[rows:]
         out = out[: rows // 2] + gate * out[rows // 2 :]
-        own = jnp.concatenate([b_ref[n], b_ref[n + 1]], axis=1) + out[:part]
-        other = jnp.concatenate([bp_ref[n], bp_ref[n + 1]], axis=1) + out[part:]
         for k in (0, 1):
-            a_ref[n + k] = own[:, k * width : (k + 1) * width]
-            y_ref[n + k] = out[part:, k * width : (k + 1) * width]
-        hi, lo = halves(jnp.concatenate([own, other], axis=0))
-        cross = lax.dot_general(
-            both,
-            jnp.concatenate([hi, lo], axis=0),
+            own_ref[n + k] = out[:part, k * width : (k + 1) * width]
+            other_ref[n + k] = out[part:, k * width : (k + 1) * width]
+
+
+def pair_cross_body(x_ref, p_ref, q_ref, f_ref, own_ref, base_ref, terms_ref, c_ref):
+    total = None
+    for n in range(0, x_ref.shape[0], 2):
+        sides = [
+            jnp.concatenate([own_ref[k], base_ref[k] + terms_ref[k]], axis=0) for k in (n, n + 1)
+        ]
+        high, low = halves(jnp.concatenate(sides, axis=1))
+        term = lax.dot_general(
+            block_pair((x_ref, p_ref, q_ref, f_ref), n),
+            jnp.concatenate([high, low], axis=0),
             ROWS_BY_ROWS,
             preferred_element_type=f32,
         )
-        total = cross if total is None else total + cross
+        total = term if total is None else total + term
     c_ref[0] = folded(total)
 
 
-def inner_terms(gate, weights, x, p, q, f, b, bp):
-    count, part, width = x.shape
-    slabs = 16
-    block = pl.BlockSpec((slabs, part, width), lambda i: (i, 0, 0))
-    return pl.pallas_call(
-        functools.partial(inner_body, slabs),
-        grid=(count // slabs,),
-        in_specs=[whole(gate), whole(weights)] + [block] * 6,
-        out_specs=[block, block, pl.BlockSpec((1, 4 * part, 2 * part), lambda i: (i, 0, 0))],
-        out_shape=[
-            jax.ShapeDtypeStruct(x.shape, f32),
-            jax.ShapeDtypeStruct(x.shape, f32),
-            jax.ShapeDtypeStruct((count // slabs, 4 * part, 2 * part), f32),
-        ],
-        compiler_params=pltpu.CompilerParams(vmem_limit_bytes=VMEM_LIMIT),
-        cost_estimate=pl.CostEstimate(
-            flops=count * 6 * 2 * 128 * 128 * 128, bytes_accessed=count * part * width * 4 * 8, transcendentals=0
-        ),
-    )(gate, weights, x, p, q, f, b, bp)
+def pair_terms(gate, weights, blocks, *done):
+    count, part, width = blocks[0].shape
+    cells = 16
+    block = pl.BlockSpec((cells, part, width), lambda i: (i, 0, 0))
+    return run(
+        pair_terms_body,
+        (count // cells,),
+        [whole(gate), whole(weights)] + [block] * 4,
+        [block, block],
+        [jax.ShapeDtypeStruct(blocks[0].shape, f32)] * 2,
+        (gate, weights, *blocks,),
+        done,
+    )
+
+
+def pair_cross(blocks, *done):
+    count, part, width = blocks[0].shape
+    cells = 16
+    block = pl.BlockSpec((cells, part, width), lambda i: (i, 0, 0))
+    shape = (count // cells, 4 * part, 2 * part)
+    return run(
+        pair_cross_body,
+        (count // cells,),
+        [block] * 7,
+        pl.BlockSpec((1,) + shape[1:], lambda i: (i, 0, 0)),
+        jax.ShapeDtypeStruct(shape, f32),
+        (*blocks,),
+        done,
+    )
+
+
+def copy_body(x_ref, o_ref):
+    o_ref[...] = x_ref[...]
+
+
+def sum_body(*refs):
+    total = refs[0][...]
+    for ref in refs[1:-1]:
+        total = total + ref[...]
+    refs[-1][...] = total
+
+
+def piece_of(lo, hi, skip, shape):
+    size = hi - lo
+    return pl.BlockSpec((1, size) + shape[2:], lambda i: (i, (lo - skip) // size, 0, 0, 0))
+
+
+def cut_piece(x, lo, hi, *done):
+    out = jax.ShapeDtypeStruct((x.shape[0], hi - lo) + x.shape[2:], f32)
+    return run(
+        copy_body, (x.shape[0],), [piece_of(lo, hi, 0, x.shape)], piece_of(lo, hi, lo, x.shape), out, (x,), done
+    )
+
+
+def add_piece(x, y, skip, lo, hi, *done):
+    out = jax.ShapeDtypeStruct((x.shape[0], hi - lo) + x.shape[2:], f32)
+    return run(
+        sum_body,
+        (x.shape[0],),
+        [piece_of(lo, hi, 0, x.shape), piece_of(lo, hi, skip, x.shape)],
+        piece_of(lo, hi, lo, x.shape),
+        out,
+        (x, y),
+        done,
+    )
+
+
+def add_all(arrays, *done):
+    shape = arrays[0].shape
+    block = pl.BlockSpec((shape[0] // 4,) + shape[1:], lambda i: (i, 0, 0))
+    out = jax.ShapeDtypeStruct(shape, f32)
+    return run(sum_body, (4,), [block] * len(arrays), block, out, tuple(arrays), done)
 
 
 def line_device(
@@ -333,82 +404,78 @@
     def exchange(value):
         return lax.all_to_all(value, "wide", 0, 0, tiled=True)
 
-    def after(value, *done):
-        return lax.optimization_barrier((value,) + done)[0]
-
-    xs = [xv[:, lo:hi].reshape(-1, part, size_large) for lo, hi in PIECES]
-    ps, qs, fs = [], [], []
-    for k in range(len(PIECES)):
-        piece = xs[k] if k < 2 else after(xs[k], ps[k - 2])
-        ps.append(shift(piece, TO_INNER))
-        qs.append(shift(piece, INNER_SWAP))
-        fs.append(shift(ps[k], INNER_SWAP))
-
-    base = base_terms(initial, target, step_size * gen_small[0].T, step_size * gen_large[1])
-
-    wide_x = [exchange(xv[:, :half])]
-    first = after(wide_x[0], base, ps[0], qs[0])
-    back = [exchange(one_terms(first, mode_one[:half]))]
-    wide_x.append(exchange(after(xv[:, half:], back[0])))
-    bases = []
-
-    def add_base(k):
+    count = len(PIECES)
+    xs, ps, qs, fs = ([None] * count for _ in range(4))
+    bases, others, own, other, far = ([None] * count for _ in range(5))
+    adjoints, wide_a, ones, twos = ([None] * count for _ in range(4))
+
+    def flat(value):
+        return value.reshape(-1, part, size_large)
+
+    def send_piece(k, *done):
+        xs[k] = flat(cut_piece(xv, *PIECES[k], *done))
+        ps[k] = shift(xs[k], TO_INNER)
+        qs[k] = shift(xs[k], INNER_SWAP)
+        fs[k] = shift(ps[k], INNER_SWAP)
+
+    def base_step(k, *done):
         lo, hi = PIECES[k]
-        at = lo % half
-        total = base.reshape(xv.shape)[:, lo:hi] + back[lo // half][:, at : at + hi - lo]
-        bases.append(total.reshape(-1, part, size_large))
-
-    back[0] = after(back[0], ps[1], qs[1])
-    add_base(0)
-    add_base(1)
-    others = [shift(b, TO_INNER) for b in bases]
-    second = after(wide_x[1], fs[0], ps[2], *bases)
-    back.append(exchange(one_terms(second, mode_one[half:])))
-
-    adjoints, wide_a, sums_two, own, far = [], [], [], [], []
-
-    def inner_step(k, *done):
-        b = after(bases[k], *done) if done else bases[k]
-        a, y, c2 = inner_terms(gate, weights, xs[k], ps[k], qs[k], fs[k], b, others[k])
-        sums_two.append(c2)
-        own.append(a)
-        far.append(shift(y, TO_OUTER))
+        bases[k] = flat(add_piece(base.reshape(xv.shape), back[lo // half], lo // half * half, lo, hi, *done))
+        others[k] = shift(bases[k], TO_INNER)
+
+    def terms_step(k, *done):
+        own[k], other[k] = pair_terms(gate, weights, (xs[k], ps[k], qs[k], fs[k]), *done)
+        far[k] = shift(other[k], TO_OUTER)
 
     def finish(k, *done):
-        a = after(own[k], *done) if done else own[k]
         lo, hi = PIECES[k]
-        adjoints.append((a + far[k]).reshape(wide, hi - lo, rows, part, size_large))
-        wide_a.append(exchange(adjoints[k]))
-
-    inner_step(0)
-    back[1] = after(back[1], own[0], qs[2])
+        total = add_all((own[k], far[k], bases[k]), *done)
+        adjoints[k] = total.reshape(wide, hi - lo, rows, part, size_large)
+        wide_a[k] = exchange(adjoints[k])
+
+    def one_step(k, *done):
+        ones[k] = one_cross(wide_x, wide_a[k], PIECES[k][0], *done)
+
+    def two_step(k, *done):
+        twos[k] = pair_cross((xs[k], ps[k], qs[k], fs[k], flat(adjoints[k]), others[k], other[k]), *done)
+
+    wide_x = exchange(xv)
+    send_piece(0)
+    send_piece(1)
     for k in (2, 3, 4):
-        add_base(k)
-        others.append(shift(bases[k], TO_INNER))
-    finish(0, bases[2])
-    inner_step(1, adjoints[0])
-    finish(1, own[1])
-    inner_step(2, adjoints[1])
-    ones = []
-
-    def cross_step(k, *done):
-        a = after(wide_a[k], *done)
-        lo, _ = PIECES[k]
-        ones.append(one_cross(wide_x[lo // half], a, lo % half))
-
-    cross_step(0, own[2])
-    cross_step(1, ones[0])
-    inner_step(3, ones[1])
+        send_piece(k, xs[1])
+    base = base_terms(initial, target, step_size * gen_small[0].T, step_size * gen_large[1], xs[4])
+    one_first = one_terms(wide_x, mode_one, 0, half, base, ps[0], qs[0], ps[1], qs[1])
+    one_second = one_terms(wide_x, mode_one, half, deep - half, one_first)
+    back = [exchange(one_first), exchange(one_second)]
+    terms_step(0, one_second)
+    base_step(0, own[0])
+    base_step(1, bases[0])
+    terms_step(1, bases[1], ps[2], ps[3], ps[4])
+    base_step(2, own[1])
+    base_step(3, bases[2])
+    base_step(4, bases[3])
+    finish(0, bases[4])
+    terms_step(2, adjoints[0])
+    finish(1, own[2])
+    two_step(0, adjoints[1])
+    two_step(1, twos[0])
+    terms_step(3, twos[1])
     finish(2, own[3])
-    inner_step(4, adjoints[2])
+    one_step(0, adjoints[2])
+    one_step(1, ones[0])
+    two_step(2, ones[1])
+    terms_step(4, twos[2])
     finish(3, own[4])
-    cross_step(2, adjoints[3])
-    finish(4, ones[2])
+    one_step(2, adjoints[3])
+    two_step(3, ones[2])
+    finish(4, twos[3])
     cross_zero, cross_three = local_cross(xv, adjoints)
-    cross_step(3, cross_three)
-    cross_step(4, ones[3])
+    two_step(4, cross_three)
+    one_step(3, twos[4])
+    one_step(4, ones[3])
     cross_one = jnp.sum(jnp.concatenate(ones, axis=0), axis=0)
-    found = jnp.where(inner, jnp.sum(jnp.concatenate(sums_two, axis=0), axis=0), 0.0)
+    found = jnp.where(inner, jnp.sum(jnp.concatenate(twos, axis=0), axis=0), 0.0)
     cross_two = jnp.einsum("xr,xy,yc->rc", spread, found, spread[: 2 * part], precision=highest)
 
     packed = jnp.concatenate(

time: 646 us -> 565 us (0.87)
  waiting for transfers between devices: 263 us -> 148 us
  Pallas kernels: 112 us -> 180 us
  blocking collectives: 52.8 us -> 0 us
  starting transfers between devices: 129 us -> 156 us
  other arithmetic: 36.9 us -> 15 us
  local copies, waits for them, and re-layouts: 43 us -> 54.6 us
    ppermute x25, waiting for transfers between devices: 237 us -> 105 us  [shift(): return lax.ppermute(value, 'narrow', pairs)]
    pallas_call x14 -> x34, Pallas kernels: 112 us -> 180 us  [run(): pl.pallas_call(kernel, grid=grid, in_specs=list(in_specs) + [pl.BlockSpec...]
    all_to_all x1 -> x0, blocking collectives: 52.8 us -> none  [exchange(): return lax.all_to_all(value, 'wide', 0, 0, tiled=True)]
    unnamed x81 -> x174, local copies, waits for them, and re-layouts: 14.8 us -> 44.1 us
    add x9 -> x0, other arithmetic: 27.8 us -> none  [the longest x5 14 us: finish(): adjoints.append((a + far[k]).reshape(wide, hi - lo, rows, part, size_large))]
    ppermute x25, starting transfers between devices: 89.2 us -> 115 us  [shift(): return lax.ppermute(value, 'narrow', pairs)]
    all_to_all x8, waiting for transfers between devices: 0.02 us -> 21.2 us  [exchange(): return lax.all_to_all(value, 'wide', 0, 0, tiled=True)]
    slice x4 -> x0, local copies, waits for them, and re-layouts: 17.5 us -> none  [the longest x2 8.98 us: line_device(): xs = [xv[:, lo:hi].reshape(-1, part, size_large) for lo, hi in PIECES]]
  transfers between devices with their start and end apart: 38 -> 38, of which waited for: 18 -> 13; matrix products, arithmetic and copies ran while one was open for 7% -> 3% of each run, Pallas kernels for 14% -> 30%
where the time goes in v2:
time: 565 us; the launch traced here: 561 us
  Pallas kernels  180 us (32%)
  starting transfers between devices  156 us (28%)
  waiting for transfers between devices  148 us (26%)
  local copies, waits for them, and re-layouts  54.6 us (10%)
  other arithmetic  15 us (3%)
  between operations  6.04 us (1%)
    pallas_call x34, Pallas kernels, run(): pl.pallas_call(kernel, grid=grid, in_specs=list(in_specs) + [pl.BlockSpec...  180 us
    ppermute x25, starting transfers between devices, shift(): return lax.ppermute(value, 'narrow', pairs)  115 us
    ppermute x25, waiting for transfers between devices, shift(): return lax.ppermute(value, 'narrow', pairs)  105 us
    unnamed x174, local copies, waits for them, and re-layouts  44.1 us
    all_to_all x8, starting transfers between devices, exchange(): return lax.all_to_all(value, 'wide', 0, 0, tiled=True)  36.2 us
    ppermute x5, waiting for transfers between devices, all_sum(): value = value + lax.ppermute(value, axis, pairs)  21.4 us
    all_to_all x8, waiting for transfers between devices, exchange(): return lax.all_to_all(value, 'wide', 0, 0, tiled=True)  21.2 us
  transfers between devices with their start and end apart: 38, of which 13 were waited for; matrix products, arithmetic and copies ran while one was open for 3% of the time, Pallas kernels for 30%

profile of v2, /device:TPU:0, one launch (start us, length us, event | category | flops | bytes accessed | tf_op | source)
XLA Modules:
  0.0 561.0 jit_solution(5116969346304245269)
XLA Ops:
  9.5 6.2 %collective-permute-start.3 = (f32[128,32,128]{2,1,0:T(8,128)S(1)}, f32[128,32,128]{2,1,0:T(8,128)}, u32[]{:S(2)}, u32[]{:S(2)}) collective-permute-start(f32[128,32,128]{2,1,0:T(8,128)S(1)} %bitcast.76), channel_id=1, source_target_pairs={{0,1},{3,2},{4,5},{7,6},{8,9},{11,10},{12,13},{15,14},{16,17},{19,... | collective-permute-start | bytes 6291464 | tf_op jit(solution)/shard_map/ppermute | solution.py:402
  39.4 21.2 %shard_map.116.refs_2_ = f32[64,8,32,128]{3,2,1,0:T(8,128)S(1)} custom-call(f32[64,8,32,128]{3,2,1,0:T(8,128)} %refs_0_.1, f32[64,8,32,128]{3,2,1,0:T(8,128)} %refs_1_.1, f32[64,64]{1,0:T(8,128)S(1)} %copy.31.refs_2_, f32[128,128]{1,0:T(8,128)S(1)} %fusion.1.refs_3_, f32[64,32,128]{2,1,0:T(8,128)S(1)} %bitcast.101), custom_call_target="tpu_custom_call" | custom-call | tf_op jit(solution)/shard_map/pallas_call | solution.py:58
  64.0 40.9 %collective-permute-done.refs_3_.refs_1_ = f32[128,32,128]{2,1,0:T(8,128)} collective-permute-done((f32[128,32,128]{2,1,0:T(8,128)}, f32[128,32,128]{2,1,0:T(8,128)}, u32[]{:S(2)}, u32[]{:S(2)}) %collective-permute-start) | collective-permute-done | bytes 2097184 | tf_op jit(solution)/shard_map/ppermute | solution.py:402
  104.8 6.7 %shard_map.117.refs_2_ = f32[8,4,8,32,128]{4,3,2,1,0:T(8,128)S(1)} custom-call(f32[8,8,8,32,128]{4,3,2,1,0:T(8,128)} %all-to-all-done.refs_0_, f32[8,64,64]{2,1,0:T(8,128)S(1)} %add_multiply_fusion.refs_1_, f32[64,8,32,128]{3,2,1,0:T(8,128)} %copy-done.3, f32[128,32,128]{2,1,0:T(8,128)} %collective-permute-done.refs_3_.refs_1_, ...), custom_call_target="tpu_custom_call" | custom-call | tf_op jit(solution)/shard_map/pallas_call | solution.py:58
  126.5 8.5 %collective-permute-start.7 = (f32[128,32,128]{2,1,0:T(8,128)}, f32[128,32,128]{2,1,0:T(8,128)}, u32[]{:S(2)}, u32[]{:S(2)}) collective-permute-start(f32[128,32,128]{2,1,0:T(8,128)} %bitcast.16.refs_2_.refs_0_), channel_id=1, source_target_pairs={{0,1},{3,2},{4,5},{7,6},{8,9},{11,10},{12,13},{15,14},{16,17},{19,... | collective-permute-start | bytes 6291464 | tf_op jit(solution)/shard_map/ppermute | solution.py:402
  137.2 6.8 %shard_map.118.refs_6_ = f32[8,4,8,32,128]{4,3,2,1,0:T(8,128)S(1)} custom-call(f32[8,8,8,32,128]{4,3,2,1,0:T(8,128)} %all-to-all-done.refs_0_, f32[8,64,64]{2,1,0:T(8,128)S(1)} %add_multiply_fusion.refs_1_, f32[8,4,8,32,128]{4,3,2,1,0:T(8,128)S(1)} %copy-done.15), custom_call_target="tpu_custom_call" | custom-call | tf_op jit(solution)/shard_map/pallas_call | solution.py:58
  146.1 21.2 %all-to-all-done.1.refs_1_ = f32[8,4,8,32,128]{4,3,2,1,0:T(8,128)} async-done(((f32[8,4,8,32,128]{4,3,2,1,0:T(8,128)}), f32[8,4,8,32,128]{4,3,2,1,0:T(8,128)}, u32[]{:S(2)}, u32[]{:S(2)}) %all-to-all-start.1) | async-done | bytes 4194336 | tf_op jit(solution)/shard_map/all_to_all | solution.py:405
  173.9 8.4 %shard_map.119 = (f32[128,32,128]{2,1,0:T(8,128)S(1)}, f32[128,32,128]{2,1,0:T(8,128)}) custom-call(f32[1,128]{1,0:T(1,128)S(1)} %convert_bitcast_fusion.refs_0_, f32[128,128]{1,0:T(8,128)S(1)} %fusion.3.refs_1_, f32[128,32,128]{2,1,0:T(8,128)} %bitcast.4.refs_2_.refs_0_, f32[128,32,128]{2,1,0:T(8,128)} %collective-permute-done.refs_3_.refs_1_, ...), custom_call_target="tpu_custom_call" | custom-call | tf_op jit(solution)/shard_map/pallas_call | solution.py:58
  183.7 10.8 %collective-permute-start.9 = (f32[64,32,128]{2,1,0:T(8,128)S(1)}, f32[64,32,128]{2,1,0:T(8,128)}, u32[]{:S(2)}, u32[]{:S(2)}) collective-permute-start(f32[64,32,128]{2,1,0:T(8,128)S(1)} %bitcast.102), channel_id=1, source_target_pairs={{0,1},{3,2},{4,5},{7,6},{8,9},{11,10},{12,13},{15,14},{16,17},{19,... | collective-permute-start | bytes 3145736 | tf_op jit(solution)/shard_map/ppermute | solution.py:402
  199.4 17.6 %collective-permute-done.9.refs_9_.refs_3_.refs_1_ = f32[64,32,128]{2,1,0:T(8,128)} collective-permute-done((f32[64,32,128]{2,1,0:T(8,128)S(1)}, f32[64,32,128]{2,1,0:T(8,128)}, u32[]{:S(2)}, u32[]{:S(2)}) %collective-permute-start.9) | collective-permute-done | bytes 1048608 | tf_op jit(solution)/shard_map/ppermute | solution.py:402
  232.2 6.4 %collective-permute-done.8.refs_8_.refs_3_.refs_1_ = f32[64,32,128]{2,1,0:T(8,128)S(1)} collective-permute-done((f32[64,32,128]{2,1,0:T(8,128)S(1)}, f32[64,32,128]{2,1,0:T(8,128)S(1)}, u32[]{:S(2)}, u32[]{:S(2)}) %collective-permute-start.8) | collective-permute-done | bytes 1048608 | tf_op jit(solution)/shard_map/ppermute | solution.py:402
  239.9 8.0 %shard_map.124 = (f32[128,32,128]{2,1,0:T(8,128)S(1)}, f32[128,32,128]{2,1,0:T(8,128)}) custom-call(f32[1,128]{1,0:T(1,128)S(1)} %convert_bitcast_fusion.refs_0_, f32[128,128]{1,0:T(8,128)S(1)} %fusion.3.refs_1_, f32[128,32,128]{2,1,0:T(8,128)S(1)} %bitcast.81, f32[128,32,128]{2,1,0:T(8,128)} %collective-permute-done.3.refs_5_.refs_3_.refs_1_, ...), custom_call_target="tpu_custom_call" | custom-call | tf_op jit(solution)/shard_map/pallas_call | solution.py:58
  276.6 7.5 %collective-permute-start.17 = (f32[128,32,128]{2,1,0:T(8,128)}, f32[128,32,128]{2,1,0:T(8,128)}, u32[]{:S(2)}, u32[]{:S(2)}) collective-permute-start(f32[128,32,128]{2,1,0:T(8,128)} %bitcast.99), channel_id=1, source_target_pairs={{0,1},{3,2},{4,5},{7,6},{8,9},{11,10},{12,13},{15,14},{16,17},{19,... | collective-permute-start | bytes 6291464 | tf_op jit(solution)/shard_map/ppermute | solution.py:402
  286.8 8.4 %shard_map.129 = (f32[128,32,128]{2,1,0:T(8,128)S(1)}, f32[128,32,128]{2,1,0:T(8,128)}) custom-call(f32[1,128]{1,0:T(1,128)S(1)} %convert_bitcast_fusion.refs_0_, f32[128,128]{1,0:T(8,128)S(1)} %fusion.3.refs_1_, f32[128,32,128]{2,1,0:T(8,128)} %bitcast.16.refs_2_.refs_0_, f32[128,32,128]{2,1,0:T(8,128)} %collective-permute-done.7.refs_7_.refs_3_.refs_1_, ...), custom_call_target="tpu_custom_call" | custom-call | tf_op jit(solution)/shard_map/pallas_call | solution.py:58
  309.7 19.3 %collective-permute-done.17.refs_5_ = f32[128,32,128]{2,1,0:T(8,128)} collective-permute-done((f32[128,32,128]{2,1,0:T(8,128)}, f32[128,32,128]{2,1,0:T(8,128)}, u32[]{:S(2)}, u32[]{:S(2)}) %collective-permute-start.17) | collective-permute-done | bytes 2097184 | tf_op jit(solution)/shard_map/ppermute | solution.py:402
  329.0 17.8 %collective-permute-start.21 = (f32[128,32,128]{2,1,0:T(8,128)}, f32[128,32,128]{2,1,0:T(8,128)}, u32[]{:S(2)}, u32[]{:S(2)}) collective-permute-start(f32[128,32,128]{2,1,0:T(8,128)} %bitcast.93), channel_id=1, source_target_pairs={{0,1},{3,2},{4,5},{7,6},{8,9},{11,10},{12,13},{15,14},{16,17},{19,... | collective-permute-start | bytes 6291464 | tf_op jit(solution)/shard_map/ppermute | solution.py:402
  348.4 8.5 %shard_map.131.refs_7_ = f32[8,128,64]{2,1,0:T(8,128)S(1)} custom-call(f32[128,32,128]{2,1,0:T(8,128)} %bitcast.4.refs_2_.refs_0_, f32[128,32,128]{2,1,0:T(8,128)} %collective-permute-done.refs_3_.refs_1_, f32[128,32,128]{2,1,0:T(8,128)} %collective-permute-done.1.refs_4_.refs_2_, f32[128,32,128]{2,1,0:T(8,128)} %collective-permute-done.2.refs_5_.refs_3_, ...), custom_call_target="tpu_custom_call" | custom-call | tf_op jit(solution)/shard_map/pallas_call | solution.py:58
  356.9 17.0 %collective-permute-done.16.refs_5_ = f32[128,32,128]{2,1,0:T(8,128)} collective-permute-done((f32[128,32,128]{2,1,0:T(8,128)}, f32[128,32,128]{2,1,0:T(8,128)}, u32[]{:S(2)}, u32[]{:S(2)}) %collective-permute-start.16) | collective-permute-done | bytes 2097184 | tf_op jit(solution)/shard_map/ppermute | solution.py:402
  373.9 7.6 %shard_map.132.refs_6_ = f32[8,128,64]{2,1,0:T(8,128)S(1)} custom-call(f32[128,32,128]{2,1,0:T(8,128)S(1)} %bitcast.82, f32[128,32,128]{2,1,0:T(8,128)} %collective-permute-done.3.refs_5_.refs_3_.refs_1_, f32[128,32,128]{2,1,0:T(8,128)} %collective-permute-done.4.refs_6_.refs_4_.refs_2_, f32[128,32,128]{2,1,0:T(8,128)S(1)} %copy-done.30, ...), custom_call_target="tpu_custom_call" | custom-call | tf_op jit(solution)/shard_map/pallas_call | solution.py:58
  397.0 12.8 %collective-permute-start.23 = (f32[64,32,128]{2,1,0:T(8,128)}, f32[64,32,128]{2,1,0:T(8,128)}, u32[]{:S(2)}, u32[]{:S(2)}) collective-permute-start(f32[64,32,128]{2,1,0:T(8,128)} %bitcast.19.refs_2_), channel_id=1, source_target_pairs={{0,1},{3,2},{4,5},{7,6},{8,9},{11,10},{12,13},{15,14},{16,17},{19,... | collective-permute-start | bytes 3145736 | tf_op jit(solution)/shard_map/ppermute | solution.py:402
  420.5 8.4 %shard_map.137.refs_6_ = f32[8,128,64]{2,1,0:T(8,128)S(1)} custom-call(f32[128,32,128]{2,1,0:T(8,128)} %bitcast.16.refs_2_.refs_0_, f32[128,32,128]{2,1,0:T(8,128)} %collective-permute-done.7.refs_7_.refs_3_.refs_1_, f32[128,32,128]{2,1,0:T(8,128)} %collective-permute-done.11.refs_4_.refs_2_, f32[128,32,128]{2,1,0:T(8,128)} %collective-permute-done.12.refs_5_.refs_3_, ...), custom_call_target="tpu_custom_call" | custom-call | tf_op jit(solution)/shard_map/pallas_call | solution.py:58
  443.6 24.3 %collective-permute-start.24 = (f32[64,32,128]{2,1,0:T(8,128)}, f32[64,32,128]{2,1,0:T(8,128)}, u32[]{:S(2)}, u32[]{:S(2)}) collective-permute-start(f32[64,32,128]{2,1,0:T(8,128)} %bitcast.20.refs_3_.refs_2_), channel_id=1, source_target_pairs={{0,1},{3,2},{4,5},{7,6},{8,9},{11,10},{12,13},{15,14},{16,17},{19,... | collective-permute-start | bytes 3145736 | tf_op jit(solution)/shard_map/ppermute | solution.py:402
  495.8 14.2 %shard_map.143 = (f32[8,64,64]{2,1,0:T(8,128)S(1)}, f32[8,128,128]{2,1,0:T(8,128)S(1)}) custom-call(f32[8,8,8,32,128]{4,3,2,1,0:T(8,128)} %bitcast.65, f32[8,2,8,32,128]{4,3,2,1,0:T(8,128)S(1)} %bitcast.88, f32[8,2,8,32,128]{4,3,2,1,0:T(8,128)S(1)} %bitcast.85, f32[8,2,8,32,128]{4,3,2,1,0:T(8,128)S(1)} %bitcast.91, ...), custom_call_target="tpu_custom_call" | custom-call | tf_op jit(solution)/shard_map/pallas_call | solution.py:58
  544.6 6.6 %collective-permute-done.29 = f32[320,128]{1,0:T(8,128)S(1)} collective-permute-done((f32[320,128]{1,0:T(8,128)S(1)}, f32[320,128]{1,0:T(8,128)S(1)}, u32[]{:S(2)}, u32[]{:S(2)}) %collective-permute-start.29) | collective-permute-done | bytes 163872 | tf_op jit(solution)/shard_map/ppermute | solution.py:47
  (338 shorter events, 240.0 us)
Async XLA Ops:
  0.6 104.2 %all-to-all-start = ((f32[8,8,8,32,128]{4,3,2,1,0:T(8,128)}), f32[8,8,8,32,128]{4,3,2,1,0:T(8,128)}, u32[]{:S(2)}, u32[]{:S(2)}) async-start(f32[8,8,8,32,128]{4,3,2,1,0:T(8,128)} %bitcast.64), calls=%async_computation | async-start | bytes 16777216 | tf_op jit(solution)/shard_map/all_to_all | solution.py:405
  9.5 54.5 %collective-permute-start.3 = (f32[128,32,128]{2,1,0:T(8,128)S(1)}, f32[128,32,128]{2,1,0:T(8,128)}, u32[]{:S(2)}, u32[]{:S(2)}) collective-permute-start(f32[128,32,128]{2,1,0:T(8,128)S(1)} %bitcast.76), channel_id=1, source_target_pairs={{0,1},{3,2},{4,5},{7,6},{8,9},{11,10},{12,13},{15,14},{16,17},{19,... | collective-permute-start | bytes 6291464 | tf_op jit(solution)/shard_map/ppermute | solution.py:402
  15.7 48.3 %collective-permute-start.4 = (f32[128,32,128]{2,1,0:T(8,128)S(1)}, f32[128,32,128]{2,1,0:T(8,128)}, u32[]{:S(2)}, u32[]{:S(2)}) collective-permute-start(f32[128,32,128]{2,1,0:T(8,128)S(1)} %bitcast.77), channel_id=1, source_target_pairs={{1,2},{2,1},{5,6},{6,5},{9,10},{10,9},{13,14},{14,13},{17,18},{18,... | collective-permute-start | bytes 6291464 | tf_op jit(solution)/shard_map/ppermute | solution.py:402
  20.7 84.1 %collective-permute-start = (f32[128,32,128]{2,1,0:T(8,128)}, f32[128,32,128]{2,1,0:T(8,128)}, u32[]{:S(2)}, u32[]{:S(2)}) collective-permute-start(f32[128,32,128]{2,1,0:T(8,128)} %bitcast.4.refs_2_.refs_0_), channel_id=1, source_target_pairs={{0,1},{3,2},{4,5},{7,6},{8,9},{11,10},{12,13},{15,14},{16,17},{19,... | collective-permute-start | bytes 6291464 | tf_op jit(solution)/shard_map/ppermute | solution.py:402
  23.5 81.3 %collective-permute-start.1 = (f32[128,32,128]{2,1,0:T(8,128)}, f32[128,32,128]{2,1,0:T(8,128)}, u32[]{:S(2)}, u32[]{:S(2)}) collective-permute-start(f32[128,32,128]{2,1,0:T(8,128)} %bitcast.4.refs_2_.refs_0_), channel_id=1, source_target_pairs={{1,2},{2,1},{5,6},{6,5},{9,10},{10,9},{13,14},{14,13},{17,18},{18,... | collective-permute-start | bytes 6291464 | tf_op jit(solution)/shard_map/ppermute | solution.py:402
  113.6 53.7 %all-to-all-start.1 = ((f32[8,4,8,32,128]{4,3,2,1,0:T(8,128)}), f32[8,4,8,32,128]{4,3,2,1,0:T(8,128)}, u32[]{:S(2)}, u32[]{:S(2)}) async-start(f32[8,4,8,32,128]{4,3,2,1,0:T(8,128)} %copy-done.14), calls=%async_computation.1 | async-start | bytes 8388608 | tf_op jit(solution)/shard_map/all_to_all | solution.py:405
  118.1 55.8 %collective-permute-start.2 = (f32[128,32,128]{2,1,0:T(8,128)}, f32[128,32,128]{2,1,0:T(8,128)}, u32[]{:S(2)}, u32[]{:S(2)}) collective-permute-start(f32[128,32,128]{2,1,0:T(8,128)} %collective-permute-done.refs_3_.refs_1_), channel_id=1, source_target_pairs={{1,2},{2,1},{5,6},{6,5},{9,10},{10,9},{13,14},{14,13},{17,18},{18,... | collective-permute-start | bytes 6291464 | tf_op jit(solution)/shard_map/ppermute | solution.py:402
  126.5 92.4 %collective-permute-start.7 = (f32[128,32,128]{2,1,0:T(8,128)}, f32[128,32,128]{2,1,0:T(8,128)}, u32[]{:S(2)}, u32[]{:S(2)}) collective-permute-start(f32[128,32,128]{2,1,0:T(8,128)} %bitcast.16.refs_2_.refs_0_), channel_id=1, source_target_pairs={{0,1},{3,2},{4,5},{7,6},{8,9},{11,10},{12,13},{15,14},{16,17},{19,... | collective-permute-start | bytes 6291464 | tf_op jit(solution)/shard_map/ppermute | solution.py:402
  167.3 83.2 %all-to-all-start.2 = ((f32[8,4,8,32,128]{4,3,2,1,0:T(8,128)}), f32[8,4,8,32,128]{4,3,2,1,0:T(8,128)}, u32[]{:S(2)}, u32[]{:S(2)}) async-start(f32[8,4,8,32,128]{4,3,2,1,0:T(8,128)} %copy-done.16), calls=%async_computation.2 | async-start | bytes 8388608 | tf_op jit(solution)/shard_map/all_to_all | solution.py:405
  173.1 65.5 %collective-permute-start.6 = (f32[128,32,128]{2,1,0:T(8,128)}, f32[128,32,128]{2,1,0:T(8,128)S(1)}, u32[]{:S(2)}, u32[]{:S(2)}) collective-permute-start(f32[128,32,128]{2,1,0:T(8,128)} %collective-permute-done.3.refs_5_.refs_3_.refs_1_), channel_id=1, source_target_pairs={{1,2},{2,1},{5,6},{6,5},{9,10},{10,9},{13,14},{14,13},{17,18},{18,... | collective-permute-start | bytes 6291464 | tf_op jit(solution)/shard_map/ppermute | solution.py:402
  182.4 86.0 %collective-permute-start.5 = (f32[128,32,128]{2,1,0:T(8,128)}, f32[128,32,128]{2,1,0:T(8,128)}, u32[]{:S(2)}, u32[]{:S(2)}) collective-permute-start(f32[128,32,128]{2,1,0:T(8,128)} %get-tuple-element.15.refs_6_), channel_id=1, source_target_pairs={{1,0},{2,3},{5,4},{6,7},{9,8},{10,11},{13,12},{14,15},{17,16},{18,... | collective-permute-start | bytes 6291464 | tf_op jit(solution)/shard_map/ppermute | solution.py:402
  217.0 69.8 %collective-permute-start.11 = (f32[128,32,128]{2,1,0:T(8,128)}, f32[128,32,128]{2,1,0:T(8,128)}, u32[]{:S(2)}, u32[]{:S(2)}) collective-permute-start(f32[128,32,128]{2,1,0:T(8,128)} %bitcast.16.refs_2_.refs_0_), channel_id=1, source_target_pairs={{1,2},{2,1},{5,6},{6,5},{9,10},{10,9},{13,14},{14,13},{17,18},{18,... | collective-permute-start | bytes 6291464 | tf_op jit(solution)/shard_map/ppermute | solution.py:402
  218.9 67.8 %collective-permute-start.12 = (f32[128,32,128]{2,1,0:T(8,128)}, f32[128,32,128]{2,1,0:T(8,128)}, u32[]{:S(2)}, u32[]{:S(2)}) collective-permute-start(f32[128,32,128]{2,1,0:T(8,128)} %collective-permute-done.7.refs_7_.refs_3_.refs_1_), channel_id=1, source_target_pairs={{1,2},{2,1},{5,6},{6,5},{9,10},{10,9},{13,14},{14,13},{17,18},{18,... | collective-permute-start | bytes 6291464 | tf_op jit(solution)/shard_map/ppermute | solution.py:402
  249.2 49.2 %collective-permute-start.10 = (f32[128,32,128]{2,1,0:T(8,128)}, f32[128,32,128]{2,1,0:T(8,128)}, u32[]{:S(2)}, u32[]{:S(2)}) collective-permute-start(f32[128,32,128]{2,1,0:T(8,128)} %get-tuple-element.17.refs_6_), channel_id=1, source_target_pairs={{1,0},{2,3},{5,4},{6,7},{9,8},{10,11},{13,12},{14,15},{17,16},{18,... | collective-permute-start | bytes 6291464 | tf_op jit(solution)/shard_map/ppermute | solution.py:402
  276.6 52.4 %collective-permute-start.17 = (f32[128,32,128]{2,1,0:T(8,128)}, f32[128,32,128]{2,1,0:T(8,128)}, u32[]{:S(2)}, u32[]{:S(2)}) collective-permute-start(f32[128,32,128]{2,1,0:T(8,128)} %bitcast.99), channel_id=1, source_target_pairs={{0,1},{3,2},{4,5},{7,6},{8,9},{11,10},{12,13},{15,14},{16,17},{19,... | collective-permute-start | bytes 6291464 | tf_op jit(solution)/shard_map/ppermute | solution.py:402
  284.1 89.8 %collective-permute-start.16 = (f32[128,32,128]{2,1,0:T(8,128)}, f32[128,32,128]{2,1,0:T(8,128)}, u32[]{:S(2)}, u32[]{:S(2)}) collective-permute-start(f32[128,32,128]{2,1,0:T(8,128)} %bitcast.96), channel_id=1, source_target_pairs={{0,1},{3,2},{4,5},{7,6},{8,9},{11,10},{12,13},{15,14},{16,17},{19,... | collective-permute-start | bytes 6291464 | tf_op jit(solution)/shard_map/ppermute | solution.py:402
  295.2 89.3 %collective-permute-start.13 = (f32[128,32,128]{2,1,0:T(8,128)}, f32[128,32,128]{2,1,0:T(8,128)}, u32[]{:S(2)}, u32[]{:S(2)}) collective-permute-start(f32[128,32,128]{2,1,0:T(8,128)} %get-tuple-element.19.refs_6_), channel_id=1, source_target_pairs={{1,0},{2,3},{5,4},{6,7},{9,8},{10,11},{13,12},{14,15},{17,16},{18,... | collective-permute-start | bytes 6291464 | tf_op jit(solution)/shard_map/ppermute | solution.py:402
  303.8 86.1 %all-to-all-start.3 = ((f32[8,2,8,32,128]{4,3,2,1,0:T(8,128)}), f32[8,2,8,32,128]{4,3,2,1,0:T(8,128)}, u32[]{:S(2)}, u32[]{:S(2)}) async-start(f32[8,2,8,32,128]{4,3,2,1,0:T(8,128)} %bitcast.83), calls=%async_computation.3 | async-start | bytes 4194304 | tf_op jit(solution)/shard_map/all_to_all | solution.py:405
  308.1 73.5 %collective-permute-start.14 = (f32[64,32,128]{2,1,0:T(8,128)}, f32[64,32,128]{2,1,0:T(8,128)S(1)}, u32[]{:S(2)}, u32[]{:S(2)}) collective-permute-start(f32[64,32,128]{2,1,0:T(8,128)} %bitcast.107), channel_id=1, source_target_pairs={{1,2},{2,1},{5,6},{6,5},{9,10},{10,9},{13,14},{14,13},{17,18},{18,... | collective-permute-start | bytes 3145736 | tf_op jit(solution)/shard_map/ppermute | solution.py:402
  309.0 72.6 %collective-permute-start.15 = (f32[64,32,128]{2,1,0:T(8,128)}, f32[64,32,128]{2,1,0:T(8,128)S(1)}, u32[]{:S(2)}, u32[]{:S(2)}) collective-permute-start(f32[64,32,128]{2,1,0:T(8,128)} %copy-done.23), channel_id=1, source_target_pairs={{1,2},{2,1},{5,6},{6,5},{9,10},{10,9},{13,14},{14,13},{17,18},{18,... | collective-permute-start | bytes 3145736 | tf_op jit(solution)/shard_map/ppermute | solution.py:402
  329.0 91.5 %collective-permute-start.21 = (f32[128,32,128]{2,1,0:T(8,128)}, f32[128,32,128]{2,1,0:T(8,128)}, u32[]{:S(2)}, u32[]{:S(2)}) collective-permute-start(f32[128,32,128]{2,1,0:T(8,128)} %bitcast.93), channel_id=1, source_target_pairs={{0,1},{3,2},{4,5},{7,6},{8,9},{11,10},{12,13},{15,14},{16,17},{19,... | collective-permute-start | bytes 6291464 | tf_op jit(solution)/shard_map/ppermute | solution.py:402
  389.9 49.5 %all-to-all-start.5 = ((f32[8,2,8,32,128]{4,3,2,1,0:T(8,128)}), f32[8,2,8,32,128]{4,3,2,1,0:T(8,128)}, u32[]{:S(2)}, u32[]{:S(2)}) async-start(f32[8,2,8,32,128]{4,3,2,1,0:T(8,128)} %bitcast.89), calls=%async_computation.5 | async-start | bytes 4194304 | tf_op jit(solution)/shard_map/all_to_all | solution.py:405
  397.0 75.4 %collective-permute-start.23 = (f32[64,32,128]{2,1,0:T(8,128)}, f32[64,32,128]{2,1,0:T(8,128)}, u32[]{:S(2)}, u32[]{:S(2)}) collective-permute-start(f32[64,32,128]{2,1,0:T(8,128)} %bitcast.19.refs_2_), channel_id=1, source_target_pairs={{0,1},{3,2},{4,5},{7,6},{8,9},{11,10},{12,13},{15,14},{16,17},{19,... | collective-permute-start | bytes 3145736 | tf_op jit(solution)/shard_map/ppermute | solution.py:402
  443.6 68.9 %collective-permute-start.24 = (f32[64,32,128]{2,1,0:T(8,128)}, f32[64,32,128]{2,1,0:T(8,128)}, u32[]{:S(2)}, u32[]{:S(2)}) collective-permute-start(f32[64,32,128]{2,1,0:T(8,128)} %bitcast.20.refs_3_.refs_2_), channel_id=1, source_target_pairs={{0,1},{3,2},{4,5},{7,6},{8,9},{11,10},{12,13},{15,14},{16,17},{19,... | collective-permute-start | bytes 3145736 | tf_op jit(solution)/shard_map/ppermute | solution.py:402
  (101 other events, 1201.6 us)

commit v3 on v2

--- a/solution.py
+++ b/solution.py
@@ -38,18 +38,7 @@
     return high, low
 
 
-def all_sum(value, axes):
-    for axis in axes:
-        extent = lax.axis_size(axis)
-        step = 1
-        while step < extent:
-            pairs = [(i, i ^ step) for i in range(extent)]
-            value = value + lax.ppermute(value, axis, pairs)
-            step *= 2
-    return value
-
-
-def run(body, grid, in_specs, out_specs, out_shape, args, done):
+def run(body, grid, in_specs, out_specs, out_shape, args, done, limit=VMEM_LIMIT):
     count, extra = len(args), len(done)
 
     def kernel(*refs):
@@ -61,7 +50,7 @@
         in_specs=list(in_specs) + [pl.BlockSpec(memory_space=pltpu.HBM)] * extra,
         out_specs=out_specs,
         out_shape=out_shape,
-        compiler_params=pltpu.CompilerParams(vmem_limit_bytes=VMEM_LIMIT),
+        compiler_params=pltpu.CompilerParams(vmem_limit_bytes=limit),
         cost_estimate=pl.CostEstimate(flops=0, bytes_accessed=0, transcendentals=0),
     )(*args, *done)
 
@@ -232,6 +221,7 @@
         ],
         (x, *adjoints,),
         done,
+        56 * 1024 * 1024,
     )
     zero = jnp.sum(zero, axis=0)
     columns, at = [], 0
@@ -264,11 +254,11 @@
             other_ref[n + k] = out[part:, k * width : (k + 1) * width]
 
 
-def pair_cross_body(x_ref, p_ref, q_ref, f_ref, own_ref, base_ref, terms_ref, c_ref):
+def pair_cross_body(x_ref, p_ref, q_ref, f_ref, b_ref, own_ref, base_ref, terms_ref, c_ref):
     total = None
     for n in range(0, x_ref.shape[0], 2):
         sides = [
-            jnp.concatenate([own_ref[k], base_ref[k] + terms_ref[k]], axis=0) for k in (n, n + 1)
+            jnp.concatenate([b_ref[k] + own_ref[k], base_ref[k] + terms_ref[k]], axis=0) for k in (n, n + 1)
         ]
         high, low = halves(jnp.concatenate(sides, axis=1))
         term = lax.dot_general(
@@ -304,12 +294,28 @@
     return run(
         pair_cross_body,
         (count // cells,),
-        [block] * 7,
+        [block] * 8,
         pl.BlockSpec((1,) + shape[1:], lambda i: (i, 0, 0)),
         jax.ShapeDtypeStruct(shape, f32),
         (*blocks,),
         done,
     )
+
+
+def last_body(scale_small, scale_large, a_ref, b_ref, small_ref, large_ref, s_ref, l_ref):
+    total = a_ref[...] + b_ref[...]
+
+    def gradient(cross, opened):
+        same = lax.broadcasted_iota(jnp.int32, cross.shape, 0) == lax.broadcasted_iota(jnp.int32, cross.shape, 1)
+        diagonal = jnp.sum(jnp.where(same, cross, 0.0), axis=1, keepdims=True)
+        return opened * (cross - diagonal)
+
+    small, large = s_ref.shape[1], l_ref.shape[1]
+    for k in (0, 1):
+        cross = total[:small, k * small : (k + 1) * small] / scale_small
+        s_ref[k] = gradient(cross, small_ref[k])
+        cross = total[small + k * large : small + (k + 1) * large] / scale_large
+        l_ref[k] = gradient(cross, large_ref[k])
 
 
 def copy_body(x_ref, o_ref):
@@ -437,7 +443,8 @@
         ones[k] = one_cross(wide_x, wide_a[k], PIECES[k][0], *done)
 
     def two_step(k, *done):
-        twos[k] = pair_cross((xs[k], ps[k], qs[k], fs[k], flat(adjoints[k]), others[k], other[k]), *done)
+        blocks = (xs[k], ps[k], qs[k], fs[k], bases[k], own[k], others[k], other[k])
+        twos[k] = pair_cross(blocks, *done)
 
     wide_x = exchange(xv)
     send_piece(0)
@@ -449,31 +456,31 @@
     one_second = one_terms(wide_x, mode_one, half, deep - half, one_first)
     back = [exchange(one_first), exchange(one_second)]
     terms_step(0, one_second)
-    base_step(0, own[0])
+    terms_step(1, own[0], ps[2], ps[3], ps[4])
+    base_step(0, own[1])
     base_step(1, bases[0])
-    terms_step(1, bases[1], ps[2], ps[3], ps[4])
-    base_step(2, own[1])
+    base_step(2, bases[1])
     base_step(3, bases[2])
     base_step(4, bases[3])
     finish(0, bases[4])
-    terms_step(2, adjoints[0])
-    finish(1, own[2])
-    two_step(0, adjoints[1])
-    two_step(1, twos[0])
+    two_step(0, adjoints[0])
+    terms_step(2, twos[0])
+    two_step(1, own[2])
     terms_step(3, twos[1])
-    finish(2, own[3])
-    one_step(0, adjoints[2])
-    one_step(1, ones[0])
-    two_step(2, ones[1])
-    terms_step(4, twos[2])
-    finish(3, own[4])
-    one_step(2, adjoints[3])
-    two_step(3, ones[2])
-    finish(4, twos[3])
+    finish(1, own[3])
+    one_step(0, adjoints[1])
+    two_step(2, ones[0])
+    terms_step(4, twos[2], far[3], others[3])
+    finish(2, own[4])
+    one_step(1, adjoints[2])
+    finish(3, ones[1])
+    two_step(3, adjoints[3])
+    one_step(2, twos[3])
+    finish(4, ones[2])
     cross_zero, cross_three = local_cross(xv, adjoints)
-    two_step(4, cross_three)
-    one_step(3, twos[4])
-    one_step(4, ones[3])
+    one_step(3, cross_three)
+    two_step(4, ones[3])
+    one_step(4, twos[4])
     cross_one = jnp.sum(jnp.concatenate(ones, axis=0), axis=0)
     found = jnp.where(inner, jnp.sum(jnp.concatenate(twos, axis=0), axis=0), 0.0)
     cross_two = jnp.einsum("xr,xy,yc->rc", spread, found, spread[: 2 * part], precision=highest)
@@ -481,13 +488,25 @@
     packed = jnp.concatenate(
         [jnp.concatenate([cross_zero, cross_one], axis=1), cross_two, cross_three], axis=0
     )
-    packed = all_sum(packed, ("wide", "narrow"))
-    small = jnp.stack([packed[:size_small, :size_small], packed[:size_small, size_small:]])
-    large = packed[size_small:].reshape(2, size_large, size_large)
-    small = small / math.sqrt(size_small * size_large * size_large)
-    large = large / math.sqrt(size_small * size_small * size_large)
-    grad_small = open_small * (small - jnp.diagonal(small, axis1=1, axis2=2)[:, :, None])
-    grad_large = open_large * (large - jnp.diagonal(large, axis1=1, axis2=2)[:, :, None])
+    def partner(value, axis, step):
+        return lax.ppermute(value, axis, [(i, i ^ step) for i in range(lax.axis_size(axis))])
+
+    for axis, step in (("narrow", 1), ("narrow", 2), ("wide", 1), ("wide", 2)):
+        packed = packed + partner(packed, axis, step)
+    arrays = (packed, partner(packed, "wide", 4), open_small, open_large)
+    grad_small, grad_large = run(
+        functools.partial(
+            last_body,
+            math.sqrt(size_small * size_large * size_large),
+            math.sqrt(size_small * size_small * size_large),
+        ),
+        (1,),
+        [whole(array) for array in arrays],
+        [whole(open_small), whole(open_large)],
+        [jax.ShapeDtypeStruct(open_small.shape, f32), jax.ShapeDtypeStruct(open_large.shape, f32)],
+        arrays,
+        (),
+    )
     return (grad_small, grad_large)
 
 

time: 565 us -> 569 us (level)
  waiting for transfers between devices: 148 us -> 167 us
  local copies, waits for them, and re-layouts: 54.6 us -> 42.4 us
    all_to_all x8, waiting for transfers between devices: 21.2 us -> 32.4 us  [exchange(): return lax.all_to_all(value, 'wide', 0, 0, tiled=True)]
    unnamed x174 -> x170, local copies, waits for them, and re-layouts: 44.1 us -> 40.2 us
    pallas_call x34 -> x35, Pallas kernels: 180 us -> 183 us  [run(): pl.pallas_call(kernel, grid=grid, in_specs=list(in_specs) + [pl.BlockSpec...]
  transfers between devices with their start and end apart: 38 -> 38, of which waited for: 13 -> 14; matrix products, arithmetic and copies ran while one was open for 3% -> 3% of each run, Pallas kernels for 30% -> 30%
where the time goes in v3:
time: 569 us; the launch traced here: 566 us
  Pallas kernels  183 us (32%)
  waiting for transfers between devices  167 us (29%)
  starting transfers between devices  153 us (27%)
  local copies, waits for them, and re-layouts  42.4 us (7%)
  other arithmetic  14 us (2%)
  between operations  5.82 us (1%)
    pallas_call x35, Pallas kernels, run(): pl.pallas_call(kernel, grid=grid, in_specs=list(in_specs) + [pl.BlockSpec...  183 us
    ppermute x25, starting transfers between devices, shift(): return lax.ppermute(value, 'narrow', pairs)  111 us
    ppermute x25, waiting for transfers between devices, shift(): return lax.ppermute(value, 'narrow', pairs)  110 us
    unnamed x170, local copies, waits for them, and re-layouts  40.2 us
    all_to_all x8, starting transfers between devices, exchange(): return lax.all_to_all(value, 'wide', 0, 0, tiled=True)  36.6 us
    all_to_all x8, waiting for transfers between devices, exchange(): return lax.all_to_all(value, 'wide', 0, 0, tiled=True)  32.4 us
    ppermute x5, waiting for transfers between devices, partner(): lax.ppermute(value, axis, [(i, i ^ step) for i in range(lax.axis_size(axi...  24.7 us
  transfers between devices with their start and end apart: 38, of which 14 were waited for; matrix products, arithmetic and copies ran while one was open for 3% of the time, Pallas kernels for 30%

profile of v3, /device:TPU:0, one launch (start us, length us, event | category | flops | bytes accessed | tf_op | source)
XLA Modules:
  0.0 565.7 jit_solution(2574754204837288674)
XLA Ops:
  38.2 21.2 %shard_map.116.refs_2_ = f32[64,8,32,128]{3,2,1,0:T(8,128)S(1)} custom-call(f32[64,8,32,128]{3,2,1,0:T(8,128)} %refs_0_.1, f32[64,8,32,128]{3,2,1,0:T(8,128)} %refs_1_.1, f32[64,64]{1,0:T(8,128)S(1)} %copy.23.refs_2_, f32[128,128]{1,0:T(8,128)S(1)} %fusion.refs_3_, f32[64,32,128]{2,1,0:T(8,128)S(1)} %bitcast.92), custom_call_target="tpu_custom_call" | custom-call | tf_op jit(solution)/shard_map/pallas_call | solution.py:47
  62.8 42.1 %collective-permute-done.refs_3_.refs_1_ = f32[128,32,128]{2,1,0:T(8,128)} collective-permute-done((f32[128,32,128]{2,1,0:T(8,128)}, f32[128,32,128]{2,1,0:T(8,128)}, u32[]{:S(2)}, u32[]{:S(2)}) %collective-permute-start) | collective-permute-done | bytes 2097184 | tf_op jit(solution)/shard_map/ppermute | solution.py:408
  104.8 6.7 %shard_map.117.refs_2_ = f32[8,4,8,32,128]{4,3,2,1,0:T(8,128)S(1)} custom-call(f32[8,8,8,32,128]{4,3,2,1,0:T(8,128)} %all-to-all-done.refs_0_, f32[8,64,64]{2,1,0:T(8,128)S(1)} %add_multiply_fusion.refs_1_, f32[64,8,32,128]{3,2,1,0:T(8,128)} %copy-done.2, f32[128,32,128]{2,1,0:T(8,128)} %collective-permute-done.refs_3_.refs_1_, ...), custom_call_target="tpu_custom_call" | custom-call | tf_op jit(solution)/shard_map/pallas_call | solution.py:47
  120.2 8.1 %collective-permute-start.9 = (f32[64,32,128]{2,1,0:T(8,128)S(1)}, f32[64,32,128]{2,1,0:T(8,128)}, u32[]{:S(2)}, u32[]{:S(2)}) collective-permute-start(f32[64,32,128]{2,1,0:T(8,128)S(1)} %bitcast.93), channel_id=1, source_target_pairs={{0,1},{3,2},{4,5},{7,6},{8,9},{11,10},{12,13},{15,14},{16,17},{19,... | collective-permute-start | bytes 3145736 | tf_op jit(solution)/shard_map/ppermute | solution.py:408
  145.3 6.8 %shard_map.118.refs_6_ = f32[8,4,8,32,128]{4,3,2,1,0:T(8,128)S(1)} custom-call(f32[8,8,8,32,128]{4,3,2,1,0:T(8,128)} %all-to-all-done.refs_0_, f32[8,64,64]{2,1,0:T(8,128)S(1)} %add_multiply_fusion.refs_1_, f32[8,4,8,32,128]{4,3,2,1,0:T(8,128)S(1)} %copy-done.4), custom_call_target="tpu_custom_call" | custom-call | tf_op jit(solution)/shard_map/pallas_call | solution.py:47
  154.2 13.1 %all-to-all-done.1.refs_1_ = f32[8,4,8,32,128]{4,3,2,1,0:T(8,128)} async-done(((f32[8,4,8,32,128]{4,3,2,1,0:T(8,128)}), f32[8,4,8,32,128]{4,3,2,1,0:T(8,128)}, u32[]{:S(2)}, u32[]{:S(2)}) %all-to-all-start.1) | async-done | bytes 4194336 | tf_op jit(solution)/shard_map/all_to_all | solution.py:411
  175.1 7.3 %shard_map.119 = (f32[128,32,128]{2,1,0:T(8,128)S(1)}, f32[128,32,128]{2,1,0:T(8,128)S(1)}) custom-call(f32[1,128]{1,0:T(1,128)S(1)} %convert_bitcast_fusion.refs_0_, f32[128,128]{1,0:T(8,128)S(1)} %fusion.2.refs_1_, f32[128,32,128]{2,1,0:T(8,128)} %bitcast.4.refs_2_.refs_0_, f32[128,32,128]{2,1,0:T(8,128)} %collective-permute-done.refs_3_.refs_1_, ...), custom_call_target="tpu_custom_call" | custom-call | tf_op jit(solution)/shard_map/pallas_call | solution.py:47
  187.1 8.9 %collective-permute-done.7.refs_7_.refs_3_.refs_1_ = f32[128,32,128]{2,1,0:T(8,128)} collective-permute-done((f32[128,32,128]{2,1,0:T(8,128)}, f32[128,32,128]{2,1,0:T(8,128)}, u32[]{:S(2)}, u32[]{:S(2)}) %collective-permute-start.7) | collective-permute-done | bytes 2097184 | tf_op jit(solution)/shard_map/ppermute | solution.py:408
  197.9 19.6 %collective-permute-done.8.refs_8_.refs_3_.refs_1_ = f32[64,32,128]{2,1,0:T(8,128)} collective-permute-done((f32[64,32,128]{2,1,0:T(8,128)}, f32[64,32,128]{2,1,0:T(8,128)}, u32[]{:S(2)}, u32[]{:S(2)}) %collective-permute-start.8) | collective-permute-done | bytes 1048608 | tf_op jit(solution)/shard_map/ppermute | solution.py:408
  217.6 8.0 %shard_map.122 = (f32[128,32,128]{2,1,0:T(8,128)S(1)}, f32[128,32,128]{2,1,0:T(8,128)}) custom-call(f32[1,128]{1,0:T(1,128)S(1)} %convert_bitcast_fusion.refs_0_, f32[128,128]{1,0:T(8,128)S(1)} %fusion.2.refs_1_, f32[128,32,128]{2,1,0:T(8,128)S(1)} %bitcast.70, f32[128,32,128]{2,1,0:T(8,128)} %collective-permute-done.3.refs_5_.refs_3_.refs_1_, ...), custom_call_target="tpu_custom_call" | custom-call | tf_op jit(solution)/shard_map/pallas_call | solution.py:47
  225.6 6.4 %shard_map.123 = f32[8,2,8,32,128]{4,3,2,1,0:T(8,128)} custom-call(f32[8,8,8,32,128]{4,3,2,1,0:T(8,128)} %bitcast.60, f32[8,4,8,32,128]{4,3,2,1,0:T(8,128)} %all-to-all-done.1.refs_1_, f32[128,32,128]{2,1,0:T(8,128)S(1)} %get-tuple-element.16.refs_2_.refs_5_.refs_0_), custom_call_target="tpu_custom_call" | custom-call | tf_op jit(solution)/shard_map/pallas_call | solution.py:47
  232.0 12.2 %collective-permute-start.16 = (f32[128,32,128]{2,1,0:T(8,128)}, f32[128,32,128]{2,1,0:T(8,128)}, u32[]{:S(2)}, u32[]{:S(2)}) collective-permute-start(f32[128,32,128]{2,1,0:T(8,128)} %bitcast.16.refs_2_.refs_4_), channel_id=1, source_target_pairs={{0,1},{3,2},{4,5},{7,6},{8,9},{11,10},{12,13},{15,14},{16,17},{19,... | collective-permute-start | bytes 6291464 | tf_op jit(solution)/shard_map/ppermute | solution.py:408
  278.2 7.2 %collective-permute-start.20 = (f32[128,32,128]{2,1,0:T(8,128)}, f32[128,32,128]{2,1,0:T(8,128)}, u32[]{:S(2)}, u32[]{:S(2)}) collective-permute-start(f32[128,32,128]{2,1,0:T(8,128)} %bitcast.73), channel_id=1, source_target_pairs={{0,1},{3,2},{4,5},{7,6},{8,9},{11,10},{12,13},{15,14},{16,17},{19,... | collective-permute-start | bytes 6291464 | tf_op jit(solution)/shard_map/ppermute | solution.py:408
  291.5 8.8 %shard_map.129.refs_6_ = f32[8,128,64]{2,1,0:T(8,128)S(1)} custom-call(f32[128,32,128]{2,1,0:T(8,128)} %bitcast.4.refs_2_.refs_0_, f32[128,32,128]{2,1,0:T(8,128)} %collective-permute-done.refs_3_.refs_1_, f32[128,32,128]{2,1,0:T(8,128)} %collective-permute-done.1.refs_4_.refs_2_, f32[128,32,128]{2,1,0:T(8,128)} %collective-permute-done.2.refs_5_.refs_3_, ...), custom_call_target="tpu_custom_call" | custom-call | tf_op jit(solution)/shard_map/pallas_call | solution.py:47
  300.3 8.7 %shard_map.130 = (f32[128,32,128]{2,1,0:T(8,128)S(1)}, f32[128,32,128]{2,1,0:T(8,128)}) custom-call(f32[1,128]{1,0:T(1,128)S(1)} %convert_bitcast_fusion.refs_0_, f32[128,128]{1,0:T(8,128)S(1)} %fusion.2.refs_1_, f32[128,32,128]{2,1,0:T(8,128)} %bitcast.14.refs_2_.refs_0_, f32[128,32,128]{2,1,0:T(8,128)} %collective-permute-done.7.refs_7_.refs_3_.refs_1_, ...), custom_call_target="tpu_custom_call" | custom-call | tf_op jit(solution)/shard_map/pallas_call | solution.py:47
  310.4 23.8 %collective-permute-done.13.refs_6_ = f32[128,32,128]{2,1,0:T(8,128)} collective-permute-done((f32[128,32,128]{2,1,0:T(8,128)}, f32[128,32,128]{2,1,0:T(8,128)}, u32[]{:S(2)}, u32[]{:S(2)}) %collective-permute-start.13) | collective-permute-done | bytes 2097184 | tf_op jit(solution)/shard_map/ppermute | solution.py:408
  335.6 8.4 %shard_map.131.refs_6_ = f32[8,128,64]{2,1,0:T(8,128)S(1)} custom-call(f32[128,32,128]{2,1,0:T(8,128)S(1)} %bitcast.71, f32[128,32,128]{2,1,0:T(8,128)} %collective-permute-done.3.refs_5_.refs_3_.refs_1_, f32[128,32,128]{2,1,0:T(8,128)} %collective-permute-done.4.refs_6_.refs_4_.refs_2_, f32[128,32,128]{2,1,0:T(8,128)} %collective-permute-done.6.refs_5_.refs_3_, ...), custom_call_target="tpu_custom_call" | custom-call | tf_op jit(solution)/shard_map/pallas_call | solution.py:47
  360.5 27.1 %collective-permute-start.22 = (f32[64,32,128]{2,1,0:T(8,128)}, f32[64,32,128]{2,1,0:T(8,128)S(1)}, u32[]{:S(2)}, u32[]{:S(2)}) collective-permute-start(f32[64,32,128]{2,1,0:T(8,128)} %bitcast.98), channel_id=1, source_target_pairs={{0,1},{3,2},{4,5},{7,6},{8,9},{11,10},{12,13},{15,14},{16,17},{19,... | collective-permute-start | bytes 3145736 | tf_op jit(solution)/shard_map/ppermute | solution.py:408
  393.7 8.5 %shard_map.135.refs_6_ = f32[8,128,64]{2,1,0:T(8,128)S(1)} custom-call(f32[128,32,128]{2,1,0:T(8,128)} %bitcast.14.refs_2_.refs_0_, f32[128,32,128]{2,1,0:T(8,128)} %collective-permute-done.7.refs_7_.refs_3_.refs_1_, f32[128,32,128]{2,1,0:T(8,128)} %collective-permute-done.14.refs_4_.refs_2_, f32[128,32,128]{2,1,0:T(8,128)} %collective-permute-done.15.refs_5_.refs_3_, ...), custom_call_target="tpu_custom_call" | custom-call | tf_op jit(solution)/shard_map/pallas_call | solution.py:47
  402.2 8.0 %collective-permute-done.22.refs_8_.refs_6_ = f32[64,32,128]{2,1,0:T(8,128)S(1)} collective-permute-done((f32[64,32,128]{2,1,0:T(8,128)}, f32[64,32,128]{2,1,0:T(8,128)S(1)}, u32[]{:S(2)}, u32[]{:S(2)}) %collective-permute-start.22) | collective-permute-done | bytes 1048608 | tf_op jit(solution)/shard_map/ppermute | solution.py:408
  435.2 19.2 %all-to-all-done.5.refs_1_ = f32[8,2,8,32,128]{4,3,2,1,0:T(8,128)} async-done(((f32[8,2,8,32,128]{4,3,2,1,0:T(8,128)}), f32[8,2,8,32,128]{4,3,2,1,0:T(8,128)}, u32[]{:S(2)}, u32[]{:S(2)}) %all-to-all-start.5) | async-done | bytes 2097184 | tf_op jit(solution)/shard_map/all_to_all | solution.py:411
  458.7 18.2 %collective-permute-start.24 = (f32[64,32,128]{2,1,0:T(8,128)S(1)}, f32[64,32,128]{2,1,0:T(8,128)}, u32[]{:S(2)}, u32[]{:S(2)}) collective-permute-start(f32[64,32,128]{2,1,0:T(8,128)S(1)} %bitcast.86), channel_id=1, source_target_pairs={{0,1},{3,2},{4,5},{7,6},{8,9},{11,10},{12,13},{15,14},{16,17},{19,... | collective-permute-start | bytes 3145736 | tf_op jit(solution)/shard_map/ppermute | solution.py:408
  506.3 14.9 %shard_map.143 = (f32[8,64,64]{2,1,0:T(8,128)}, f32[8,128,128]{2,1,0:T(8,128)}) custom-call(f32[8,8,8,32,128]{4,3,2,1,0:T(8,128)} %bitcast.54, f32[8,2,8,32,128]{4,3,2,1,0:T(8,128)} %bitcast.78, f32[8,2,8,32,128]{4,3,2,1,0:T(8,128)} %bitcast.80, f32[8,2,8,32,128]{4,3,2,1,0:T(8,128)} %bitcast.83, f32[8,1,8,32,128]{4,3,2,1,0:T(8,128)} %bitcast.90, ...), custom_call_target="tpu_custom_call" | custom-call | tf_op jit(solution)/shard_map/pallas_call | solution.py:47
  543.0 8.5 %collective-permute-done.26 = f32[320,128]{1,0:T(8,128)S(1)} collective-permute-done((f32[320,128]{1,0:T(8,128)S(1)}, f32[320,128]{1,0:T(8,128)S(1)}, u32[]{:S(2)}, u32[]{:S(2)}) %collective-permute-start.26) | collective-permute-done | bytes 163872 | tf_op jit(solution)/shard_map/ppermute | solution.py:492
  (321 shorter events, 238.2 us)
Async XLA Ops:
  0.6 104.2 %all-to-all-start = ((f32[8,8,8,32,128]{4,3,2,1,0:T(8,128)}), f32[8,8,8,32,128]{4,3,2,1,0:T(8,128)}, u32[]{:S(2)}, u32[]{:S(2)}) async-start(f32[8,8,8,32,128]{4,3,2,1,0:T(8,128)} %bitcast.53), calls=%async_computation | async-start | bytes 16777216 | tf_op jit(solution)/shard_map/all_to_all | solution.py:411
  9.5 53.2 %collective-permute-start.3 = (f32[128,32,128]{2,1,0:T(8,128)S(1)}, f32[128,32,128]{2,1,0:T(8,128)}, u32[]{:S(2)}, u32[]{:S(2)}) collective-permute-start(f32[128,32,128]{2,1,0:T(8,128)S(1)} %bitcast.65), channel_id=1, source_target_pairs={{0,1},{3,2},{4,5},{7,6},{8,9},{11,10},{12,13},{15,14},{16,17},{19,... | collective-permute-start | bytes 6291464 | tf_op jit(solution)/shard_map/ppermute | solution.py:408
  20.6 84.2 %collective-permute-start = (f32[128,32,128]{2,1,0:T(8,128)}, f32[128,32,128]{2,1,0:T(8,128)}, u32[]{:S(2)}, u32[]{:S(2)}) collective-permute-start(f32[128,32,128]{2,1,0:T(8,128)} %bitcast.4.refs_2_.refs_0_), channel_id=1, source_target_pairs={{0,1},{3,2},{4,5},{7,6},{8,9},{11,10},{12,13},{15,14},{16,17},{19,... | collective-permute-start | bytes 6291464 | tf_op jit(solution)/shard_map/ppermute | solution.py:408
  23.5 81.3 %collective-permute-start.1 = (f32[128,32,128]{2,1,0:T(8,128)}, f32[128,32,128]{2,1,0:T(8,128)}, u32[]{:S(2)}, u32[]{:S(2)}) collective-permute-start(f32[128,32,128]{2,1,0:T(8,128)} %bitcast.4.refs_2_.refs_0_), channel_id=1, source_target_pairs={{1,2},{2,1},{5,6},{6,5},{9,10},{10,9},{13,14},{14,13},{17,18},{18,... | collective-permute-start | bytes 6291464 | tf_op jit(solution)/shard_map/ppermute | solution.py:408
  113.6 53.7 %all-to-all-start.1 = ((f32[8,4,8,32,128]{4,3,2,1,0:T(8,128)}), f32[8,4,8,32,128]{4,3,2,1,0:T(8,128)}, u32[]{:S(2)}, u32[]{:S(2)}) async-start(f32[8,4,8,32,128]{4,3,2,1,0:T(8,128)} %copy-done.3), calls=%async_computation.1 | async-start | bytes 8388608 | tf_op jit(solution)/shard_map/all_to_all | solution.py:411
  118.2 56.9 %collective-permute-start.2 = (f32[128,32,128]{2,1,0:T(8,128)}, f32[128,32,128]{2,1,0:T(8,128)}, u32[]{:S(2)}, u32[]{:S(2)}) collective-permute-start(f32[128,32,128]{2,1,0:T(8,128)} %collective-permute-done.refs_3_.refs_1_), channel_id=1, source_target_pairs={{1,2},{2,1},{5,6},{6,5},{9,10},{10,9},{13,14},{14,13},{17,18},{18,... | collective-permute-start | bytes 6291464 | tf_op jit(solution)/shard_map/ppermute | solution.py:408
  120.2 64.8 %collective-permute-start.9 = (f32[64,32,128]{2,1,0:T(8,128)S(1)}, f32[64,32,128]{2,1,0:T(8,128)}, u32[]{:S(2)}, u32[]{:S(2)}) collective-permute-start(f32[64,32,128]{2,1,0:T(8,128)S(1)} %bitcast.93), channel_id=1, source_target_pairs={{0,1},{3,2},{4,5},{7,6},{8,9},{11,10},{12,13},{15,14},{16,17},{19,... | collective-permute-start | bytes 3145736 | tf_op jit(solution)/shard_map/ppermute | solution.py:408
  134.8 61.2 %collective-permute-start.7 = (f32[128,32,128]{2,1,0:T(8,128)}, f32[128,32,128]{2,1,0:T(8,128)}, u32[]{:S(2)}, u32[]{:S(2)}) collective-permute-start(f32[128,32,128]{2,1,0:T(8,128)} %bitcast.14.refs_2_.refs_0_), channel_id=1, source_target_pairs={{0,1},{3,2},{4,5},{7,6},{8,9},{11,10},{12,13},{15,14},{16,17},{19,... | collective-permute-start | bytes 6291464 | tf_op jit(solution)/shard_map/ppermute | solution.py:408
  140.1 77.4 %collective-permute-start.8 = (f32[64,32,128]{2,1,0:T(8,128)}, f32[64,32,128]{2,1,0:T(8,128)}, u32[]{:S(2)}, u32[]{:S(2)}) collective-permute-start(f32[64,32,128]{2,1,0:T(8,128)} %bitcast.15.refs_2_.refs_0_), channel_id=1, source_target_pairs={{0,1},{3,2},{4,5},{7,6},{8,9},{11,10},{12,13},{15,14},{16,17},{19,... | collective-permute-start | bytes 3145736 | tf_op jit(solution)/shard_map/ppermute | solution.py:408
  167.3 88.1 %all-to-all-start.2 = ((f32[8,4,8,32,128]{4,3,2,1,0:T(8,128)}), f32[8,4,8,32,128]{4,3,2,1,0:T(8,128)}, u32[]{:S(2)}, u32[]{:S(2)}) async-start(f32[8,4,8,32,128]{4,3,2,1,0:T(8,128)} %copy-done.5), calls=%async_computation.2 | async-start | bytes 8388608 | tf_op jit(solution)/shard_map/all_to_all | solution.py:411
  183.8 69.1 %collective-permute-start.5 = (f32[128,32,128]{2,1,0:T(8,128)S(1)}, f32[128,32,128]{2,1,0:T(8,128)S(1)}, u32[]{:S(2)}, u32[]{:S(2)}) collective-permute-start(f32[128,32,128]{2,1,0:T(8,128)S(1)} %get-tuple-element.15.refs_7_), channel_id=1, source_target_pairs={{1,0},{2,3},{5,4},{6,7},{9,8},{10,11},{13,12},{14,15},{17,16},{18,... | collective-permute-start | bytes 6291464 | tf_op jit(solution)/shard_map/ppermute | solution.py:408
  185.1 93.1 %collective-permute-start.14 = (f32[128,32,128]{2,1,0:T(8,128)}, f32[128,32,128]{2,1,0:T(8,128)}, u32[]{:S(2)}, u32[]{:S(2)}) collective-permute-start(f32[128,32,128]{2,1,0:T(8,128)} %bitcast.14.refs_2_.refs_0_), channel_id=1, source_target_pairs={{1,2},{2,1},{5,6},{6,5},{9,10},{10,9},{13,14},{14,13},{17,18},{18,... | collective-permute-start | bytes 6291464 | tf_op jit(solution)/shard_map/ppermute | solution.py:408
  196.0 89.4 %collective-permute-start.15 = (f32[128,32,128]{2,1,0:T(8,128)}, f32[128,32,128]{2,1,0:T(8,128)}, u32[]{:S(2)}, u32[]{:S(2)}) collective-permute-start(f32[128,32,128]{2,1,0:T(8,128)} %collective-permute-done.7.refs_7_.refs_3_.refs_1_), channel_id=1, source_target_pairs={{1,2},{2,1},{5,6},{6,5},{9,10},{10,9},{13,14},{14,13},{17,18},{18,... | collective-permute-start | bytes 6291464 | tf_op jit(solution)/shard_map/ppermute | solution.py:408
  232.0 57.2 %collective-permute-start.16 = (f32[128,32,128]{2,1,0:T(8,128)}, f32[128,32,128]{2,1,0:T(8,128)}, u32[]{:S(2)}, u32[]{:S(2)}) collective-permute-start(f32[128,32,128]{2,1,0:T(8,128)} %bitcast.16.refs_2_.refs_4_), channel_id=1, source_target_pairs={{0,1},{3,2},{4,5},{7,6},{8,9},{11,10},{12,13},{15,14},{16,17},{19,... | collective-permute-start | bytes 6291464 | tf_op jit(solution)/shard_map/ppermute | solution.py:408
  250.2 83.9 %collective-permute-start.13 = (f32[128,32,128]{2,1,0:T(8,128)}, f32[128,32,128]{2,1,0:T(8,128)}, u32[]{:S(2)}, u32[]{:S(2)}) collective-permute-start(f32[128,32,128]{2,1,0:T(8,128)} %bitcast.17.refs_2_.refs_4_), channel_id=1, source_target_pairs={{0,1},{3,2},{4,5},{7,6},{8,9},{11,10},{12,13},{15,14},{16,17},{19,... | collective-permute-start | bytes 6291464 | tf_op jit(solution)/shard_map/ppermute | solution.py:408
  254.2 94.9 %collective-permute-start.10 = (f32[128,32,128]{2,1,0:T(8,128)}, f32[128,32,128]{2,1,0:T(8,128)}, u32[]{:S(2)}, u32[]{:S(2)}) collective-permute-start(f32[128,32,128]{2,1,0:T(8,128)} %get-tuple-element.17.refs_7_), channel_id=1, source_target_pairs={{1,0},{2,3},{5,4},{6,7},{9,8},{10,11},{13,12},{14,15},{17,16},{18,... | collective-permute-start | bytes 6291464 | tf_op jit(solution)/shard_map/ppermute | solution.py:408
  273.8 80.7 %all-to-all-start.3 = ((f32[8,2,8,32,128]{4,3,2,1,0:T(8,128)}), f32[8,2,8,32,128]{4,3,2,1,0:T(8,128)}, u32[]{:S(2)}, u32[]{:S(2)}) async-start(f32[8,2,8,32,128]{4,3,2,1,0:T(8,128)} %bitcast.76), calls=%async_computation.3 | async-start | bytes 4194304 | tf_op jit(solution)/shard_map/all_to_all | solution.py:411
  278.2 109.4 %collective-permute-start.20 = (f32[128,32,128]{2,1,0:T(8,128)}, f32[128,32,128]{2,1,0:T(8,128)}, u32[]{:S(2)}, u32[]{:S(2)}) collective-permute-start(f32[128,32,128]{2,1,0:T(8,128)} %bitcast.73), channel_id=1, source_target_pairs={{0,1},{3,2},{4,5},{7,6},{8,9},{11,10},{12,13},{15,14},{16,17},{19,... | collective-permute-start | bytes 6291464 | tf_op jit(solution)/shard_map/ppermute | solution.py:408
  285.4 58.7 %collective-permute-start.11 = (f32[64,32,128]{2,1,0:T(8,128)}, f32[64,32,128]{2,1,0:T(8,128)S(1)}, u32[]{:S(2)}, u32[]{:S(2)}) collective-permute-start(f32[64,32,128]{2,1,0:T(8,128)} %bitcast.15.refs_2_.refs_0_), channel_id=1, source_target_pairs={{1,2},{2,1},{5,6},{6,5},{9,10},{10,9},{13,14},{14,13},{17,18},{18,... | collective-permute-start | bytes 3145736 | tf_op jit(solution)/shard_map/ppermute | solution.py:408
  289.2 54.9 %collective-permute-start.12 = (f32[64,32,128]{2,1,0:T(8,128)}, f32[64,32,128]{2,1,0:T(8,128)S(1)}, u32[]{:S(2)}, u32[]{:S(2)}) collective-permute-start(f32[64,32,128]{2,1,0:T(8,128)} %collective-permute-done.8.refs_8_.refs_3_.refs_1_), channel_id=1, source_target_pairs={{1,2},{2,1},{5,6},{6,5},{9,10},{10,9},{13,14},{14,13},{17,18},{18,... | collective-permute-start | bytes 3145736 | tf_op jit(solution)/shard_map/ppermute | solution.py:408
  334.1 85.0 %collective-permute-start.17 = (f32[128,32,128]{2,1,0:T(8,128)}, f32[128,32,128]{2,1,0:T(8,128)}, u32[]{:S(2)}, u32[]{:S(2)}) collective-permute-start(f32[128,32,128]{2,1,0:T(8,128)} %get-tuple-element.20.refs_7_), channel_id=1, source_target_pairs={{1,0},{2,3},{5,4},{6,7},{9,8},{10,11},{13,12},{14,15},{17,16},{18,... | collective-permute-start | bytes 6291464 | tf_op jit(solution)/shard_map/ppermute | solution.py:408
  354.5 68.7 %all-to-all-start.4 = ((f32[8,2,8,32,128]{4,3,2,1,0:T(8,128)}), f32[8,2,8,32,128]{4,3,2,1,0:T(8,128)}, u32[]{:S(2)}, u32[]{:S(2)}) async-start(f32[8,2,8,32,128]{4,3,2,1,0:T(8,128)} %bitcast.79), calls=%async_computation.4 | async-start | bytes 4194304 | tf_op jit(solution)/shard_map/all_to_all | solution.py:411
  427.8 65.9 %collective-permute-start.23 = (f32[64,32,128]{2,1,0:T(8,128)}, f32[64,32,128]{2,1,0:T(8,128)}, u32[]{:S(2)}, u32[]{:S(2)}) collective-permute-start(f32[64,32,128]{2,1,0:T(8,128)} %copy-done.55), channel_id=1, source_target_pairs={{1,0},{2,3},{5,4},{6,7},{9,8},{10,11},{13,12},{14,15},{17,16},{18,... | collective-permute-start | bytes 3145736 | tf_op jit(solution)/shard_map/ppermute | solution.py:408
  458.7 69.1 %collective-permute-start.24 = (f32[64,32,128]{2,1,0:T(8,128)S(1)}, f32[64,32,128]{2,1,0:T(8,128)}, u32[]{:S(2)}, u32[]{:S(2)}) collective-permute-start(f32[64,32,128]{2,1,0:T(8,128)S(1)} %bitcast.86), channel_id=1, source_target_pairs={{0,1},{3,2},{4,5},{7,6},{8,9},{11,10},{12,13},{15,14},{16,17},{19,... | collective-permute-start | bytes 3145736 | tf_op jit(solution)/shard_map/ppermute | solution.py:408
  (99 other events, 1149.6 us)

commit v4 on v2

--- a/solution.py
+++ b/solution.py
@@ -36,17 +36,6 @@
     high = value.astype(bf16)
     low = (value - high.astype(f32)).astype(bf16)
     return high, low
-
-
-def all_sum(value, axes):
-    for axis in axes:
-        extent = lax.axis_size(axis)
-        step = 1
-        while step < extent:
-            pairs = [(i, i ^ step) for i in range(extent)]
-            value = value + lax.ppermute(value, axis, pairs)
-            step *= 2
-    return value
 
 
 def run(body, grid, in_specs, out_specs, out_shape, args, done):
@@ -310,6 +299,22 @@
         (*blocks,),
         done,
     )
+
+
+def last_body(scale_small, scale_large, a_ref, b_ref, small_ref, large_ref, s_ref, l_ref):
+    total = a_ref[...] + b_ref[...]
+
+    def gradient(cross, opened):
+        same = lax.broadcasted_iota(jnp.int32, cross.shape, 0) == lax.broadcasted_iota(jnp.int32, cross.shape, 1)
+        diagonal = jnp.sum(jnp.where(same, cross, 0.0), axis=1, keepdims=True)
+        return opened * (cross - diagonal)
+
+    small, large = s_ref.shape[1], l_ref.shape[1]
+    for k in (0, 1):
+        cross = total[:small, k * small : (k + 1) * small] / scale_small
+        s_ref[k] = gradient(cross, small_ref[k])
+        cross = total[small + k * large : small + (k + 1) * large] / scale_large
+        l_ref[k] = gradient(cross, large_ref[k])
 
 
 def copy_body(x_ref, o_ref):
@@ -481,13 +486,25 @@
     packed = jnp.concatenate(
         [jnp.concatenate([cross_zero, cross_one], axis=1), cross_two, cross_three], axis=0
     )
-    packed = all_sum(packed, ("wide", "narrow"))
-    small = jnp.stack([packed[:size_small, :size_small], packed[:size_small, size_small:]])
-    large = packed[size_small:].reshape(2, size_large, size_large)
-    small = small / math.sqrt(size_small * size_large * size_large)
-    large = large / math.sqrt(size_small * size_small * size_large)
-    grad_small = open_small * (small - jnp.diagonal(small, axis1=1, axis2=2)[:, :, None])
-    grad_large = open_large * (large - jnp.diagonal(large, axis1=1, axis2=2)[:, :, None])
+    def partner(value, axis, step):
+        return lax.ppermute(value, axis, [(i, i ^ step) for i in range(lax.axis_size(axis))])
+
+    for axis, step in (("wide", 1), ("wide", 2), ("wide", 4), ("narrow", 1)):
+        packed = packed + partner(packed, axis, step)
+    arrays = (packed, partner(packed, "narrow", 2), open_small, open_large)
+    grad_small, grad_large = run(
+        functools.partial(
+            last_body,
+            math.sqrt(size_small * size_large * size_large),
+            math.sqrt(size_small * size_small * size_large),
+        ),
+        (1,),
+        [whole(array) for array in arrays],
+        [whole(open_small), whole(open_large)],
+        [jax.ShapeDtypeStruct(open_small.shape, f32), jax.ShapeDtypeStruct(open_large.shape, f32)],
+        arrays,
+        (),
+    )
     return (grad_small, grad_large)
 
 

time: 565 us -> 557 us (0.986)
  local copies, waits for them, and re-layouts: 54.6 us -> 43.4 us
    pallas_call x34 -> x35, Pallas kernels: 180 us -> 177 us  [run(): pl.pallas_call(kernel, grid=grid, in_specs=list(in_specs) + [pl.BlockSpec...]
    unnamed x174 -> x168, local copies, waits for them, and re-layouts: 44.1 us -> 41.3 us
  transfers between devices with their start and end apart: 38 -> 38, of which waited for: 13 -> 13; matrix products, arithmetic and copies ran while one was open for 3% -> 4% of each run, Pallas kernels for 30% -> 30%
where the time goes in v4:
time: 557 us; the launch traced here: 553 us
  Pallas kernels  177 us (32%)
  starting transfers between devices  158 us (28%)
  waiting for transfers between devices  152 us (27%)
  local copies, waits for them, and re-layouts  43.4 us (8%)
  other arithmetic  16.5 us (3%)
  between operations  5.72 us (1%)
    pallas_call x35, Pallas kernels, run(): pl.pallas_call(kernel, grid=grid, in_specs=list(in_specs) + [pl.BlockSpec...  177 us
    ppermute x25, starting transfers between devices, shift(): return lax.ppermute(value, 'narrow', pairs)  117 us
    ppermute x25, waiting for transfers between devices, shift(): return lax.ppermute(value, 'narrow', pairs)  109 us
    unnamed x168, local copies, waits for them, and re-layouts  41.3 us
    all_to_all x8, starting transfers between devices, exchange(): return lax.all_to_all(value, 'wide', 0, 0, tiled=True)  36.2 us
    ppermute x5, waiting for transfers between devices, partner(): lax.ppermute(value, axis, [(i, i ^ step) for i in range(lax.axis_size(axi...  21.5 us
    all_to_all x8, waiting for transfers between devices, exchange(): return lax.all_to_all(value, 'wide', 0, 0, tiled=True)  21.1 us
  transfers between devices with their start and end apart: 38, of which 13 were waited for; matrix products, arithmetic and copies ran while one was open for 4% of the time, Pallas kernels for 30%

profile of v4, /device:TPU:0, one launch (start us, length us, event | category | flops | bytes accessed | tf_op | source)
XLA Modules:
  0.0 553.3 jit_solution(11384422283672650355)
XLA Ops:
  38.1 21.2 %shard_map.116.refs_2_ = f32[64,8,32,128]{3,2,1,0:T(8,128)S(1)} custom-call(f32[64,8,32,128]{3,2,1,0:T(8,128)} %refs_0_.1, f32[64,8,32,128]{3,2,1,0:T(8,128)} %refs_1_.1, f32[64,64]{1,0:T(8,128)S(1)} %copy.23.refs_2_, f32[128,128]{1,0:T(8,128)S(1)} %fusion.refs_3_, f32[64,32,128]{2,1,0:T(8,128)S(1)} %bitcast.87), custom_call_target="tpu_custom_call" | custom-call | tf_op jit(solution)/shard_map/pallas_call | solution.py:47
  62.7 42.1 %collective-permute-done.refs_3_.refs_1_ = f32[128,32,128]{2,1,0:T(8,128)} collective-permute-done((f32[128,32,128]{2,1,0:T(8,128)}, f32[128,32,128]{2,1,0:T(8,128)}, u32[]{:S(2)}, u32[]{:S(2)}) %collective-permute-start) | collective-permute-done | bytes 2097184 | tf_op jit(solution)/shard_map/ppermute | solution.py:407
  104.8 6.8 %shard_map.117.refs_2_ = f32[8,4,8,32,128]{4,3,2,1,0:T(8,128)S(1)} custom-call(f32[8,8,8,32,128]{4,3,2,1,0:T(8,128)} %all-to-all-done.refs_0_, f32[8,64,64]{2,1,0:T(8,128)S(1)} %add_multiply_fusion.refs_1_, f32[64,8,32,128]{3,2,1,0:T(8,128)} %copy-done.3, f32[128,32,128]{2,1,0:T(8,128)} %collective-permute-done.refs_3_.refs_1_, ...), custom_call_target="tpu_custom_call" | custom-call | tf_op jit(solution)/shard_map/pallas_call | solution.py:47
  126.5 8.6 %collective-permute-start.7 = (f32[128,32,128]{2,1,0:T(8,128)}, f32[128,32,128]{2,1,0:T(8,128)}, u32[]{:S(2)}, u32[]{:S(2)}) collective-permute-start(f32[128,32,128]{2,1,0:T(8,128)} %bitcast.16.refs_2_.refs_0_), channel_id=1, source_target_pairs={{0,1},{3,2},{4,5},{7,6},{8,9},{11,10},{12,13},{15,14},{16,17},{19,... | collective-permute-start | bytes 6291464 | tf_op jit(solution)/shard_map/ppermute | solution.py:407
  137.3 6.8 %shard_map.118.refs_6_ = f32[8,4,8,32,128]{4,3,2,1,0:T(8,128)S(1)} custom-call(f32[8,8,8,32,128]{4,3,2,1,0:T(8,128)} %all-to-all-done.refs_0_, f32[8,64,64]{2,1,0:T(8,128)S(1)} %add_multiply_fusion.refs_1_, f32[8,4,8,32,128]{4,3,2,1,0:T(8,128)S(1)} %copy-done.11), custom_call_target="tpu_custom_call" | custom-call | tf_op jit(solution)/shard_map/pallas_call | solution.py:47
  146.1 21.1 %all-to-all-done.1.refs_1_ = f32[8,4,8,32,128]{4,3,2,1,0:T(8,128)} async-done(((f32[8,4,8,32,128]{4,3,2,1,0:T(8,128)}), f32[8,4,8,32,128]{4,3,2,1,0:T(8,128)}, u32[]{:S(2)}, u32[]{:S(2)}) %all-to-all-start.1) | async-done | bytes 4194336 | tf_op jit(solution)/shard_map/all_to_all | solution.py:410
  173.9 8.4 %shard_map.119 = (f32[128,32,128]{2,1,0:T(8,128)S(1)}, f32[128,32,128]{2,1,0:T(8,128)}) custom-call(f32[1,128]{1,0:T(1,128)S(1)} %convert_bitcast_fusion.refs_0_, f32[128,128]{1,0:T(8,128)S(1)} %fusion.2.refs_1_, f32[128,32,128]{2,1,0:T(8,128)} %bitcast.4.refs_2_.refs_0_, f32[128,32,128]{2,1,0:T(8,128)} %collective-permute-done.refs_3_.refs_1_, ...), custom_call_target="tpu_custom_call" | custom-call | tf_op jit(solution)/shard_map/pallas_call | solution.py:47
  183.7 9.8 %collective-permute-start.9 = (f32[64,32,128]{2,1,0:T(8,128)S(1)}, f32[64,32,128]{2,1,0:T(8,128)S(1)}, u32[]{:S(2)}, u32[]{:S(2)}) collective-permute-start(f32[64,32,128]{2,1,0:T(8,128)S(1)} %bitcast.88), channel_id=1, source_target_pairs={{0,1},{3,2},{4,5},{7,6},{8,9},{11,10},{12,13},{15,14},{16,17},{19,... | collective-permute-start | bytes 3145736 | tf_op jit(solution)/shard_map/ppermute | solution.py:407
  198.4 18.5 %collective-permute-done.9.refs_9_.refs_3_.refs_1_ = f32[64,32,128]{2,1,0:T(8,128)S(1)} collective-permute-done((f32[64,32,128]{2,1,0:T(8,128)S(1)}, f32[64,32,128]{2,1,0:T(8,128)S(1)}, u32[]{:S(2)}, u32[]{:S(2)}) %collective-permute-start.9) | collective-permute-done | bytes 1048608 | tf_op jit(solution)/shard_map/ppermute | solution.py:407
  232.2 6.4 %collective-permute-done.8.refs_8_.refs_3_.refs_1_ = f32[64,32,128]{2,1,0:T(8,128)S(1)} collective-permute-done((f32[64,32,128]{2,1,0:T(8,128)S(1)}, f32[64,32,128]{2,1,0:T(8,128)S(1)}, u32[]{:S(2)}, u32[]{:S(2)}) %collective-permute-start.8) | collective-permute-done | bytes 1048608 | tf_op jit(solution)/shard_map/ppermute | solution.py:407
  239.9 8.0 %shard_map.124 = (f32[128,32,128]{2,1,0:T(8,128)S(1)}, f32[128,32,128]{2,1,0:T(8,128)}) custom-call(f32[1,128]{1,0:T(1,128)S(1)} %convert_bitcast_fusion.refs_0_, f32[128,128]{1,0:T(8,128)S(1)} %fusion.2.refs_1_, f32[128,32,128]{2,1,0:T(8,128)S(1)} %bitcast.70, f32[128,32,128]{2,1,0:T(8,128)} %collective-permute-done.3.refs_5_.refs_3_.refs_1_, ...), custom_call_target="tpu_custom_call" | custom-call | tf_op jit(solution)/shard_map/pallas_call | solution.py:47
  261.5 6.4 %shard_map.127 = f32[8,1,8,32,128]{4,3,2,1,0:T(8,128)} custom-call(f32[8,8,8,32,128]{4,3,2,1,0:T(8,128)} %bitcast.64, f32[8,4,8,32,128]{4,3,2,1,0:T(8,128)} %all-to-all-done.2.refs_1_, f32[64,32,128]{2,1,0:T(8,128)S(1)} %bitcast.92), custom_call_target="tpu_custom_call" | custom-call | tf_op jit(solution)/shard_map/pallas_call | solution.py:47
  276.1 7.5 %collective-permute-start.17 = (f32[128,32,128]{2,1,0:T(8,128)}, f32[128,32,128]{2,1,0:T(8,128)}, u32[]{:S(2)}, u32[]{:S(2)}) collective-permute-start(f32[128,32,128]{2,1,0:T(8,128)} %bitcast.85), channel_id=1, source_target_pairs={{0,1},{3,2},{4,5},{7,6},{8,9},{11,10},{12,13},{15,14},{16,17},{19,... | collective-permute-start | bytes 6291464 | tf_op jit(solution)/shard_map/ppermute | solution.py:407
  286.2 8.4 %shard_map.129 = (f32[128,32,128]{2,1,0:T(8,128)S(1)}, f32[128,32,128]{2,1,0:T(8,128)}) custom-call(f32[1,128]{1,0:T(1,128)S(1)} %convert_bitcast_fusion.refs_0_, f32[128,128]{1,0:T(8,128)S(1)} %fusion.2.refs_1_, f32[128,32,128]{2,1,0:T(8,128)} %bitcast.16.refs_2_.refs_0_, f32[128,32,128]{2,1,0:T(8,128)} %collective-permute-done.7.refs_7_.refs_3_.refs_1_, ...), custom_call_target="tpu_custom_call" | custom-call | tf_op jit(solution)/shard_map/pallas_call | solution.py:47
  309.7 18.7 %collective-permute-done.17.refs_5_ = f32[128,32,128]{2,1,0:T(8,128)} collective-permute-done((f32[128,32,128]{2,1,0:T(8,128)}, f32[128,32,128]{2,1,0:T(8,128)}, u32[]{:S(2)}, u32[]{:S(2)}) %collective-permute-start.17) | collective-permute-done | bytes 2097184 | tf_op jit(solution)/shard_map/ppermute | solution.py:407
  328.4 18.4 %collective-permute-start.21 = (f32[128,32,128]{2,1,0:T(8,128)}, f32[128,32,128]{2,1,0:T(8,128)}, u32[]{:S(2)}, u32[]{:S(2)}) collective-permute-start(f32[128,32,128]{2,1,0:T(8,128)} %bitcast.79), channel_id=1, source_target_pairs={{0,1},{3,2},{4,5},{7,6},{8,9},{11,10},{12,13},{15,14},{16,17},{19,... | collective-permute-start | bytes 6291464 | tf_op jit(solution)/shard_map/ppermute | solution.py:407
  348.4 8.5 %shard_map.131.refs_7_ = f32[8,128,64]{2,1,0:T(8,128)S(1)} custom-call(f32[128,32,128]{2,1,0:T(8,128)} %bitcast.4.refs_2_.refs_0_, f32[128,32,128]{2,1,0:T(8,128)} %collective-permute-done.refs_3_.refs_1_, f32[128,32,128]{2,1,0:T(8,128)} %collective-permute-done.1.refs_4_.refs_2_, f32[128,32,128]{2,1,0:T(8,128)} %collective-permute-done.2.refs_5_.refs_3_, ...), custom_call_target="tpu_custom_call" | custom-call | tf_op jit(solution)/shard_map/pallas_call | solution.py:47
  356.9 16.5 %collective-permute-done.16.refs_5_ = f32[128,32,128]{2,1,0:T(8,128)} collective-permute-done((f32[128,32,128]{2,1,0:T(8,128)}, f32[128,32,128]{2,1,0:T(8,128)}, u32[]{:S(2)}, u32[]{:S(2)}) %collective-permute-start.16) | collective-permute-done | bytes 2097184 | tf_op jit(solution)/shard_map/ppermute | solution.py:407
  373.4 7.6 %shard_map.132.refs_6_ = f32[8,128,64]{2,1,0:T(8,128)S(1)} custom-call(f32[128,32,128]{2,1,0:T(8,128)S(1)} %bitcast.71, f32[128,32,128]{2,1,0:T(8,128)} %collective-permute-done.3.refs_5_.refs_3_.refs_1_, f32[128,32,128]{2,1,0:T(8,128)} %collective-permute-done.4.refs_6_.refs_4_.refs_2_, f32[128,32,128]{2,1,0:T(8,128)S(1)} %copy-done.31, ...), custom_call_target="tpu_custom_call" | custom-call | tf_op jit(solution)/shard_map/pallas_call | solution.py:47
  396.8 13.4 %collective-permute-start.23 = (f32[64,32,128]{2,1,0:T(8,128)S(1)}, f32[64,32,128]{2,1,0:T(8,128)}, u32[]{:S(2)}, u32[]{:S(2)}) collective-permute-start(f32[64,32,128]{2,1,0:T(8,128)S(1)} %bitcast.93), channel_id=1, source_target_pairs={{0,1},{3,2},{4,5},{7,6},{8,9},{11,10},{12,13},{15,14},{16,17},{19,... | collective-permute-start | bytes 3145736 | tf_op jit(solution)/shard_map/ppermute | solution.py:407
  419.1 8.7 %shard_map.137.refs_6_ = f32[8,128,64]{2,1,0:T(8,128)S(1)} custom-call(f32[128,32,128]{2,1,0:T(8,128)} %bitcast.16.refs_2_.refs_0_, f32[128,32,128]{2,1,0:T(8,128)} %collective-permute-done.7.refs_7_.refs_3_.refs_1_, f32[128,32,128]{2,1,0:T(8,128)} %collective-permute-done.11.refs_4_.refs_2_, f32[128,32,128]{2,1,0:T(8,128)} %collective-permute-done.12.refs_5_.refs_3_, ...), custom_call_target="tpu_custom_call" | custom-call | tf_op jit(solution)/shard_map/pallas_call | solution.py:47
  438.9 25.7 %collective-permute-start.24 = (f32[64,32,128]{2,1,0:T(8,128)}, f32[64,32,128]{2,1,0:T(8,128)}, u32[]{:S(2)}, u32[]{:S(2)}) collective-permute-start(f32[64,32,128]{2,1,0:T(8,128)} %bitcast.20.refs_3_.refs_2_), channel_id=1, source_target_pairs={{0,1},{3,2},{4,5},{7,6},{8,9},{11,10},{12,13},{15,14},{16,17},{19,... | collective-permute-start | bytes 3145736 | tf_op jit(solution)/shard_map/ppermute | solution.py:407
  496.3 14.2 %shard_map.143 = (f32[8,64,64]{2,1,0:T(8,128)S(1)}, f32[8,128,128]{2,1,0:T(8,128)S(1)}) custom-call(f32[8,8,8,32,128]{4,3,2,1,0:T(8,128)} %bitcast.54, f32[8,2,8,32,128]{4,3,2,1,0:T(8,128)S(1)} %bitcast.77, f32[8,2,8,32,128]{4,3,2,1,0:T(8,128)S(1)} %bitcast.74, f32[8,2,8,32,128]{4,3,2,1,0:T(8,128)} %bitcast.23.refs_2_.refs_3_, ...), custom_call_target="tpu_custom_call" | custom-call | tf_op jit(solution)/shard_map/pallas_call | solution.py:47
  545.8 6.6 %collective-permute-done.29.refs_1_ = f32[320,128]{1,0:T(8,128)S(1)} collective-permute-done((f32[320,128]{1,0:T(8,128)S(1)}, f32[320,128]{1,0:T(8,128)S(1)}, u32[]{:S(2)}, u32[]{:S(2)}) %collective-permute-start.29) | collective-permute-done | bytes 163872 | tf_op jit(solution)/shard_map/ppermute | solution.py:490
  (319 shorter events, 229.3 us)
Async XLA Ops:
  0.6 104.2 %all-to-all-start = ((f32[8,8,8,32,128]{4,3,2,1,0:T(8,128)}), f32[8,8,8,32,128]{4,3,2,1,0:T(8,128)}, u32[]{:S(2)}, u32[]{:S(2)}) async-start(f32[8,8,8,32,128]{4,3,2,1,0:T(8,128)} %bitcast.53), calls=%async_computation | async-start | bytes 16777216 | tf_op jit(solution)/shard_map/all_to_all | solution.py:410
  9.5 53.2 %collective-permute-start.3 = (f32[128,32,128]{2,1,0:T(8,128)S(1)}, f32[128,32,128]{2,1,0:T(8,128)}, u32[]{:S(2)}, u32[]{:S(2)}) collective-permute-start(f32[128,32,128]{2,1,0:T(8,128)S(1)} %bitcast.65), channel_id=1, source_target_pairs={{0,1},{3,2},{4,5},{7,6},{8,9},{11,10},{12,13},{15,14},{16,17},{19,... | collective-permute-start | bytes 6291464 | tf_op jit(solution)/shard_map/ppermute | solution.py:407
  15.7 47.0 %collective-permute-start.4 = (f32[128,32,128]{2,1,0:T(8,128)S(1)}, f32[128,32,128]{2,1,0:T(8,128)}, u32[]{:S(2)}, u32[]{:S(2)}) collective-permute-start(f32[128,32,128]{2,1,0:T(8,128)S(1)} %bitcast.66), channel_id=1, source_target_pairs={{1,2},{2,1},{5,6},{6,5},{9,10},{10,9},{13,14},{14,13},{17,18},{18,... | collective-permute-start | bytes 6291464 | tf_op jit(solution)/shard_map/ppermute | solution.py:407
  20.6 84.2 %collective-permute-start = (f32[128,32,128]{2,1,0:T(8,128)}, f32[128,32,128]{2,1,0:T(8,128)}, u32[]{:S(2)}, u32[]{:S(2)}) collective-permute-start(f32[128,32,128]{2,1,0:T(8,128)} %bitcast.4.refs_2_.refs_0_), channel_id=1, source_target_pairs={{0,1},{3,2},{4,5},{7,6},{8,9},{11,10},{12,13},{15,14},{16,17},{19,... | collective-permute-start | bytes 6291464 | tf_op jit(solution)/shard_map/ppermute | solution.py:407
  23.5 81.3 %collective-permute-start.1 = (f32[128,32,128]{2,1,0:T(8,128)}, f32[128,32,128]{2,1,0:T(8,128)}, u32[]{:S(2)}, u32[]{:S(2)}) collective-permute-start(f32[128,32,128]{2,1,0:T(8,128)} %bitcast.4.refs_2_.refs_0_), channel_id=1, source_target_pairs={{1,2},{2,1},{5,6},{6,5},{9,10},{10,9},{13,14},{14,13},{17,18},{18,... | collective-permute-start | bytes 6291464 | tf_op jit(solution)/shard_map/ppermute | solution.py:407
  113.6 53.7 %all-to-all-start.1 = ((f32[8,4,8,32,128]{4,3,2,1,0:T(8,128)}), f32[8,4,8,32,128]{4,3,2,1,0:T(8,128)}, u32[]{:S(2)}, u32[]{:S(2)}) async-start(f32[8,4,8,32,128]{4,3,2,1,0:T(8,128)} %copy-done.10), calls=%async_computation.1 | async-start | bytes 8388608 | tf_op jit(solution)/shard_map/all_to_all | solution.py:410
  118.1 55.8 %collective-permute-start.2 = (f32[128,32,128]{2,1,0:T(8,128)}, f32[128,32,128]{2,1,0:T(8,128)}, u32[]{:S(2)}, u32[]{:S(2)}) collective-permute-start(f32[128,32,128]{2,1,0:T(8,128)} %collective-permute-done.refs_3_.refs_1_), channel_id=1, source_target_pairs={{1,2},{2,1},{5,6},{6,5},{9,10},{10,9},{13,14},{14,13},{17,18},{18,... | collective-permute-start | bytes 6291464 | tf_op jit(solution)/shard_map/ppermute | solution.py:407
  126.5 92.5 %collective-permute-start.7 = (f32[128,32,128]{2,1,0:T(8,128)}, f32[128,32,128]{2,1,0:T(8,128)}, u32[]{:S(2)}, u32[]{:S(2)}) collective-permute-start(f32[128,32,128]{2,1,0:T(8,128)} %bitcast.16.refs_2_.refs_0_), channel_id=1, source_target_pairs={{0,1},{3,2},{4,5},{7,6},{8,9},{11,10},{12,13},{15,14},{16,17},{19,... | collective-permute-start | bytes 6291464 | tf_op jit(solution)/shard_map/ppermute | solution.py:407
  167.3 83.2 %all-to-all-start.2 = ((f32[8,4,8,32,128]{4,3,2,1,0:T(8,128)}), f32[8,4,8,32,128]{4,3,2,1,0:T(8,128)}, u32[]{:S(2)}, u32[]{:S(2)}) async-start(f32[8,4,8,32,128]{4,3,2,1,0:T(8,128)} %copy-done.12), calls=%async_computation.2 | async-start | bytes 8388608 | tf_op jit(solution)/shard_map/all_to_all | solution.py:410
  173.1 65.4 %collective-permute-start.6 = (f32[128,32,128]{2,1,0:T(8,128)}, f32[128,32,128]{2,1,0:T(8,128)S(1)}, u32[]{:S(2)}, u32[]{:S(2)}) collective-permute-start(f32[128,32,128]{2,1,0:T(8,128)} %collective-permute-done.3.refs_5_.refs_3_.refs_1_), channel_id=1, source_target_pairs={{1,2},{2,1},{5,6},{6,5},{9,10},{10,9},{13,14},{14,13},{17,18},{18,... | collective-permute-start | bytes 6291464 | tf_op jit(solution)/shard_map/ppermute | solution.py:407
  182.4 85.5 %collective-permute-start.5 = (f32[128,32,128]{2,1,0:T(8,128)}, f32[128,32,128]{2,1,0:T(8,128)}, u32[]{:S(2)}, u32[]{:S(2)}) collective-permute-start(f32[128,32,128]{2,1,0:T(8,128)} %get-tuple-element.15.refs_6_), channel_id=1, source_target_pairs={{1,0},{2,3},{5,4},{6,7},{9,8},{10,11},{13,12},{14,15},{17,16},{18,... | collective-permute-start | bytes 6291464 | tf_op jit(solution)/shard_map/ppermute | solution.py:407
  216.9 69.3 %collective-permute-start.11 = (f32[128,32,128]{2,1,0:T(8,128)}, f32[128,32,128]{2,1,0:T(8,128)}, u32[]{:S(2)}, u32[]{:S(2)}) collective-permute-start(f32[128,32,128]{2,1,0:T(8,128)} %bitcast.16.refs_2_.refs_0_), channel_id=1, source_target_pairs={{1,2},{2,1},{5,6},{6,5},{9,10},{10,9},{13,14},{14,13},{17,18},{18,... | collective-permute-start | bytes 6291464 | tf_op jit(solution)/shard_map/ppermute | solution.py:407
  219.0 67.2 %collective-permute-start.12 = (f32[128,32,128]{2,1,0:T(8,128)}, f32[128,32,128]{2,1,0:T(8,128)}, u32[]{:S(2)}, u32[]{:S(2)}) collective-permute-start(f32[128,32,128]{2,1,0:T(8,128)} %collective-permute-done.7.refs_7_.refs_3_.refs_1_), channel_id=1, source_target_pairs={{1,2},{2,1},{5,6},{6,5},{9,10},{10,9},{13,14},{14,13},{17,18},{18,... | collective-permute-start | bytes 6291464 | tf_op jit(solution)/shard_map/ppermute | solution.py:407
  249.2 49.2 %collective-permute-start.10 = (f32[128,32,128]{2,1,0:T(8,128)}, f32[128,32,128]{2,1,0:T(8,128)}, u32[]{:S(2)}, u32[]{:S(2)}) collective-permute-start(f32[128,32,128]{2,1,0:T(8,128)} %get-tuple-element.17.refs_6_), channel_id=1, source_target_pairs={{1,0},{2,3},{5,4},{6,7},{9,8},{10,11},{13,12},{14,15},{17,16},{18,... | collective-permute-start | bytes 6291464 | tf_op jit(solution)/shard_map/ppermute | solution.py:407
  276.1 52.4 %collective-permute-start.17 = (f32[128,32,128]{2,1,0:T(8,128)}, f32[128,32,128]{2,1,0:T(8,128)}, u32[]{:S(2)}, u32[]{:S(2)}) collective-permute-start(f32[128,32,128]{2,1,0:T(8,128)} %bitcast.85), channel_id=1, source_target_pairs={{0,1},{3,2},{4,5},{7,6},{8,9},{11,10},{12,13},{15,14},{16,17},{19,... | collective-permute-start | bytes 6291464 | tf_op jit(solution)/shard_map/ppermute | solution.py:407
  283.6 89.8 %collective-permute-start.16 = (f32[128,32,128]{2,1,0:T(8,128)}, f32[128,32,128]{2,1,0:T(8,128)}, u32[]{:S(2)}, u32[]{:S(2)}) collective-permute-start(f32[128,32,128]{2,1,0:T(8,128)} %bitcast.82), channel_id=1, source_target_pairs={{0,1},{3,2},{4,5},{7,6},{8,9},{11,10},{12,13},{15,14},{16,17},{19,... | collective-permute-start | bytes 6291464 | tf_op jit(solution)/shard_map/ppermute | solution.py:407
  294.6 89.4 %collective-permute-start.13 = (f32[128,32,128]{2,1,0:T(8,128)}, f32[128,32,128]{2,1,0:T(8,128)}, u32[]{:S(2)}, u32[]{:S(2)}) collective-permute-start(f32[128,32,128]{2,1,0:T(8,128)} %get-tuple-element.19.refs_6_), channel_id=1, source_target_pairs={{1,0},{2,3},{5,4},{6,7},{9,8},{10,11},{13,12},{14,15},{17,16},{18,... | collective-permute-start | bytes 6291464 | tf_op jit(solution)/shard_map/ppermute | solution.py:407
  303.7 85.7 %all-to-all-start.3 = ((f32[8,2,8,32,128]{4,3,2,1,0:T(8,128)}), f32[8,2,8,32,128]{4,3,2,1,0:T(8,128)}, u32[]{:S(2)}, u32[]{:S(2)}) async-start(f32[8,2,8,32,128]{4,3,2,1,0:T(8,128)} %bitcast.72), calls=%async_computation.3 | async-start | bytes 4194304 | tf_op jit(solution)/shard_map/all_to_all | solution.py:410
  308.1 73.0 %collective-permute-start.14 = (f32[64,32,128]{2,1,0:T(8,128)}, f32[64,32,128]{2,1,0:T(8,128)S(1)}, u32[]{:S(2)}, u32[]{:S(2)}) collective-permute-start(f32[64,32,128]{2,1,0:T(8,128)} %bitcast.96), channel_id=1, source_target_pairs={{1,2},{2,1},{5,6},{6,5},{9,10},{10,9},{13,14},{14,13},{17,18},{18,... | collective-permute-start | bytes 3145736 | tf_op jit(solution)/shard_map/ppermute | solution.py:407
  309.0 72.1 %collective-permute-start.15 = (f32[64,32,128]{2,1,0:T(8,128)}, f32[64,32,128]{2,1,0:T(8,128)S(1)}, u32[]{:S(2)}, u32[]{:S(2)}) collective-permute-start(f32[64,32,128]{2,1,0:T(8,128)} %copy-done.22), channel_id=1, source_target_pairs={{1,2},{2,1},{5,6},{6,5},{9,10},{10,9},{13,14},{14,13},{17,18},{18,... | collective-permute-start | bytes 3145736 | tf_op jit(solution)/shard_map/ppermute | solution.py:407
  328.4 90.7 %collective-permute-start.21 = (f32[128,32,128]{2,1,0:T(8,128)}, f32[128,32,128]{2,1,0:T(8,128)}, u32[]{:S(2)}, u32[]{:S(2)}) collective-permute-start(f32[128,32,128]{2,1,0:T(8,128)} %bitcast.79), channel_id=1, source_target_pairs={{0,1},{3,2},{4,5},{7,6},{8,9},{11,10},{12,13},{15,14},{16,17},{19,... | collective-permute-start | bytes 6291464 | tf_op jit(solution)/shard_map/ppermute | solution.py:407
  396.8 72.3 %collective-permute-start.23 = (f32[64,32,128]{2,1,0:T(8,128)S(1)}, f32[64,32,128]{2,1,0:T(8,128)}, u32[]{:S(2)}, u32[]{:S(2)}) collective-permute-start(f32[64,32,128]{2,1,0:T(8,128)S(1)} %bitcast.93), channel_id=1, source_target_pairs={{0,1},{3,2},{4,5},{7,6},{8,9},{11,10},{12,13},{15,14},{16,17},{19,... | collective-permute-start | bytes 3145736 | tf_op jit(solution)/shard_map/ppermute | solution.py:407
  430.8 46.3 %collective-permute-start.22 = (f32[64,32,128]{2,1,0:T(8,128)}, f32[64,32,128]{2,1,0:T(8,128)}, u32[]{:S(2)}, u32[]{:S(2)}) collective-permute-start(f32[64,32,128]{2,1,0:T(8,128)} %get-tuple-element.23.refs_6_), channel_id=1, source_target_pairs={{1,0},{2,3},{5,4},{6,7},{9,8},{10,11},{13,12},{14,15},{17,16},{18,... | collective-permute-start | bytes 3145736 | tf_op jit(solution)/shard_map/ppermute | solution.py:407
  438.9 74.2 %collective-permute-start.24 = (f32[64,32,128]{2,1,0:T(8,128)}, f32[64,32,128]{2,1,0:T(8,128)}, u32[]{:S(2)}, u32[]{:S(2)}) collective-permute-start(f32[64,32,128]{2,1,0:T(8,128)} %bitcast.20.refs_3_.refs_2_), channel_id=1, source_target_pairs={{0,1},{3,2},{4,5},{7,6},{8,9},{11,10},{12,13},{15,14},{16,17},{19,... | collective-permute-start | bytes 3145736 | tf_op jit(solution)/shard_map/ppermute | solution.py:407
  (98 other events, 1258.4 us)

commit v5 on v4

--- a/solution.py
+++ b/solution.py
@@ -38,7 +38,7 @@
     return high, low
 
 
-def run(body, grid, in_specs, out_specs, out_shape, args, done):
+def run(body, grid, in_specs, out_specs, out_shape, args, done, limit=VMEM_LIMIT):
     count, extra = len(args), len(done)
 
     def kernel(*refs):
@@ -50,7 +50,7 @@
         in_specs=list(in_specs) + [pl.BlockSpec(memory_space=pltpu.HBM)] * extra,
         out_specs=out_specs,
         out_shape=out_shape,
-        compiler_params=pltpu.CompilerParams(vmem_limit_bytes=VMEM_LIMIT),
+        compiler_params=pltpu.CompilerParams(vmem_limit_bytes=limit),
         cost_estimate=pl.CostEstimate(flops=0, bytes_accessed=0, transcendentals=0),
     )(*args, *done)
 
@@ -221,6 +221,7 @@
         ],
         (x, *adjoints,),
         done,
+        56 * 1024 * 1024,
     )
     zero = jnp.sum(zero, axis=0)
     columns, at = [], 0

time: 557 us -> 554 us (level)
    unnamed x168 -> x154, local copies, waits for them, and re-layouts: 41.3 us -> 37.8 us
  transfers between devices with their start and end apart: 38 -> 38, of which waited for: 13 -> 13; matrix products, arithmetic and copies ran while one was open for 4% -> 4% of each run, Pallas kernels for 30% -> 31%
where the time goes in v5:
time: 554 us; the launch traced here: 550 us
  Pallas kernels  179 us (32%)
  starting transfers between devices  159 us (29%)
  waiting for transfers between devices  149 us (27%)
  local copies, waits for them, and re-layouts  40 us (7%)
  other arithmetic  16.4 us (3%)
  between operations  5.74 us (1%)
    pallas_call x35, Pallas kernels, run(): pl.pallas_call(kernel, grid=grid, in_specs=list(in_specs) + [pl.BlockSpec...  179 us
    ppermute x25, starting transfers between devices, shift(): return lax.ppermute(value, 'narrow', pairs)  118 us
    ppermute x25, waiting for transfers between devices, shift(): return lax.ppermute(value, 'narrow', pairs)  106 us
    unnamed x154, local copies, waits for them, and re-layouts  37.8 us
    all_to_all x8, starting transfers between devices, exchange(): return lax.all_to_all(value, 'wide', 0, 0, tiled=True)  36.3 us
    ppermute x5, waiting for transfers between devices, partner(): lax.ppermute(value, axis, [(i, i ^ step) for i in range(lax.axis_size(axi...  21.5 us
    all_to_all x8, waiting for transfers between devices, exchange(): return lax.all_to_all(value, 'wide', 0, 0, tiled=True)  21.2 us
  transfers between devices with their start and end apart: 38, of which 13 were waited for; matrix products, arithmetic and copies ran while one was open for 4% of the time, Pallas kernels for 31%

profile of v5, /device:TPU:0, one launch (start us, length us, event | category | flops | bytes accessed | tf_op | source)
XLA Modules:
  0.0 550.3 jit_solution(453860097459548539)
XLA Ops:
  9.5 6.2 %collective-permute-start.3 = (f32[128,32,128]{2,1,0:T(8,128)S(1)}, f32[128,32,128]{2,1,0:T(8,128)}, u32[]{:S(2)}, u32[]{:S(2)}) collective-permute-start(f32[128,32,128]{2,1,0:T(8,128)S(1)} %bitcast.65), channel_id=1, source_target_pairs={{0,1},{3,2},{4,5},{7,6},{8,9},{11,10},{12,13},{15,14},{16,17},{19,... | collective-permute-start | bytes 6291464 | tf_op jit(solution)/shard_map/ppermute | solution.py:408
  38.3 21.2 %shard_map.116.refs_2_ = f32[64,8,32,128]{3,2,1,0:T(8,128)S(1)} custom-call(f32[64,8,32,128]{3,2,1,0:T(8,128)} %refs_0_.1, f32[64,8,32,128]{3,2,1,0:T(8,128)} %refs_1_.1, f32[64,64]{1,0:T(8,128)S(1)} %copy.23.refs_2_, f32[128,128]{1,0:T(8,128)S(1)} %fusion.refs_3_, f32[64,32,128]{2,1,0:T(8,128)S(1)} %bitcast.87), custom_call_target="tpu_custom_call" | custom-call | tf_op jit(solution)/shard_map/pallas_call | solution.py:47
  62.9 42.0 %collective-permute-done.refs_3_.refs_1_ = f32[128,32,128]{2,1,0:T(8,128)} collective-permute-done((f32[128,32,128]{2,1,0:T(8,128)}, f32[128,32,128]{2,1,0:T(8,128)}, u32[]{:S(2)}, u32[]{:S(2)}) %collective-permute-start) | collective-permute-done | bytes 2097184 | tf_op jit(solution)/shard_map/ppermute | solution.py:408
  104.9 6.7 %shard_map.117.refs_2_ = f32[8,4,8,32,128]{4,3,2,1,0:T(8,128)S(1)} custom-call(f32[8,8,8,32,128]{4,3,2,1,0:T(8,128)} %all-to-all-done.refs_0_, f32[8,64,64]{2,1,0:T(8,128)S(1)} %add_multiply_fusion.refs_1_, f32[64,8,32,128]{3,2,1,0:T(8,128)} %copy-done.3, f32[128,32,128]{2,1,0:T(8,128)} %collective-permute-done.refs_3_.refs_1_, ...), custom_call_target="tpu_custom_call" | custom-call | tf_op jit(solution)/shard_map/pallas_call | solution.py:47
  126.5 8.6 %collective-permute-start.7 = (f32[128,32,128]{2,1,0:T(8,128)}, f32[128,32,128]{2,1,0:T(8,128)}, u32[]{:S(2)}, u32[]{:S(2)}) collective-permute-start(f32[128,32,128]{2,1,0:T(8,128)} %bitcast.16.refs_2_.refs_0_), channel_id=1, source_target_pairs={{0,1},{3,2},{4,5},{7,6},{8,9},{11,10},{12,13},{15,14},{16,17},{19,... | collective-permute-start | bytes 6291464 | tf_op jit(solution)/shard_map/ppermute | solution.py:408
  137.3 6.8 %shard_map.118.refs_6_ = f32[8,4,8,32,128]{4,3,2,1,0:T(8,128)S(1)} custom-call(f32[8,8,8,32,128]{4,3,2,1,0:T(8,128)} %all-to-all-done.refs_0_, f32[8,64,64]{2,1,0:T(8,128)S(1)} %add_multiply_fusion.refs_1_, f32[8,4,8,32,128]{4,3,2,1,0:T(8,128)S(1)} %copy-done.9), custom_call_target="tpu_custom_call" | custom-call | tf_op jit(solution)/shard_map/pallas_call | solution.py:47
  146.1 21.2 %all-to-all-done.1.refs_1_ = f32[8,4,8,32,128]{4,3,2,1,0:T(8,128)} async-done(((f32[8,4,8,32,128]{4,3,2,1,0:T(8,128)}), f32[8,4,8,32,128]{4,3,2,1,0:T(8,128)}, u32[]{:S(2)}, u32[]{:S(2)}) %all-to-all-start.1) | async-done | bytes 4194336 | tf_op jit(solution)/shard_map/all_to_all | solution.py:411
  173.9 8.4 %shard_map.119 = (f32[128,32,128]{2,1,0:T(8,128)S(1)}, f32[128,32,128]{2,1,0:T(8,128)}) custom-call(f32[1,128]{1,0:T(1,128)S(1)} %convert_bitcast_fusion.refs_0_, f32[128,128]{1,0:T(8,128)S(1)} %fusion.2.refs_1_, f32[128,32,128]{2,1,0:T(8,128)} %bitcast.4.refs_2_.refs_0_, f32[128,32,128]{2,1,0:T(8,128)} %collective-permute-done.refs_3_.refs_1_, ...), custom_call_target="tpu_custom_call" | custom-call | tf_op jit(solution)/shard_map/pallas_call | solution.py:47
  183.7 9.8 %collective-permute-start.9 = (f32[64,32,128]{2,1,0:T(8,128)S(1)}, f32[64,32,128]{2,1,0:T(8,128)S(1)}, u32[]{:S(2)}, u32[]{:S(2)}) collective-permute-start(f32[64,32,128]{2,1,0:T(8,128)S(1)} %bitcast.88), channel_id=1, source_target_pairs={{0,1},{3,2},{4,5},{7,6},{8,9},{11,10},{12,13},{15,14},{16,17},{19,... | collective-permute-start | bytes 3145736 | tf_op jit(solution)/shard_map/ppermute | solution.py:408
  198.4 18.5 %collective-permute-done.9.refs_9_.refs_3_.refs_1_ = f32[64,32,128]{2,1,0:T(8,128)S(1)} collective-permute-done((f32[64,32,128]{2,1,0:T(8,128)S(1)}, f32[64,32,128]{2,1,0:T(8,128)S(1)}, u32[]{:S(2)}, u32[]{:S(2)}) %collective-permute-start.9) | collective-permute-done | bytes 1048608 | tf_op jit(solution)/shard_map/ppermute | solution.py:408
  232.1 6.4 %collective-permute-done.8.refs_8_.refs_3_.refs_1_ = f32[64,32,128]{2,1,0:T(8,128)S(1)} collective-permute-done((f32[64,32,128]{2,1,0:T(8,128)S(1)}, f32[64,32,128]{2,1,0:T(8,128)S(1)}, u32[]{:S(2)}, u32[]{:S(2)}) %collective-permute-start.8) | collective-permute-done | bytes 1048608 | tf_op jit(solution)/shard_map/ppermute | solution.py:408
  239.8 8.0 %shard_map.124 = (f32[128,32,128]{2,1,0:T(8,128)S(1)}, f32[128,32,128]{2,1,0:T(8,128)}) custom-call(f32[1,128]{1,0:T(1,128)S(1)} %convert_bitcast_fusion.refs_0_, f32[128,128]{1,0:T(8,128)S(1)} %fusion.2.refs_1_, f32[128,32,128]{2,1,0:T(8,128)S(1)} %bitcast.70, f32[128,32,128]{2,1,0:T(8,128)} %collective-permute-done.3.refs_5_.refs_3_.refs_1_, ...), custom_call_target="tpu_custom_call" | custom-call | tf_op jit(solution)/shard_map/pallas_call | solution.py:47
  275.6 7.5 %collective-permute-start.17 = (f32[128,32,128]{2,1,0:T(8,128)}, f32[128,32,128]{2,1,0:T(8,128)}, u32[]{:S(2)}, u32[]{:S(2)}) collective-permute-start(f32[128,32,128]{2,1,0:T(8,128)} %bitcast.85), channel_id=1, source_target_pairs={{0,1},{3,2},{4,5},{7,6},{8,9},{11,10},{12,13},{15,14},{16,17},{19,... | collective-permute-start | bytes 6291464 | tf_op jit(solution)/shard_map/ppermute | solution.py:408
  285.7 8.4 %shard_map.129 = (f32[128,32,128]{2,1,0:T(8,128)S(1)}, f32[128,32,128]{2,1,0:T(8,128)}) custom-call(f32[1,128]{1,0:T(1,128)S(1)} %convert_bitcast_fusion.refs_0_, f32[128,128]{1,0:T(8,128)S(1)} %fusion.2.refs_1_, f32[128,32,128]{2,1,0:T(8,128)} %bitcast.16.refs_2_.refs_0_, f32[128,32,128]{2,1,0:T(8,128)} %collective-permute-done.7.refs_7_.refs_3_.refs_1_, ...), custom_call_target="tpu_custom_call" | custom-call | tf_op jit(solution)/shard_map/pallas_call | solution.py:47
  309.7 18.3 %collective-permute-done.17.refs_5_ = f32[128,32,128]{2,1,0:T(8,128)} collective-permute-done((f32[128,32,128]{2,1,0:T(8,128)}, f32[128,32,128]{2,1,0:T(8,128)}, u32[]{:S(2)}, u32[]{:S(2)}) %collective-permute-start.17) | collective-permute-done | bytes 2097184 | tf_op jit(solution)/shard_map/ppermute | solution.py:408
  328.0 18.8 %collective-permute-start.21 = (f32[128,32,128]{2,1,0:T(8,128)}, f32[128,32,128]{2,1,0:T(8,128)}, u32[]{:S(2)}, u32[]{:S(2)}) collective-permute-start(f32[128,32,128]{2,1,0:T(8,128)} %bitcast.79), channel_id=1, source_target_pairs={{0,1},{3,2},{4,5},{7,6},{8,9},{11,10},{12,13},{15,14},{16,17},{19,... | collective-permute-start | bytes 6291464 | tf_op jit(solution)/shard_map/ppermute | solution.py:408
  348.5 8.5 %shard_map.131.refs_7_ = f32[8,128,64]{2,1,0:T(8,128)S(1)} custom-call(f32[128,32,128]{2,1,0:T(8,128)} %bitcast.4.refs_2_.refs_0_, f32[128,32,128]{2,1,0:T(8,128)} %collective-permute-done.refs_3_.refs_1_, f32[128,32,128]{2,1,0:T(8,128)} %collective-permute-done.1.refs_4_.refs_2_, f32[128,32,128]{2,1,0:T(8,128)} %collective-permute-done.2.refs_5_.refs_3_, ...), custom_call_target="tpu_custom_call" | custom-call | tf_op jit(solution)/shard_map/pallas_call | solution.py:47
  357.0 16.0 %collective-permute-done.16.refs_5_ = f32[128,32,128]{2,1,0:T(8,128)} collective-permute-done((f32[128,32,128]{2,1,0:T(8,128)}, f32[128,32,128]{2,1,0:T(8,128)}, u32[]{:S(2)}, u32[]{:S(2)}) %collective-permute-start.16) | collective-permute-done | bytes 2097184 | tf_op jit(solution)/shard_map/ppermute | solution.py:408
  373.0 7.6 %shard_map.132.refs_6_ = f32[8,128,64]{2,1,0:T(8,128)S(1)} custom-call(f32[128,32,128]{2,1,0:T(8,128)S(1)} %bitcast.71, f32[128,32,128]{2,1,0:T(8,128)} %collective-permute-done.3.refs_5_.refs_3_.refs_1_, f32[128,32,128]{2,1,0:T(8,128)} %collective-permute-done.4.refs_6_.refs_4_.refs_2_, f32[128,32,128]{2,1,0:T(8,128)S(1)} %copy-done.28, ...), custom_call_target="tpu_custom_call" | custom-call | tf_op jit(solution)/shard_map/pallas_call | solution.py:47
  396.4 13.9 %collective-permute-start.23 = (f32[64,32,128]{2,1,0:T(8,128)}, f32[64,32,128]{2,1,0:T(8,128)}, u32[]{:S(2)}, u32[]{:S(2)}) collective-permute-start(f32[64,32,128]{2,1,0:T(8,128)} %bitcast.19.refs_2_), channel_id=1, source_target_pairs={{0,1},{3,2},{4,5},{7,6},{8,9},{11,10},{12,13},{15,14},{16,17},{19,... | collective-permute-start | bytes 3145736 | tf_op jit(solution)/shard_map/ppermute | solution.py:408
  419.2 8.7 %shard_map.137.refs_6_ = f32[8,128,64]{2,1,0:T(8,128)S(1)} custom-call(f32[128,32,128]{2,1,0:T(8,128)} %bitcast.16.refs_2_.refs_0_, f32[128,32,128]{2,1,0:T(8,128)} %collective-permute-done.7.refs_7_.refs_3_.refs_1_, f32[128,32,128]{2,1,0:T(8,128)} %collective-permute-done.11.refs_4_.refs_2_, f32[128,32,128]{2,1,0:T(8,128)} %collective-permute-done.12.refs_5_.refs_3_, ...), custom_call_target="tpu_custom_call" | custom-call | tf_op jit(solution)/shard_map/pallas_call | solution.py:47
  441.1 26.0 %collective-permute-start.24 = (f32[64,32,128]{2,1,0:T(8,128)S(1)}, f32[64,32,128]{2,1,0:T(8,128)}, u32[]{:S(2)}, u32[]{:S(2)}) collective-permute-start(f32[64,32,128]{2,1,0:T(8,128)S(1)} %bitcast.93), channel_id=1, source_target_pairs={{0,1},{3,2},{4,5},{7,6},{8,9},{11,10},{12,13},{15,14},{16,17},{19,... | collective-permute-start | bytes 3145736 | tf_op jit(solution)/shard_map/ppermute | solution.py:408
  492.3 14.9 %shard_map.143 = (f32[8,64,64]{2,1,0:T(8,128)}, f32[8,128,128]{2,1,0:T(8,128)}) custom-call(f32[8,8,8,32,128]{4,3,2,1,0:T(8,128)} %bitcast.54, f32[8,2,8,32,128]{4,3,2,1,0:T(8,128)} %bitcast.77, f32[8,2,8,32,128]{4,3,2,1,0:T(8,128)} %bitcast.74, f32[8,2,8,32,128]{4,3,2,1,0:T(8,128)} %bitcast.23.refs_2_.refs_3_, ...), custom_call_target="tpu_custom_call" | custom-call | tf_op jit(solution)/shard_map/pallas_call | solution.py:47
  542.8 6.6 %collective-permute-done.29.refs_1_ = f32[320,128]{1,0:T(8,128)S(1)} collective-permute-done((f32[320,128]{1,0:T(8,128)S(1)}, f32[320,128]{1,0:T(8,128)S(1)}, u32[]{:S(2)}, u32[]{:S(2)}) %collective-permute-start.29) | collective-permute-done | bytes 163872 | tf_op jit(solution)/shard_map/ppermute | solution.py:491
  (305 shorter events, 225.4 us)
Async XLA Ops:
  0.6 104.2 %all-to-all-start = ((f32[8,8,8,32,128]{4,3,2,1,0:T(8,128)}), f32[8,8,8,32,128]{4,3,2,1,0:T(8,128)}, u32[]{:S(2)}, u32[]{:S(2)}) async-start(f32[8,8,8,32,128]{4,3,2,1,0:T(8,128)} %bitcast.53), calls=%async_computation | async-start | bytes 16777216 | tf_op jit(solution)/shard_map/all_to_all | solution.py:411
  9.5 53.4 %collective-permute-start.3 = (f32[128,32,128]{2,1,0:T(8,128)S(1)}, f32[128,32,128]{2,1,0:T(8,128)}, u32[]{:S(2)}, u32[]{:S(2)}) collective-permute-start(f32[128,32,128]{2,1,0:T(8,128)S(1)} %bitcast.65), channel_id=1, source_target_pairs={{0,1},{3,2},{4,5},{7,6},{8,9},{11,10},{12,13},{15,14},{16,17},{19,... | collective-permute-start | bytes 6291464 | tf_op jit(solution)/shard_map/ppermute | solution.py:408
  15.7 47.1 %collective-permute-start.4 = (f32[128,32,128]{2,1,0:T(8,128)S(1)}, f32[128,32,128]{2,1,0:T(8,128)}, u32[]{:S(2)}, u32[]{:S(2)}) collective-permute-start(f32[128,32,128]{2,1,0:T(8,128)S(1)} %bitcast.66), channel_id=1, source_target_pairs={{1,2},{2,1},{5,6},{6,5},{9,10},{10,9},{13,14},{14,13},{17,18},{18,... | collective-permute-start | bytes 6291464 | tf_op jit(solution)/shard_map/ppermute | solution.py:408
  20.7 84.2 %collective-permute-start = (f32[128,32,128]{2,1,0:T(8,128)}, f32[128,32,128]{2,1,0:T(8,128)}, u32[]{:S(2)}, u32[]{:S(2)}) collective-permute-start(f32[128,32,128]{2,1,0:T(8,128)} %bitcast.4.refs_2_.refs_0_), channel_id=1, source_target_pairs={{0,1},{3,2},{4,5},{7,6},{8,9},{11,10},{12,13},{15,14},{16,17},{19,... | collective-permute-start | bytes 6291464 | tf_op jit(solution)/shard_map/ppermute | solution.py:408
  23.5 81.3 %collective-permute-start.1 = (f32[128,32,128]{2,1,0:T(8,128)}, f32[128,32,128]{2,1,0:T(8,128)}, u32[]{:S(2)}, u32[]{:S(2)}) collective-permute-start(f32[128,32,128]{2,1,0:T(8,128)} %bitcast.4.refs_2_.refs_0_), channel_id=1, source_target_pairs={{1,2},{2,1},{5,6},{6,5},{9,10},{10,9},{13,14},{14,13},{17,18},{18,... | collective-permute-start | bytes 6291464 | tf_op jit(solution)/shard_map/ppermute | solution.py:408
  113.6 53.7 %all-to-all-start.1 = ((f32[8,4,8,32,128]{4,3,2,1,0:T(8,128)}), f32[8,4,8,32,128]{4,3,2,1,0:T(8,128)}, u32[]{:S(2)}, u32[]{:S(2)}) async-start(f32[8,4,8,32,128]{4,3,2,1,0:T(8,128)} %copy-done.8), calls=%async_computation.1 | async-start | bytes 8388608 | tf_op jit(solution)/shard_map/all_to_all | solution.py:411
  118.2 55.8 %collective-permute-start.2 = (f32[128,32,128]{2,1,0:T(8,128)}, f32[128,32,128]{2,1,0:T(8,128)}, u32[]{:S(2)}, u32[]{:S(2)}) collective-permute-start(f32[128,32,128]{2,1,0:T(8,128)} %collective-permute-done.refs_3_.refs_1_), channel_id=1, source_target_pairs={{1,2},{2,1},{5,6},{6,5},{9,10},{10,9},{13,14},{14,13},{17,18},{18,... | collective-permute-start | bytes 6291464 | tf_op jit(solution)/shard_map/ppermute | solution.py:408
  126.5 92.4 %collective-permute-start.7 = (f32[128,32,128]{2,1,0:T(8,128)}, f32[128,32,128]{2,1,0:T(8,128)}, u32[]{:S(2)}, u32[]{:S(2)}) collective-permute-start(f32[128,32,128]{2,1,0:T(8,128)} %bitcast.16.refs_2_.refs_0_), channel_id=1, source_target_pairs={{0,1},{3,2},{4,5},{7,6},{8,9},{11,10},{12,13},{15,14},{16,17},{19,... | collective-permute-start | bytes 6291464 | tf_op jit(solution)/shard_map/ppermute | solution.py:408
  167.3 83.2 %all-to-all-start.2 = ((f32[8,4,8,32,128]{4,3,2,1,0:T(8,128)}), f32[8,4,8,32,128]{4,3,2,1,0:T(8,128)}, u32[]{:S(2)}, u32[]{:S(2)}) async-start(f32[8,4,8,32,128]{4,3,2,1,0:T(8,128)} %copy-done.10), calls=%async_computation.2 | async-start | bytes 8388608 | tf_op jit(solution)/shard_map/all_to_all | solution.py:411
  173.1 65.4 %collective-permute-start.6 = (f32[128,32,128]{2,1,0:T(8,128)}, f32[128,32,128]{2,1,0:T(8,128)S(1)}, u32[]{:S(2)}, u32[]{:S(2)}) collective-permute-start(f32[128,32,128]{2,1,0:T(8,128)} %collective-permute-done.3.refs_5_.refs_3_.refs_1_), channel_id=1, source_target_pairs={{1,2},{2,1},{5,6},{6,5},{9,10},{10,9},{13,14},{14,13},{17,18},{18,... | collective-permute-start | bytes 6291464 | tf_op jit(solution)/shard_map/ppermute | solution.py:408
  182.4 84.8 %collective-permute-start.5 = (f32[128,32,128]{2,1,0:T(8,128)}, f32[128,32,128]{2,1,0:T(8,128)}, u32[]{:S(2)}, u32[]{:S(2)}) collective-permute-start(f32[128,32,128]{2,1,0:T(8,128)} %get-tuple-element.15.refs_6_), channel_id=1, source_target_pairs={{1,0},{2,3},{5,4},{6,7},{9,8},{10,11},{13,12},{14,15},{17,16},{18,... | collective-permute-start | bytes 6291464 | tf_op jit(solution)/shard_map/ppermute | solution.py:408
  216.9 68.8 %collective-permute-start.11 = (f32[128,32,128]{2,1,0:T(8,128)}, f32[128,32,128]{2,1,0:T(8,128)}, u32[]{:S(2)}, u32[]{:S(2)}) collective-permute-start(f32[128,32,128]{2,1,0:T(8,128)} %bitcast.16.refs_2_.refs_0_), channel_id=1, source_target_pairs={{1,2},{2,1},{5,6},{6,5},{9,10},{10,9},{13,14},{14,13},{17,18},{18,... | collective-permute-start | bytes 6291464 | tf_op jit(solution)/shard_map/ppermute | solution.py:408
  218.9 66.9 %collective-permute-start.12 = (f32[128,32,128]{2,1,0:T(8,128)}, f32[128,32,128]{2,1,0:T(8,128)}, u32[]{:S(2)}, u32[]{:S(2)}) collective-permute-start(f32[128,32,128]{2,1,0:T(8,128)} %collective-permute-done.7.refs_7_.refs_3_.refs_1_), channel_id=1, source_target_pairs={{1,2},{2,1},{5,6},{6,5},{9,10},{10,9},{13,14},{14,13},{17,18},{18,... | collective-permute-start | bytes 6291464 | tf_op jit(solution)/shard_map/ppermute | solution.py:408
  249.2 49.2 %collective-permute-start.10 = (f32[128,32,128]{2,1,0:T(8,128)}, f32[128,32,128]{2,1,0:T(8,128)}, u32[]{:S(2)}, u32[]{:S(2)}) collective-permute-start(f32[128,32,128]{2,1,0:T(8,128)} %get-tuple-element.17.refs_6_), channel_id=1, source_target_pairs={{1,0},{2,3},{5,4},{6,7},{9,8},{10,11},{13,12},{14,15},{17,16},{18,... | collective-permute-start | bytes 6291464 | tf_op jit(solution)/shard_map/ppermute | solution.py:408
  275.6 52.4 %collective-permute-start.17 = (f32[128,32,128]{2,1,0:T(8,128)}, f32[128,32,128]{2,1,0:T(8,128)}, u32[]{:S(2)}, u32[]{:S(2)}) collective-permute-start(f32[128,32,128]{2,1,0:T(8,128)} %bitcast.85), channel_id=1, source_target_pairs={{0,1},{3,2},{4,5},{7,6},{8,9},{11,10},{12,13},{15,14},{16,17},{19,... | collective-permute-start | bytes 6291464 | tf_op jit(solution)/shard_map/ppermute | solution.py:408
  283.1 89.9 %collective-permute-start.16 = (f32[128,32,128]{2,1,0:T(8,128)}, f32[128,32,128]{2,1,0:T(8,128)}, u32[]{:S(2)}, u32[]{:S(2)}) collective-permute-start(f32[128,32,128]{2,1,0:T(8,128)} %bitcast.82), channel_id=1, source_target_pairs={{0,1},{3,2},{4,5},{7,6},{8,9},{11,10},{12,13},{15,14},{16,17},{19,... | collective-permute-start | bytes 6291464 | tf_op jit(solution)/shard_map/ppermute | solution.py:408
  294.2 89.5 %collective-permute-start.13 = (f32[128,32,128]{2,1,0:T(8,128)}, f32[128,32,128]{2,1,0:T(8,128)}, u32[]{:S(2)}, u32[]{:S(2)}) collective-permute-start(f32[128,32,128]{2,1,0:T(8,128)} %get-tuple-element.19.refs_6_), channel_id=1, source_target_pairs={{1,0},{2,3},{5,4},{6,7},{9,8},{10,11},{13,12},{14,15},{17,16},{18,... | collective-permute-start | bytes 6291464 | tf_op jit(solution)/shard_map/ppermute | solution.py:408
  303.7 85.3 %all-to-all-start.3 = ((f32[8,2,8,32,128]{4,3,2,1,0:T(8,128)}), f32[8,2,8,32,128]{4,3,2,1,0:T(8,128)}, u32[]{:S(2)}, u32[]{:S(2)}) async-start(f32[8,2,8,32,128]{4,3,2,1,0:T(8,128)} %bitcast.72), calls=%async_computation.3 | async-start | bytes 4194304 | tf_op jit(solution)/shard_map/all_to_all | solution.py:411
  308.1 72.6 %collective-permute-start.14 = (f32[64,32,128]{2,1,0:T(8,128)}, f32[64,32,128]{2,1,0:T(8,128)S(1)}, u32[]{:S(2)}, u32[]{:S(2)}) collective-permute-start(f32[64,32,128]{2,1,0:T(8,128)} %bitcast.96), channel_id=1, source_target_pairs={{1,2},{2,1},{5,6},{6,5},{9,10},{10,9},{13,14},{14,13},{17,18},{18,... | collective-permute-start | bytes 3145736 | tf_op jit(solution)/shard_map/ppermute | solution.py:408
  309.0 71.7 %collective-permute-start.15 = (f32[64,32,128]{2,1,0:T(8,128)}, f32[64,32,128]{2,1,0:T(8,128)S(1)}, u32[]{:S(2)}, u32[]{:S(2)}) collective-permute-start(f32[64,32,128]{2,1,0:T(8,128)} %copy-done.21), channel_id=1, source_target_pairs={{1,2},{2,1},{5,6},{6,5},{9,10},{10,9},{13,14},{14,13},{17,18},{18,... | collective-permute-start | bytes 3145736 | tf_op jit(solution)/shard_map/ppermute | solution.py:408
  328.0 91.2 %collective-permute-start.21 = (f32[128,32,128]{2,1,0:T(8,128)}, f32[128,32,128]{2,1,0:T(8,128)}, u32[]{:S(2)}, u32[]{:S(2)}) collective-permute-start(f32[128,32,128]{2,1,0:T(8,128)} %bitcast.79), channel_id=1, source_target_pairs={{0,1},{3,2},{4,5},{7,6},{8,9},{11,10},{12,13},{15,14},{16,17},{19,... | collective-permute-start | bytes 6291464 | tf_op jit(solution)/shard_map/ppermute | solution.py:408
  389.1 47.5 %all-to-all-start.5 = ((f32[8,2,8,32,128]{4,3,2,1,0:T(8,128)}), f32[8,2,8,32,128]{4,3,2,1,0:T(8,128)}, u32[]{:S(2)}, u32[]{:S(2)}) async-start(f32[8,2,8,32,128]{4,3,2,1,0:T(8,128)} %bitcast.23.refs_2_.refs_3_), calls=%async_computation.5 | async-start | bytes 4194304 | tf_op jit(solution)/shard_map/all_to_all | solution.py:411
  396.4 75.2 %collective-permute-start.23 = (f32[64,32,128]{2,1,0:T(8,128)}, f32[64,32,128]{2,1,0:T(8,128)}, u32[]{:S(2)}, u32[]{:S(2)}) collective-permute-start(f32[64,32,128]{2,1,0:T(8,128)} %bitcast.19.refs_2_), channel_id=1, source_target_pairs={{0,1},{3,2},{4,5},{7,6},{8,9},{11,10},{12,13},{15,14},{16,17},{19,... | collective-permute-start | bytes 3145736 | tf_op jit(solution)/shard_map/ppermute | solution.py:408
  441.1 68.8 %collective-permute-start.24 = (f32[64,32,128]{2,1,0:T(8,128)S(1)}, f32[64,32,128]{2,1,0:T(8,128)}, u32[]{:S(2)}, u32[]{:S(2)}) collective-permute-start(f32[64,32,128]{2,1,0:T(8,128)S(1)} %bitcast.93), channel_id=1, source_target_pairs={{0,1},{3,2},{4,5},{7,6},{8,9},{11,10},{12,13},{15,14},{16,17},{19,... | collective-permute-start | bytes 3145736 | tf_op jit(solution)/shard_map/ppermute | solution.py:408
  (91 other events, 1222.8 us)

commit v6 on v5

--- a/solution.py
+++ b/solution.py
@@ -471,7 +471,7 @@
     one_step(0, adjoints[2])
     one_step(1, ones[0])
     two_step(2, ones[1])
-    terms_step(4, twos[2])
+    terms_step(4, twos[2], others[3], others[4])
     finish(3, own[4])
     one_step(2, adjoints[3])
     two_step(3, ones[2])

time: 554 us -> 565 us (1.020)
  waiting for transfers between devices: 149 us -> 176 us
  starting transfers between devices: 159 us -> 148 us
    ppermute x25, waiting for transfers between devices: 106 us -> 133 us  [shift(): return lax.ppermute(value, 'narrow', pairs)]
    ppermute x25, starting transfers between devices: 118 us -> 108 us  [shift(): return lax.ppermute(value, 'narrow', pairs)]
    unnamed x154 -> x178, local copies, waits for them, and re-layouts: 37.8 us -> 37.8 us
  transfers between devices with their start and end apart: 38 -> 38, of which waited for: 13 -> 15; matrix products, arithmetic and copies ran while one was open for 4% -> 3% of each run, Pallas kernels for 31% -> 30%
where the time goes in v6:
time: 565 us; the launch traced here: 562 us
  Pallas kernels  177 us (31%)
  waiting for transfers between devices  176 us (31%)
  starting transfers between devices  148 us (26%)
  local copies, waits for them, and re-layouts  40 us (7%)
  other arithmetic  13.7 us (2%)
  between operations  5.87 us (1%)
    pallas_call x35, Pallas kernels, run(): pl.pallas_call(kernel, grid=grid, in_specs=list(in_specs) + [pl.BlockSpec...  177 us
    ppermute x25, waiting for transfers between devices, shift(): return lax.ppermute(value, 'narrow', pairs)  133 us
    ppermute x25, starting transfers between devices, shift(): return lax.ppermute(value, 'narrow', pairs)  108 us
    unnamed x178, local copies, waits for them, and re-layouts  37.8 us
    all_to_all x8, starting transfers between devices, exchange(): return lax.all_to_all(value, 'wide', 0, 0, tiled=True)  36.4 us
    ppermute x5, waiting for transfers between devices, partner(): lax.ppermute(value, axis, [(i, i ^ step) for i in range(lax.axis_size(axi...  22.3 us
    all_to_all x8, waiting for transfers between devices, exchange(): return lax.all_to_all(value, 'wide', 0, 0, tiled=True)  21.2 us
  transfers between devices with their start and end apart: 38, of which 15 were waited for; matrix products, arithmetic and copies ran while one was open for 3% of the time, Pallas kernels for 30%

profile of v6, /device:TPU:0, one launch (start us, length us, event | category | flops | bytes accessed | tf_op | source)
XLA Modules:
  0.0 562.0 jit_solution(2697173972236653928)
XLA Ops:
  38.2 21.2 %shard_map.116.refs_2_ = f32[64,8,32,128]{3,2,1,0:T(8,128)S(1)} custom-call(f32[64,8,32,128]{3,2,1,0:T(8,128)} %refs_0_.1, f32[64,8,32,128]{3,2,1,0:T(8,128)} %refs_1_.1, f32[64,64]{1,0:T(8,128)S(1)} %copy.23.refs_2_, f32[128,128]{1,0:T(8,128)S(1)} %fusion.refs_3_, f32[64,32,128]{2,1,0:T(8,128)S(1)} %bitcast.87), custom_call_target="tpu_custom_call" | custom-call | tf_op jit(solution)/shard_map/pallas_call | solution.py:47
  62.8 42.0 %collective-permute-done.refs_3_.refs_1_ = f32[128,32,128]{2,1,0:T(8,128)} collective-permute-done((f32[128,32,128]{2,1,0:T(8,128)}, f32[128,32,128]{2,1,0:T(8,128)}, u32[]{:S(2)}, u32[]{:S(2)}) %collective-permute-start) | collective-permute-done | bytes 2097184 | tf_op jit(solution)/shard_map/ppermute | solution.py:408
  104.8 6.8 %shard_map.117.refs_2_ = f32[8,4,8,32,128]{4,3,2,1,0:T(8,128)S(1)} custom-call(f32[8,8,8,32,128]{4,3,2,1,0:T(8,128)} %all-to-all-done.refs_0_, f32[8,64,64]{2,1,0:T(8,128)S(1)} %add_multiply_fusion.refs_1_, f32[64,8,32,128]{3,2,1,0:T(8,128)} %copy-done.3, f32[128,32,128]{2,1,0:T(8,128)} %collective-permute-done.refs_3_.refs_1_, ...), custom_call_target="tpu_custom_call" | custom-call | tf_op jit(solution)/shard_map/pallas_call | solution.py:47
  126.5 8.6 %collective-permute-start.7 = (f32[128,32,128]{2,1,0:T(8,128)}, f32[128,32,128]{2,1,0:T(8,128)}, u32[]{:S(2)}, u32[]{:S(2)}) collective-permute-start(f32[128,32,128]{2,1,0:T(8,128)} %bitcast.16.refs_2_.refs_0_), channel_id=1, source_target_pairs={{0,1},{3,2},{4,5},{7,6},{8,9},{11,10},{12,13},{15,14},{16,17},{19,... | collective-permute-start | bytes 6291464 | tf_op jit(solution)/shard_map/ppermute | solution.py:408
  137.3 6.8 %shard_map.118.refs_6_ = f32[8,4,8,32,128]{4,3,2,1,0:T(8,128)S(1)} custom-call(f32[8,8,8,32,128]{4,3,2,1,0:T(8,128)} %all-to-all-done.refs_0_, f32[8,64,64]{2,1,0:T(8,128)S(1)} %add_multiply_fusion.refs_1_, f32[8,4,8,32,128]{4,3,2,1,0:T(8,128)S(1)} %copy-done.9), custom_call_target="tpu_custom_call" | custom-call | tf_op jit(solution)/shard_map/pallas_call | solution.py:47
  146.1 21.2 %all-to-all-done.1.refs_1_ = f32[8,4,8,32,128]{4,3,2,1,0:T(8,128)} async-done(((f32[8,4,8,32,128]{4,3,2,1,0:T(8,128)}), f32[8,4,8,32,128]{4,3,2,1,0:T(8,128)}, u32[]{:S(2)}, u32[]{:S(2)}) %all-to-all-start.1) | async-done | bytes 4194336 | tf_op jit(solution)/shard_map/all_to_all | solution.py:411
  173.9 8.4 %shard_map.119 = (f32[128,32,128]{2,1,0:T(8,128)S(1)}, f32[128,32,128]{2,1,0:T(8,128)}) custom-call(f32[1,128]{1,0:T(1,128)S(1)} %convert_bitcast_fusion.refs_0_, f32[128,128]{1,0:T(8,128)S(1)} %fusion.2.refs_1_, f32[128,32,128]{2,1,0:T(8,128)} %bitcast.4.refs_2_.refs_0_, f32[128,32,128]{2,1,0:T(8,128)} %collective-permute-done.refs_3_.refs_1_, ...), custom_call_target="tpu_custom_call" | custom-call | tf_op jit(solution)/shard_map/pallas_call | solution.py:47
  183.7 9.8 %collective-permute-start.9 = (f32[64,32,128]{2,1,0:T(8,128)S(1)}, f32[64,32,128]{2,1,0:T(8,128)S(1)}, u32[]{:S(2)}, u32[]{:S(2)}) collective-permute-start(f32[64,32,128]{2,1,0:T(8,128)S(1)} %bitcast.88), channel_id=1, source_target_pairs={{0,1},{3,2},{4,5},{7,6},{8,9},{11,10},{12,13},{15,14},{16,17},{19,... | collective-permute-start | bytes 3145736 | tf_op jit(solution)/shard_map/ppermute | solution.py:408
  198.4 18.5 %collective-permute-done.9.refs_9_.refs_3_.refs_1_ = f32[64,32,128]{2,1,0:T(8,128)S(1)} collective-permute-done((f32[64,32,128]{2,1,0:T(8,128)S(1)}, f32[64,32,128]{2,1,0:T(8,128)S(1)}, u32[]{:S(2)}, u32[]{:S(2)}) %collective-permute-start.9) | collective-permute-done | bytes 1048608 | tf_op jit(solution)/shard_map/ppermute | solution.py:408
  232.2 6.4 %collective-permute-done.8.refs_8_.refs_3_.refs_1_ = f32[64,32,128]{2,1,0:T(8,128)S(1)} collective-permute-done((f32[64,32,128]{2,1,0:T(8,128)S(1)}, f32[64,32,128]{2,1,0:T(8,128)S(1)}, u32[]{:S(2)}, u32[]{:S(2)}) %collective-permute-start.8) | collective-permute-done | bytes 1048608 | tf_op jit(solution)/shard_map/ppermute | solution.py:408
  239.9 8.0 %shard_map.124 = (f32[128,32,128]{2,1,0:T(8,128)S(1)}, f32[128,32,128]{2,1,0:T(8,128)}) custom-call(f32[1,128]{1,0:T(1,128)S(1)} %convert_bitcast_fusion.refs_0_, f32[128,128]{1,0:T(8,128)S(1)} %fusion.2.refs_1_, f32[128,32,128]{2,1,0:T(8,128)S(1)} %bitcast.70, f32[128,32,128]{2,1,0:T(8,128)} %collective-permute-done.3.refs_5_.refs_3_.refs_1_, ...), custom_call_target="tpu_custom_call" | custom-call | tf_op jit(solution)/shard_map/pallas_call | solution.py:47
  275.2 7.5 %collective-permute-start.17 = (f32[128,32,128]{2,1,0:T(8,128)}, f32[128,32,128]{2,1,0:T(8,128)}, u32[]{:S(2)}, u32[]{:S(2)}) collective-permute-start(f32[128,32,128]{2,1,0:T(8,128)} %bitcast.85), channel_id=1, source_target_pairs={{0,1},{3,2},{4,5},{7,6},{8,9},{11,10},{12,13},{15,14},{16,17},{19,... | collective-permute-start | bytes 6291464 | tf_op jit(solution)/shard_map/ppermute | solution.py:408
  285.3 8.4 %shard_map.129 = (f32[128,32,128]{2,1,0:T(8,128)S(1)}, f32[128,32,128]{2,1,0:T(8,128)}) custom-call(f32[1,128]{1,0:T(1,128)S(1)} %convert_bitcast_fusion.refs_0_, f32[128,128]{1,0:T(8,128)S(1)} %fusion.2.refs_1_, f32[128,32,128]{2,1,0:T(8,128)} %bitcast.16.refs_2_.refs_0_, f32[128,32,128]{2,1,0:T(8,128)} %collective-permute-done.7.refs_7_.refs_3_.refs_1_, ...), custom_call_target="tpu_custom_call" | custom-call | tf_op jit(solution)/shard_map/pallas_call | solution.py:47
  308.1 32.8 %collective-permute-start.21 = (f32[128,32,128]{2,1,0:T(8,128)}, f32[128,32,128]{2,1,0:T(8,128)}, u32[]{:S(2)}, u32[]{:S(2)}) collective-permute-start(f32[128,32,128]{2,1,0:T(8,128)} %bitcast.79), channel_id=1, source_target_pairs={{0,1},{3,2},{4,5},{7,6},{8,9},{11,10},{12,13},{15,14},{16,17},{19,... | collective-permute-start | bytes 6291464 | tf_op jit(solution)/shard_map/ppermute | solution.py:408
  344.2 8.5 %shard_map.131.refs_7_ = f32[8,128,64]{2,1,0:T(8,128)S(1)} custom-call(f32[128,32,128]{2,1,0:T(8,128)} %bitcast.4.refs_2_.refs_0_, f32[128,32,128]{2,1,0:T(8,128)} %collective-permute-done.refs_3_.refs_1_, f32[128,32,128]{2,1,0:T(8,128)} %collective-permute-done.1.refs_4_.refs_2_, f32[128,32,128]{2,1,0:T(8,128)} %collective-permute-done.2.refs_5_.refs_3_, ...), custom_call_target="tpu_custom_call" | custom-call | tf_op jit(solution)/shard_map/pallas_call | solution.py:47
  352.7 19.8 %collective-permute-done.16.refs_5_ = f32[128,32,128]{2,1,0:T(8,128)} collective-permute-done((f32[128,32,128]{2,1,0:T(8,128)}, f32[128,32,128]{2,1,0:T(8,128)}, u32[]{:S(2)}, u32[]{:S(2)}) %collective-permute-start.16) | collective-permute-done | bytes 2097184 | tf_op jit(solution)/shard_map/ppermute | solution.py:408
  372.5 7.6 %shard_map.132.refs_6_ = f32[8,128,64]{2,1,0:T(8,128)S(1)} custom-call(f32[128,32,128]{2,1,0:T(8,128)S(1)} %bitcast.71, f32[128,32,128]{2,1,0:T(8,128)} %collective-permute-done.3.refs_5_.refs_3_.refs_1_, f32[128,32,128]{2,1,0:T(8,128)} %collective-permute-done.4.refs_6_.refs_4_.refs_2_, f32[128,32,128]{2,1,0:T(8,128)S(1)} %copy-done.31, ...), custom_call_target="tpu_custom_call" | custom-call | tf_op jit(solution)/shard_map/pallas_call | solution.py:47
  394.5 14.6 %collective-permute-start.23 = (f32[64,32,128]{2,1,0:T(8,128)S(1)}, f32[64,32,128]{2,1,0:T(8,128)S(1)}, u32[]{:S(2)}, u32[]{:S(2)}) collective-permute-start(f32[64,32,128]{2,1,0:T(8,128)S(1)} %bitcast.93), channel_id=1, source_target_pairs={{0,1},{3,2},{4,5},{7,6},{8,9},{11,10},{12,13},{15,14},{16,17},{19,... | collective-permute-start | bytes 3145736 | tf_op jit(solution)/shard_map/ppermute | solution.py:408
  410.5 7.0 %collective-permute-done.21.refs_5_ = f32[128,32,128]{2,1,0:T(8,128)} collective-permute-done((f32[128,32,128]{2,1,0:T(8,128)}, f32[128,32,128]{2,1,0:T(8,128)}, u32[]{:S(2)}, u32[]{:S(2)}) %collective-permute-start.21) | collective-permute-done | bytes 2097184 | tf_op jit(solution)/shard_map/ppermute | solution.py:408
  427.7 8.8 %shard_map.137.refs_6_ = f32[8,128,64]{2,1,0:T(8,128)S(1)} custom-call(f32[128,32,128]{2,1,0:T(8,128)} %bitcast.16.refs_2_.refs_0_, f32[128,32,128]{2,1,0:T(8,128)} %collective-permute-done.7.refs_7_.refs_3_.refs_1_, f32[128,32,128]{2,1,0:T(8,128)} %collective-permute-done.11.refs_4_.refs_2_, f32[128,32,128]{2,1,0:T(8,128)} %collective-permute-done.12.refs_5_.refs_3_, ...), custom_call_target="tpu_custom_call" | custom-call | tf_op jit(solution)/shard_map/pallas_call | solution.py:47
  439.8 21.9 %collective-permute-done.22.refs_7_.refs_5_ = f32[64,32,128]{2,1,0:T(8,128)S(1)} collective-permute-done((f32[64,32,128]{2,1,0:T(8,128)S(1)}, f32[64,32,128]{2,1,0:T(8,128)S(1)}, u32[]{:S(2)}, u32[]{:S(2)}) %collective-permute-start.22) | collective-permute-done | bytes 1048608 | tf_op jit(solution)/shard_map/ppermute | solution.py:408
  481.2 10.3 %collective-permute-done.24.refs_1_ = f32[64,32,128]{2,1,0:T(8,128)} collective-permute-done((f32[64,32,128]{2,1,0:T(8,128)}, f32[64,32,128]{2,1,0:T(8,128)}, u32[]{:S(2)}, u32[]{:S(2)}) %collective-permute-start.24) | collective-permute-done | bytes 1048608 | tf_op jit(solution)/shard_map/ppermute | solution.py:408
  504.0 15.0 %shard_map.143 = (f32[8,64,64]{2,1,0:T(8,128)}, f32[8,128,128]{2,1,0:T(8,128)}) custom-call(f32[8,8,8,32,128]{4,3,2,1,0:T(8,128)} %bitcast.54, f32[8,2,8,32,128]{4,3,2,1,0:T(8,128)} %bitcast.77, f32[8,2,8,32,128]{4,3,2,1,0:T(8,128)} %bitcast.74, f32[8,2,8,32,128]{4,3,2,1,0:T(8,128)} %bitcast.23.refs_2_.refs_3_, ...), custom_call_target="tpu_custom_call" | custom-call | tf_op jit(solution)/shard_map/pallas_call | solution.py:47
  553.6 7.5 %collective-permute-done.29.refs_1_ = f32[320,128]{1,0:T(8,128)S(1)} collective-permute-done((f32[320,128]{1,0:T(8,128)S(1)}, f32[320,128]{1,0:T(8,128)S(1)}, u32[]{:S(2)}, u32[]{:S(2)}) %collective-permute-start.29) | collective-permute-done | bytes 163872 | tf_op jit(solution)/shard_map/ppermute | solution.py:491
  (329 shorter events, 228.8 us)
Async XLA Ops:
  0.6 104.2 %all-to-all-start = ((f32[8,8,8,32,128]{4,3,2,1,0:T(8,128)}), f32[8,8,8,32,128]{4,3,2,1,0:T(8,128)}, u32[]{:S(2)}, u32[]{:S(2)}) async-start(f32[8,8,8,32,128]{4,3,2,1,0:T(8,128)} %bitcast.53), calls=%async_computation | async-start | bytes 16777216 | tf_op jit(solution)/shard_map/all_to_all | solution.py:411
  9.5 53.3 %collective-permute-start.3 = (f32[128,32,128]{2,1,0:T(8,128)S(1)}, f32[128,32,128]{2,1,0:T(8,128)}, u32[]{:S(2)}, u32[]{:S(2)}) collective-permute-start(f32[128,32,128]{2,1,0:T(8,128)S(1)} %bitcast.65), channel_id=1, source_target_pairs={{0,1},{3,2},{4,5},{7,6},{8,9},{11,10},{12,13},{15,14},{16,17},{19,... | collective-permute-start | bytes 6291464 | tf_op jit(solution)/shard_map/ppermute | solution.py:408
  15.7 47.1 %collective-permute-start.4 = (f32[128,32,128]{2,1,0:T(8,128)S(1)}, f32[128,32,128]{2,1,0:T(8,128)}, u32[]{:S(2)}, u32[]{:S(2)}) collective-permute-start(f32[128,32,128]{2,1,0:T(8,128)S(1)} %bitcast.66), channel_id=1, source_target_pairs={{1,2},{2,1},{5,6},{6,5},{9,10},{10,9},{13,14},{14,13},{17,18},{18,... | collective-permute-start | bytes 6291464 | tf_op jit(solution)/shard_map/ppermute | solution.py:408
  20.7 84.2 %collective-permute-start = (f32[128,32,128]{2,1,0:T(8,128)}, f32[128,32,128]{2,1,0:T(8,128)}, u32[]{:S(2)}, u32[]{:S(2)}) collective-permute-start(f32[128,32,128]{2,1,0:T(8,128)} %bitcast.4.refs_2_.refs_0_), channel_id=1, source_target_pairs={{0,1},{3,2},{4,5},{7,6},{8,9},{11,10},{12,13},{15,14},{16,17},{19,... | collective-permute-start | bytes 6291464 | tf_op jit(solution)/shard_map/ppermute | solution.py:408
  23.5 81.3 %collective-permute-start.1 = (f32[128,32,128]{2,1,0:T(8,128)}, f32[128,32,128]{2,1,0:T(8,128)}, u32[]{:S(2)}, u32[]{:S(2)}) collective-permute-start(f32[128,32,128]{2,1,0:T(8,128)} %bitcast.4.refs_2_.refs_0_), channel_id=1, source_target_pairs={{1,2},{2,1},{5,6},{6,5},{9,10},{10,9},{13,14},{14,13},{17,18},{18,... | collective-permute-start | bytes 6291464 | tf_op jit(solution)/shard_map/ppermute | solution.py:408
  113.6 53.7 %all-to-all-start.1 = ((f32[8,4,8,32,128]{4,3,2,1,0:T(8,128)}), f32[8,4,8,32,128]{4,3,2,1,0:T(8,128)}, u32[]{:S(2)}, u32[]{:S(2)}) async-start(f32[8,4,8,32,128]{4,3,2,1,0:T(8,128)} %copy-done.8), calls=%async_computation.1 | async-start | bytes 8388608 | tf_op jit(solution)/shard_map/all_to_all | solution.py:411
  118.2 55.8 %collective-permute-start.2 = (f32[128,32,128]{2,1,0:T(8,128)}, f32[128,32,128]{2,1,0:T(8,128)}, u32[]{:S(2)}, u32[]{:S(2)}) collective-permute-start(f32[128,32,128]{2,1,0:T(8,128)} %collective-permute-done.refs_3_.refs_1_), channel_id=1, source_target_pairs={{1,2},{2,1},{5,6},{6,5},{9,10},{10,9},{13,14},{14,13},{17,18},{18,... | collective-permute-start | bytes 6291464 | tf_op jit(solution)/shard_map/ppermute | solution.py:408
  126.5 92.5 %collective-permute-start.7 = (f32[128,32,128]{2,1,0:T(8,128)}, f32[128,32,128]{2,1,0:T(8,128)}, u32[]{:S(2)}, u32[]{:S(2)}) collective-permute-start(f32[128,32,128]{2,1,0:T(8,128)} %bitcast.16.refs_2_.refs_0_), channel_id=1, source_target_pairs={{0,1},{3,2},{4,5},{7,6},{8,9},{11,10},{12,13},{15,14},{16,17},{19,... | collective-permute-start | bytes 6291464 | tf_op jit(solution)/shard_map/ppermute | solution.py:408
  167.3 83.2 %all-to-all-start.2 = ((f32[8,4,8,32,128]{4,3,2,1,0:T(8,128)}), f32[8,4,8,32,128]{4,3,2,1,0:T(8,128)}, u32[]{:S(2)}, u32[]{:S(2)}) async-start(f32[8,4,8,32,128]{4,3,2,1,0:T(8,128)} %copy-done.10), calls=%async_computation.2 | async-start | bytes 8388608 | tf_op jit(solution)/shard_map/all_to_all | solution.py:411
  173.1 65.5 %collective-permute-start.6 = (f32[128,32,128]{2,1,0:T(8,128)}, f32[128,32,128]{2,1,0:T(8,128)S(1)}, u32[]{:S(2)}, u32[]{:S(2)}) collective-permute-start(f32[128,32,128]{2,1,0:T(8,128)} %collective-permute-done.3.refs_5_.refs_3_.refs_1_), channel_id=1, source_target_pairs={{1,2},{2,1},{5,6},{6,5},{9,10},{10,9},{13,14},{14,13},{17,18},{18,... | collective-permute-start | bytes 6291464 | tf_op jit(solution)/shard_map/ppermute | solution.py:408
  182.4 84.2 %collective-permute-start.5 = (f32[128,32,128]{2,1,0:T(8,128)}, f32[128,32,128]{2,1,0:T(8,128)}, u32[]{:S(2)}, u32[]{:S(2)}) collective-permute-start(f32[128,32,128]{2,1,0:T(8,128)} %get-tuple-element.15.refs_6_), channel_id=1, source_target_pairs={{1,0},{2,3},{5,4},{6,7},{9,8},{10,11},{13,12},{14,15},{17,16},{18,... | collective-permute-start | bytes 6291464 | tf_op jit(solution)/shard_map/ppermute | solution.py:408
  217.0 68.4 %collective-permute-start.11 = (f32[128,32,128]{2,1,0:T(8,128)}, f32[128,32,128]{2,1,0:T(8,128)}, u32[]{:S(2)}, u32[]{:S(2)}) collective-permute-start(f32[128,32,128]{2,1,0:T(8,128)} %bitcast.16.refs_2_.refs_0_), channel_id=1, source_target_pairs={{1,2},{2,1},{5,6},{6,5},{9,10},{10,9},{13,14},{14,13},{17,18},{18,... | collective-permute-start | bytes 6291464 | tf_op jit(solution)/shard_map/ppermute | solution.py:408
  219.0 66.3 %collective-permute-start.12 = (f32[128,32,128]{2,1,0:T(8,128)}, f32[128,32,128]{2,1,0:T(8,128)}, u32[]{:S(2)}, u32[]{:S(2)}) collective-permute-start(f32[128,32,128]{2,1,0:T(8,128)} %collective-permute-done.7.refs_7_.refs_3_.refs_1_), channel_id=1, source_target_pairs={{1,2},{2,1},{5,6},{6,5},{9,10},{10,9},{13,14},{14,13},{17,18},{18,... | collective-permute-start | bytes 6291464 | tf_op jit(solution)/shard_map/ppermute | solution.py:408
  249.2 49.2 %collective-permute-start.10 = (f32[128,32,128]{2,1,0:T(8,128)}, f32[128,32,128]{2,1,0:T(8,128)}, u32[]{:S(2)}, u32[]{:S(2)}) collective-permute-start(f32[128,32,128]{2,1,0:T(8,128)} %get-tuple-element.17.refs_6_), channel_id=1, source_target_pairs={{1,0},{2,3},{5,4},{6,7},{9,8},{10,11},{13,12},{14,15},{17,16},{18,... | collective-permute-start | bytes 6291464 | tf_op jit(solution)/shard_map/ppermute | solution.py:408
  275.2 66.5 %collective-permute-start.17 = (f32[128,32,128]{2,1,0:T(8,128)}, f32[128,32,128]{2,1,0:T(8,128)}, u32[]{:S(2)}, u32[]{:S(2)}) collective-permute-start(f32[128,32,128]{2,1,0:T(8,128)} %bitcast.85), channel_id=1, source_target_pairs={{0,1},{3,2},{4,5},{7,6},{8,9},{11,10},{12,13},{15,14},{16,17},{19,... | collective-permute-start | bytes 6291464 | tf_op jit(solution)/shard_map/ppermute | solution.py:408
  282.7 89.8 %collective-permute-start.16 = (f32[128,32,128]{2,1,0:T(8,128)}, f32[128,32,128]{2,1,0:T(8,128)}, u32[]{:S(2)}, u32[]{:S(2)}) collective-permute-start(f32[128,32,128]{2,1,0:T(8,128)} %bitcast.82), channel_id=1, source_target_pairs={{0,1},{3,2},{4,5},{7,6},{8,9},{11,10},{12,13},{15,14},{16,17},{19,... | collective-permute-start | bytes 6291464 | tf_op jit(solution)/shard_map/ppermute | solution.py:408
  293.7 89.4 %collective-permute-start.13 = (f32[128,32,128]{2,1,0:T(8,128)}, f32[128,32,128]{2,1,0:T(8,128)}, u32[]{:S(2)}, u32[]{:S(2)}) collective-permute-start(f32[128,32,128]{2,1,0:T(8,128)} %get-tuple-element.19.refs_6_), channel_id=1, source_target_pairs={{1,0},{2,3},{5,4},{6,7},{9,8},{10,11},{13,12},{14,15},{17,16},{18,... | collective-permute-start | bytes 6291464 | tf_op jit(solution)/shard_map/ppermute | solution.py:408
  303.8 84.8 %all-to-all-start.3 = ((f32[8,2,8,32,128]{4,3,2,1,0:T(8,128)}), f32[8,2,8,32,128]{4,3,2,1,0:T(8,128)}, u32[]{:S(2)}, u32[]{:S(2)}) async-start(f32[8,2,8,32,128]{4,3,2,1,0:T(8,128)} %bitcast.72), calls=%async_computation.3 | async-start | bytes 4194304 | tf_op jit(solution)/shard_map/all_to_all | solution.py:411
  308.1 109.3 %collective-permute-start.21 = (f32[128,32,128]{2,1,0:T(8,128)}, f32[128,32,128]{2,1,0:T(8,128)}, u32[]{:S(2)}, u32[]{:S(2)}) collective-permute-start(f32[128,32,128]{2,1,0:T(8,128)} %bitcast.79), channel_id=1, source_target_pairs={{0,1},{3,2},{4,5},{7,6},{8,9},{11,10},{12,13},{15,14},{16,17},{19,... | collective-permute-start | bytes 6291464 | tf_op jit(solution)/shard_map/ppermute | solution.py:408
  388.5 80.0 %all-to-all-start.5 = ((f32[8,2,8,32,128]{4,3,2,1,0:T(8,128)}), f32[8,2,8,32,128]{4,3,2,1,0:T(8,128)}, u32[]{:S(2)}, u32[]{:S(2)}) async-start(f32[8,2,8,32,128]{4,3,2,1,0:T(8,128)} %bitcast.23.refs_2_.refs_3_), calls=%async_computation.5 | async-start | bytes 4194304 | tf_op jit(solution)/shard_map/all_to_all | solution.py:411
  393.0 43.5 %collective-permute-start.19 = (f32[64,32,128]{2,1,0:T(8,128)S(1)}, f32[64,32,128]{2,1,0:T(8,128)S(1)}, u32[]{:S(2)}, u32[]{:S(2)}) collective-permute-start(f32[64,32,128]{2,1,0:T(8,128)S(1)} %bitcast.89), channel_id=1, source_target_pairs={{1,2},{2,1},{5,6},{6,5},{9,10},{10,9},{13,14},{14,13},{17,18},{18,... | collective-permute-start | bytes 3145736 | tf_op jit(solution)/shard_map/ppermute | solution.py:408
  394.5 45.3 %collective-permute-start.23 = (f32[64,32,128]{2,1,0:T(8,128)S(1)}, f32[64,32,128]{2,1,0:T(8,128)S(1)}, u32[]{:S(2)}, u32[]{:S(2)}) collective-permute-start(f32[64,32,128]{2,1,0:T(8,128)S(1)} %bitcast.93), channel_id=1, source_target_pairs={{0,1},{3,2},{4,5},{7,6},{8,9},{11,10},{12,13},{15,14},{16,17},{19,... | collective-permute-start | bytes 3145736 | tf_op jit(solution)/shard_map/ppermute | solution.py:408
  409.1 52.6 %collective-permute-start.22 = (f32[64,32,128]{2,1,0:T(8,128)S(1)}, f32[64,32,128]{2,1,0:T(8,128)S(1)}, u32[]{:S(2)}, u32[]{:S(2)}) collective-permute-start(f32[64,32,128]{2,1,0:T(8,128)S(1)} %bitcast.96), channel_id=1, source_target_pairs={{0,1},{3,2},{4,5},{7,6},{8,9},{11,10},{12,13},{15,14},{16,17},{19,... | collective-permute-start | bytes 3145736 | tf_op jit(solution)/shard_map/ppermute | solution.py:408
  417.4 48.4 %collective-permute-start.18 = (f32[64,32,128]{2,1,0:T(8,128)}, f32[64,32,128]{2,1,0:T(8,128)S(1)}, u32[]{:S(2)}, u32[]{:S(2)}) collective-permute-start(f32[64,32,128]{2,1,0:T(8,128)} %copy-done.61), channel_id=1, source_target_pairs={{1,0},{2,3},{5,4},{6,7},{9,8},{10,11},{13,12},{14,15},{17,16},{18,... | collective-permute-start | bytes 3145736 | tf_op jit(solution)/shard_map/ppermute | solution.py:408
  (103 other events, 1327.5 us)
